TPU v7x, 32 devices: a whole 2x2x4 slice. The times are simulated.
32 devices in a mesh: groups: 2 (over y), fsdp: 8 (over z, x), blk: 2 (over core).
Axes of the slice: x: 2, y: 2, z: 4, core: 2. Of those that a mesh axis runs over, the one named last changes fastest.
Arguments:
- block_input: bfloat16 [8192, 5120], P(('groups', 'fsdp', 'blk')), parts along dimension 0, may hold values from -3 to 3
- gate: float32 [10240], P('groups'), parts along dimension 0, may hold values from -6 to 6
- q_fresh: bfloat16 [8192, 2560], P(('groups', 'fsdp', 'blk')), parts along dimension 0, may hold values from -48.5 to 48.5
- kv_fresh: bfloat16 [8192, 2, 2560], P(('groups', 'fsdp', 'blk')), parts along dimension 0, may hold values from -6 to 6
- kv_cache: bfloat16 [8192, 2, 2560], P(('groups', 'fsdp', 'blk')), parts along dimension 0, may hold values from -6 to 6
- active_list: int32 [16, 2, 2], P(('groups', 'fsdp')), parts along dimension 0, may hold values from 0 to 1, as said below
- active_count: int32 [16, 2], P(('groups', 'fsdp')), parts along dimension 0, may hold values from 0 to 2, as said below
- key_list: int32 [16, 4, 3], P(('groups', 'fsdp')), parts along dimension 0, may hold values from 0 to 3, as said below
- out_weight: bfloat16 [2560, 5120], P('fsdp'), may hold values from -0.125 to 0.125
Outputs:
- block_output: bfloat16 [8192, 5120], P(('groups', 'fsdp', 'blk')), parts along dimension 0
There are 2 independent parts, one for each index of `groups`. A program takes and returns all parts, laid end to end along the dimension named above; an argument that names none is the same for every part. Nothing has to cross between parts.
Inputs may be any that keep to these rules, and one draw needn't show every extreme that they name: `active_list`: each row [f, b] holds every tile number once; its first active_count[f, b] entries are the active tiles. `active_count`: some token block has all 2 tiles active. `key_list`: entry [f, g] holds 3 different tile ids of group f, the first one being g.
All inputs are finite; a program needn't handle non-finite values.
Results may differ from a plain program's by a relative error of at most 0.0034.
Values may be sent and summed in bfloat16 or wider, within the bound.
No kernel may reach another device: no remote copies, remote signals or barrier semaphores. Data moves between devices by JAX's collectives and lax.ppermute only.
A program may use at most 128 MiB of HBM per device.

v0:
```python
import math

import jax
import jax.numpy as jnp
from jax import lax
from jax.sharding import PartitionSpec as P

HEADS = 20
HEAD_DIM = 128


MASKED = -1e30


def swapped(block, axis, apart):
    count = lax.axis_size(axis)
    route = []
    for low in range(count):
        high = low | 1 << apart
        if high != low and high < count:
            route += [(low, high), (high, low)]
    return lax.ppermute(block, axis, route)


def tile_flags(tile_list, tile_count):
    slot_ids = jnp.arange(tile_list.shape[0], dtype=jnp.int32)
    listed = (tile_list[:, None] == slot_ids[None, :]) & (slot_ids[:, None] < tile_count)
    return jnp.any(listed, axis=0)


def block_partial(query_tile, key_rows, value_rows, allowed):
    tile_rows = query_tile.shape[0]
    query3 = query_tile.reshape(tile_rows, HEADS, HEAD_DIM)
    key3 = key_rows.reshape(key_rows.shape[0], HEADS, HEAD_DIM)
    value3 = value_rows.reshape(value_rows.shape[0], HEADS, HEAD_DIM)
    scores = jnp.einsum(
        "qhd,khd->hqk", query3, key3, preferred_element_type=jnp.float32
    ) / math.sqrt(HEAD_DIM)
    scores = jnp.where(allowed[None, None, :], scores, MASKED)
    row_max = jnp.max(scores, axis=2)
    exp_terms = jnp.where(allowed[None, None, :], jnp.exp(scores - row_max[:, :, None]), 0.0)
    row_total = jnp.sum(exp_terms, axis=2)
    weights = exp_terms.astype(jnp.bfloat16)
    block_out = jnp.einsum("hqk,khd->hqd", weights, value3, preferred_element_type=jnp.float32)
    return (block_out, row_max, row_total)


def attend_block(
    queries, tile_list, tile_count, query_side, key_rows, value_rows, key_side, key_table
):
    tiles_dev = tile_list.shape[0]
    tile_rows = queries.shape[0] // tiles_dev
    slot_ids = jnp.arange(tiles_dev, dtype=jnp.int32)
    key_tiles = key_side * tiles_dev + slot_ids
    init_state = (
        jnp.zeros((tiles_dev, HEADS, tile_rows, HEAD_DIM), jnp.float32),
        jnp.full((tiles_dev, HEADS, tile_rows), MASKED, jnp.float32),
        jnp.zeros((tiles_dev, HEADS, tile_rows), jnp.float32),
    )

    def one_slot(slot_idx, carry_state):
        tile_pos = tile_list[slot_idx]
        query_tile = lax.dynamic_slice_in_dim(queries, tile_pos * tile_rows, tile_rows, 0)
        listed = key_table[query_side * tiles_dev + tile_pos]
        allowed_tiles = jnp.any(key_tiles[:, None] == listed[None, :], axis=1)
        allowed = jnp.repeat(allowed_tiles, tile_rows, total_repeat_length=tiles_dev * tile_rows)
        partial_value = block_partial(query_tile, key_rows, value_rows, allowed)
        return tuple(
            (whole.at[tile_pos].set(piece) for whole, piece in zip(carry_state, partial_value))
        )

    return lax.fori_loop(0, tile_count, one_slot, init_state)


def merge_states(earlier, later_state):
    out_one, max_one, total_one = earlier
    out_two, max_two, total_two = later_state
    joint_max = jnp.maximum(max_one, max_two)
    scale_one = jnp.exp(max_one - joint_max)
    scale_two = jnp.exp(max_two - joint_max)
    summed = out_one * scale_one[..., None] + out_two * scale_two[..., None]
    return (summed, total_one * scale_one + total_two * scale_two)


def local(
    block_input, gate, q_fresh, kv_fresh, kv_cache, active_list, active_count, key_list, out_weight
):
    own_side = lax.axis_index("blk")
    other_side = 1 - own_side
    tiles_dev = active_list.shape[2]
    tok_dev = block_input.shape[0]
    tile_rows = tok_dev // tiles_dev
    own_list = active_list[0, own_side]
    own_count = active_count[0, own_side]
    flags = tile_flags(own_list, own_count)
    row_flags = jnp.repeat(flags, tile_rows, total_repeat_length=tok_dev)
    resident = jnp.where(row_flags[:, None, None], kv_fresh, kv_cache)
    key_table = key_list[0]
    own_state = attend_block(
        q_fresh, own_list, own_count, own_side, resident[:, 0], resident[:, 1], own_side, key_table
    )
    other_kv = swapped(resident, "blk", 0)
    other_state = attend_block(
        q_fresh,
        own_list,
        own_count,
        own_side,
        other_kv[:, 0],
        other_kv[:, 1],
        other_side,
        key_table,
    )
    summed, denom = merge_states(own_state, other_state)
    denom = jnp.where(flags[:, None, None], denom, 1.0)
    attended = (
        (summed / denom[..., None])
        .transpose(0, 2, 1, 3)
        .reshape(tok_dev, HEADS * HEAD_DIM)
        .astype(jnp.bfloat16)
    )
    half_cols = out_weight.shape[1] // 2
    own_cols = lax.dynamic_slice_in_dim(out_weight, own_side * half_cols, half_cols, 1)
    half_weight = lax.all_gather(own_cols, "fsdp", axis=0, tiled=True)
    partner_rows = swapped(attended, "blk", 0)
    own_part = jnp.dot(attended, half_weight, preferred_element_type=jnp.float32)
    partner_part = jnp.dot(partner_rows, half_weight, preferred_element_type=jnp.float32)
    returned = swapped(partner_part, "blk", 0)
    projected = jnp.where(
        own_side == 0,
        jnp.concatenate([own_part, returned], axis=1),
        jnp.concatenate([returned, own_part], axis=1),
    )
    mixed = block_input.astype(jnp.float32) + gate[None, :] * projected
    return jnp.where(row_flags[:, None], mixed.astype(jnp.bfloat16), block_input)


def solution(mesh):
    in_specs = (
        P(("groups", "fsdp", "blk"), None),
        P("groups"),
        P(("groups", "fsdp", "blk"), None),
        P(("groups", "fsdp", "blk"), None, None),
        P(("groups", "fsdp", "blk"), None, None),
        P(("groups", "fsdp"), None, None),
        P(("groups", "fsdp"), None),
        P(("groups", "fsdp"), None, None),
        P("fsdp", None),
    )
    out_specs = P(("groups", "fsdp", "blk"), None)
    return jax.shard_map(local, mesh=mesh, in_specs=in_specs, out_specs=out_specs, check_vma=False)
```

profile of v0, /device:TPU:0, one launch (start us, length us, event | category | flops | bytes accessed | tf_op | source)
XLA Modules:
  0.0 244.5 jit_solution(7101395316258449989)
XLA Ops:
  6.6 1.5 constant_dynamic-slice_fusion.5
  8.0 0.7 iota_compare_fusion
  8.7 0.7 fusion.47
  9.5 0.6 fusion.55
  10.1 1.4 select_reduce_fusion
  11.5 7.3 %copy.34 = bf16[256,2,2560]{0,2,1:T(8,128)(2,1)} copy(bf16[256,2,2560]{2,1,0:T(2,128)(2,1)} %param.36) | data formatting | bytes 5242880 | tf_op args[3]
  18.8 7.3 %copy.35 = bf16[256,2,2560]{0,2,1:T(8,128)(2,1)} copy(bf16[256,2,2560]{2,1,0:T(2,128)(2,1)} %param.37) | data formatting | bytes 5242880 | tf_op args[4]
  26.1 4.3 %broadcast_select_fusion = bf16[256,2,2560]{0,2,1:T(8,128)(2,1)} fusion(bf16[256,2,2560]{0,2,1:T(8,128)(2,1)} %copy.34, bf16[256,2,2560]{0,2,1:T(8,128)(2,1)} %copy.35, pred[256]{0:T(512)(128)(4,1)S(1)} %and_select_fusion), kind=kLoop, calls=%fused_computation.64 | loop fusion | flops 1310720 | bytes 7864576 | tf_op jit(solution)/shard_map/jit(_where)/select_n | solution.py:97
  30.4 0.5 collective-permute-start
  30.9 1.3 constant_dynamic-slice_fusion.4
  32.2 2.4 copy.36
  34.7 3.4 %fusion.53 = (bf16[256,1,2560]{0,2,1:T(8,128)(2,1)}, bf16[256,1,2560]{0,2,1:T(8,128)(2,1)}) fusion(bf16[256,2,2560]{0,2,1:T(8,128)(2,1)} %broadcast_select_fusion), kind=kLoop, calls=%fused_computation.88 | loop fusion | bytes 5242880 | tf_op jit(solution)/shard_map/slice | solution.py:100
  38.1 1.8 broadcast.442.clone.1
  39.9 36.4 %while.47 = (s32[]{:T(128)}, f32[2,20,128,128]{3,2,1,0:T(8,128)}, f32[2,20,128]{2,1,0:T(8,128)S(1)}, f32[2,20,128]{2,1,0:T(8,128)S(1)}, s32[]{:T(128)}, /*index=...) while((s32[]{:T(128)}, f32[2,20,128,128]{3,2,1,0:T(8,128)}, ...), condition=%wide.region_7.9_spmd.clone.clone, body=%wide.region_1.8_spmd.clone.clone.sunk | while | flops 344394592 | bytes 15190492 | solution.py:72
  40.6 0.7 dynamic_slice.87
  42.2 0.7 fusion.98
  42.9 1.2 select_select_fusion.5
  44.8 1.2 constant_dynamic-slice_fusion.10
  46.0 2.0 fusion.99
  48.0 1.2 fusion.100
  51.3 0.8 and_reduce_fusion.12
  52.1 0.7 fusion.101
  52.8 0.8 and_reduce_fusion.11
  53.6 4.2 %select_dynamic-update-slice_fusion.5 = f32[2,20,128,128]{3,2,1,0:T(8,128)} fusion(f32[2,20,128,128]{3,2,1,0:T(8,128)} %get-tuple-element.974, s32[]{:T(128)} %select_n.324, bf16[256,20,128]{0,2,1:T(8,128)(2,1)} %bitcast.138, f32[20,128,256]{2,1,0:T(8,128)S(1)} %get-tuple-element.886, f32[20,128]{1,0:T(8,128)S(1)} %get-tuple-element.887, ...), kind=kOutput, calls=%fused_computation.36.clone.1 | convolution fusion | flops 171376640 | bytes 6565120 | tf_op jit(solution)/shard_map/while/body/hqk,khd->hqd/dot_general | solution.py:44
  58.5 0.7 dynamic_slice.87
  60.1 0.7 fusion.98
  60.7 1.2 select_select_fusion.5
  62.7 1.1 constant_dynamic-slice_fusion.10
  63.8 2.0 fusion.99
  65.8 1.2 fusion.100
  69.1 0.8 and_reduce_fusion.12
  69.9 0.7 fusion.101
  70.6 0.8 and_reduce_fusion.11
  71.4 4.2 %select_dynamic-update-slice_fusion.5 = f32[2,20,128,128]{3,2,1,0:T(8,128)} fusion(f32[2,20,128,128]{3,2,1,0:T(8,128)} %get-tuple-element.974, s32[]{:T(128)} %select_n.324, bf16[256,20,128]{0,2,1:T(8,128)(2,1)} %bitcast.138, f32[20,128,256]{2,1,0:T(8,128)S(1)} %get-tuple-element.886, f32[20,128]{1,0:T(8,128)S(1)} %get-tuple-element.887, ...), kind=kOutput, calls=%fused_computation.36.clone.1 | convolution fusion | flops 171376640 | bytes 6565120 | tf_op jit(solution)/shard_map/while/body/hqk,khd->hqd/dot_general | solution.py:44
  76.3 3.4 %fusion.54 = (bf16[256,1,2560]{0,2,1:T(8,128)(2,1)}, bf16[256,1,2560]{0,2,1:T(8,128)(2,1)}) fusion(bf16[256,2,2560]{0,2,1:T(8,128)(2,1)} %collective-permute-done), kind=kLoop, calls=%fused_computation.89 | loop fusion | bytes 5242880 | tf_op jit(solution)/shard_map/slice | solution.py:109
  79.7 1.8 broadcast.442.clone
  81.5 34.7 %while.46 = (s32[]{:T(128)}, f32[2,20,128,128]{3,2,1,0:T(8,128)}, f32[2,20,128]{2,1,0:T(8,128)S(1)}, f32[2,20,128]{2,1,0:T(8,128)S(1)}, s32[]{:T(128)}, /*index=...) while((s32[]{:T(128)}, f32[2,20,128,128]{3,2,1,0:T(8,128)}, ...), condition=%wide.region_14.16_spmd.clone, body=%wide.region_8.15_spmd.clone.sunk | while | flops 344394592 | bytes 15190500 | solution.py:72
  82.2 0.6 dynamic_slice.84
  83.7 0.6 fusion.89
  84.3 1.2 select_select_fusion.4
  86.1 1.1 constant_dynamic-slice_fusion.9
  87.2 2.0 fusion.90
  89.2 1.2 fusion.91
  92.3 0.7 and_reduce_fusion.10
  93.0 0.6 fusion.92
  93.6 0.7 and_reduce_fusion.9
  94.4 4.1 %select_dynamic-update-slice_fusion.4 = f32[2,20,128,128]{3,2,1,0:T(8,128)} fusion(f32[2,20,128,128]{3,2,1,0:T(8,128)} %get-tuple-element.912, s32[]{:T(128)} %select_n.313, bf16[256,20,128]{0,2,1:T(8,128)(2,1)} %bitcast.137, f32[20,128,256]{2,1,0:T(8,128)S(1)} %get-tuple-element.869, f32[20,128]{1,0:T(8,128)S(1)} %get-tuple-element.870, ...), kind=kOutput, calls=%fused_computation.8.clone.1 | convolution fusion | flops 171376640 | bytes 6565120 | tf_op jit(solution)/shard_map/while/body/hqk,khd->hqd/dot_general | solution.py:44
  99.2 0.6 dynamic_slice.84
  100.6 0.6 fusion.89
  101.2 1.2 select_select_fusion.4
  103.0 1.1 constant_dynamic-slice_fusion.9
  104.2 2.0 fusion.90
  106.2 1.2 fusion.91
  109.2 0.7 and_reduce_fusion.10
  109.9 0.6 fusion.92
  110.6 0.7 and_reduce_fusion.9
  111.3 4.1 %select_dynamic-update-slice_fusion.4 = f32[2,20,128,128]{3,2,1,0:T(8,128)} fusion(f32[2,20,128,128]{3,2,1,0:T(8,128)} %get-tuple-element.912, s32[]{:T(128)} %select_n.313, bf16[256,20,128]{0,2,1:T(8,128)(2,1)} %bitcast.137, f32[20,128,256]{2,1,0:T(8,128)S(1)} %get-tuple-element.869, f32[20,128]{1,0:T(8,128)S(1)} %get-tuple-element.870, ...), kind=kOutput, calls=%fused_computation.8.clone.1 | convolution fusion | flops 171376640 | bytes 6565120 | tf_op jit(solution)/shard_map/while/body/hqk,khd->hqd/dot_general | solution.py:44
  116.4 5.1 %fusion.42 = bf16[2,128,20,128]{3,1,2,0:T(8,128)(2,1)S(1)} fusion(f32[2,20,128]{2,1,0:T(8,128)S(1)} %get-tuple-element.703, f32[2,20,128,128]{3,2,1,0:T(8,128)} %get-tuple-element.525, f32[2,20,128]{2,1,0:T(8,128)S(1)} %get-tuple-element.705, f32[2,20,128,128]{3,2,1,0:T(8,128)} %get-tuple-element.522, f32[2,20,128]{2,1,0:T(8,128)S(1)} %get-tuple-element.704), kind=kLoop, calls=%fused_computation.66 | loop fusion | flops 3276800 | bytes 6615040 | tf_op jit(solution)/shard_map/convert_element_type | solution.py:119
  121.5 1.0 copy.38
  122.8 3.0 %collective-permute-done.1 = bf16[256,2560]{0,1:T(8,128)(2,1)S(1)} collective-permute-done((bf16[256,2560]{0,1:T(8,128)(2,1)S(1)}, bf16[256,2560]{0,1:T(8,128)(2,1)S(1)}, u32[]{:S(2)}, u32[]{:S(2)}) %collective-permute-start.1) | collective-permute-done | bytes 1310752 | tf_op jit(solution)/shard_map/ppermute | solution.py:22
  125.8 91.8 %all-gather.2.cloned.1.call-done = bf16[2560,2560]{1,0:T(8,128)(2,1)} async-done(((bf16[320,2560]{1,0:T(8,128)(2,1)}), bf16[2560,2560]{1,0:T(8,128)(2,1)}) %all-gather.2.cloned.1.call-update) | async-done | bytes 13107216 | tf_op jit(solution)/shard_map/all_gather | solution.py:123
  217.6 8.1 %fusion.56 = f32[256,2560]{1,0:T(8,128)} fusion(bf16[256,2560]{0,1:T(8,128)(2,1)S(1)} %collective-permute-done.1, bf16[2560,2560]{1,0:T(8,128)(2,1)} %all-gather.2.cloned.1.call-done), kind=kOutput, calls=%fused_computation.91 | convolution fusion | flops 3355443200 | bytes 17039360 | tf_op jit(solution)/shard_map/dot_general | solution.py:126
  225.7 6.8 %fusion.48 = f32[256,2560]{1,0:T(8,128)S(1)} fusion(bf16[2560,2560]{1,0:T(8,128)(2,1)} %all-gather.2.cloned.1.call-done, bf16[320,8,2,128]{3,2,1,0:T(2,128)(2,1)S(1)} %bitcast.136), kind=kOutput, calls=%fused_computation.85 | convolution fusion | flops 3355443200 | bytes 17039360 | tf_op jit(solution)/shard_map/dot_general | solution.py:125
  232.6 5.0 %fusion.41 = bf16[256,5120]{1,0:T(8,128)(2,1)} fusion(bf16[256,5120]{1,0:T(8,128)(2,1)S(1)} %copy-done.2, f32[256,2560]{1,0:T(8,128)S(1)} %fusion.48, f32[256,2560]{1,0:T(8,128)} %collective-permute-done.2, f32[5120]{0:T(1024)S(1)} %copy-done.5, pred[256]{0:T(512)(128)(4,1)S(1)} %and_select_fusion, pred[]{:T(512)S(6)} %eq.84), kind=kLoop, calls=%fused_computation.62 | loop fusion | flops 10485760 | bytes 10506497 | tf_op jit(solution)/shard_map/jit(_where)/select_n | solution.py:134
  (43 shorter events, 1.4 us)
Async XLA Ops:
  6.5 24.4 %copy-start = (bf16[320,5120]{1,0:T(8,128)(2,1)S(1)}, bf16[320,5120]{1,0:T(8,128)(2,1)}, u32[]{:S(2)}) copy-start(bf16[320,5120]{1,0:T(8,128)(2,1)} %param.41) | copy-start | bytes 9830404
  6.5 211.1 %all-gather.2.cloned.1.call-start = ((), (), s32[]{:S(2)}) async-start(), calls=%async_computation | async-start | bytes 14745600 | tf_op jit(solution)/shard_map/all_gather | solution.py:123
  30.4 45.9 %collective-permute-start = (bf16[256,2,2560]{0,2,1:T(8,128)(2,1)}, bf16[256,2,2560]{0,2,1:T(8,128)(2,1)}, u32[]{:S(2)}, u32[]{:S(2)}) collective-permute-start(bf16[256,2,2560]{0,2,1:T(8,128)(2,1)} %broadcast_select_fusion), channel_id=1, source_target_pairs={{0,1},{1,0},{2,3},{3,2},{4,5},{5,4},{6,7},{7,6},{8,9},{9,8},{10,11... | collective-permute-start | bytes 7864328 | tf_op jit(solution)/shard_map/ppermute | solution.py:22
  32.2 2.5 %copy-start.6 = (s32[1,4,3]{1,0,2:T(1,128)S(1)}, s32[1,4,3]{1,0,2:T(1,128)}, u32[]{:S(2)}) copy-start(s32[1,4,3]{1,0,2:T(1,128)} %param.40) | copy-start | bytes 148
  38.1 1.8 copy-start.3
  38.1 1.8 copy-start.4
  122.7 3.1 %collective-permute-start.1 = (bf16[256,2560]{0,1:T(8,128)(2,1)S(1)}, bf16[256,2560]{0,1:T(8,128)(2,1)S(1)}, u32[]{:S(2)}, u32[]{:S(2)}) collective-permute-start(bf16[256,2560]{0,1:T(8,128)(2,1)S(1)} %bitcast.139), channel_id=1, source_target_pairs={{0,1},{1,0},{2,3},{3,2},{4,5},{5,4},{6,7},{7,6},{8,9},{9,8},{10,11... | collective-permute-start | bytes 3932168 | tf_op jit(solution)/shard_map/ppermute | solution.py:22
  225.7 6.9 %collective-permute-start.2 = (f32[256,2560]{1,0:T(8,128)}, f32[256,2560]{1,0:T(8,128)}, u32[]{:S(2)}, u32[]{:S(2)}) collective-permute-start(f32[256,2560]{1,0:T(8,128)} %fusion.56), channel_id=1, source_target_pairs={{0,1},{1,0},{2,3},{3,2},{4,5},{5,4},{6,7},{7,6},{8,9},{9,8},{10,11... | collective-permute-start | bytes 7864328 | tf_op jit(solution)/shard_map/ppermute | solution.py:22
  225.7 6.9 %copy-start.2 = (bf16[256,5120]{1,0:T(8,128)(2,1)S(1)}, bf16[256,5120]{1,0:T(8,128)(2,1)}, u32[]{:S(2)}) copy-start(bf16[256,5120]{1,0:T(8,128)(2,1)} %param.33) | copy-start | bytes 7864324
  225.7 6.9 %copy-start.5 = (f32[5120]{0:T(1024)S(1)}, f32[5120]{0:T(1024)}, u32[]{:S(2)}) copy-start(f32[5120]{0:T(1024)} %param.34) | copy-start | bytes 61444
  232.6 5.0 %copy-start.1 = (bf16[320,5120]{1,0:T(8,128)(2,1)S(1)}, bf16[320,5120]{1,0:T(8,128)(2,1)}, u32[]{:S(2)}) copy-start(bf16[320,5120]{1,0:T(8,128)(2,1)} %param.41) | copy-start | bytes 9830404
Sparse Core Ops, SparseCore 0:
  32.3 185.2 all-gather.1
where the time goes:
time: 246 us; the launch traced here: 244 us
  waiting for transfers between devices  94.8 us (39%)
  local copies, waits for them, and re-layouts  42.6 us (17%)
  matrix products  39.6 us (16%)
  other arithmetic  35.8 us (15%)
  loops' own time  17.6 us (7%)
  between operations  13.5 us (5%)
    all_gather x1, waiting for transfers between devices, local(): half_weight = lax.all_gather(own_cols, 'fsdp', axis=0, tiled=True)  91.8 us
    another operation x2, loops' own time, attend_block(): return lax.fori_loop(0, tile_count, one_slot, init_state)  17.6 us
    unnamed x19, local copies, waits for them, and re-layouts  17.4 us
    dot_general x4, matrix products, block_partial(): jnp.einsum('hqk,khd->hqd', weights, value3, preferred_element_type=jnp.fl...  16.6 us
    dot_general x1, matrix products, local(): jnp.dot(partner_rows, half_weight, preferred_element_type=jnp.float32)  8.14 us
    dot_general x4, matrix products, block_partial(): jnp.einsum('qhd,khd->hqk', query3, key3, preferred_element_type=jnp.float32)  7.95 us
    dot_general x1, matrix products, local(): jnp.dot(attended, half_weight, preferred_element_type=jnp.float32)  6.85 us
    another operation x8, other arithmetic  6.15 us
  transfers between devices with their start and end apart: 4, of which 2 were waited for; matrix products, arithmetic and copies ran while one was open for 33% of the time, Pallas kernels for 0%

commit v1 on v0

v1 whole, which is shorter than its diff:
```python
import functools
import math

import jax
import jax.numpy as jnp
from jax import lax
from jax.experimental import pallas as pl
from jax.experimental.pallas import tpu as pltpu
from jax.sharding import PartitionSpec as P

HEAD_DIM = 128
MASKED = -1e30
LANES = 256
VMEM_BYTES = 48 << 20


def params():
    return pltpu.CompilerParams(vmem_limit_bytes=VMEM_BYTES)


def exchanged(block, axis):
    return lax.ppermute(block, axis, [(0, 1), (1, 0)])


def ring_order(count):
    return list(range(0, count, 2)) + list(range(count - 1, 0, -2))


def resident_kernel(flags_ref, fresh_ref, cache_ref, out_ref, held, sems):
    tiles, rows = held.shape[0], held.shape[1]
    width = held.shape[3]

    def copy(source, tile):
        return pltpu.make_async_copy(
            source.at[pl.ds(tile * rows, rows)], held.at[tile], sems.at[tile]
        )

    for tile in range(tiles):

        @pl.when(flags_ref[tile] != 0)
        def _(tile=tile):
            copy(fresh_ref, tile).start()

        @pl.when(flags_ref[tile] == 0)
        def _(tile=tile):
            copy(cache_ref, tile).start()

    to_row = lax.broadcasted_iota(jnp.int32, (2 * rows, 2 * rows), 0)
    from_row = lax.broadcasted_iota(jnp.int32, (2 * rows, 2 * rows), 1)
    wanted = jnp.where(to_row < rows, 2 * to_row, 2 * (to_row - rows) + 1)
    order = (from_row == wanted).astype(jnp.bfloat16)
    for tile in range(tiles):
        copy(fresh_ref, tile).wait()
        pairs = held[tile].reshape(2 * rows, width)
        sorted_rows = jnp.dot(order, pairs, preferred_element_type=jnp.float32)
        sorted_rows = sorted_rows.astype(jnp.bfloat16)
        out_ref[0, tile * rows : (tile + 1) * rows] = sorted_rows[:rows]
        out_ref[1, tile * rows : (tile + 1) * rows] = sorted_rows[rows:]


def resident_planes(flags, fresh, cache):
    tokens, _, width = fresh.shape
    tiles = flags.shape[0]
    rows = tokens // tiles
    return pl.pallas_call(
        resident_kernel,
        out_shape=jax.ShapeDtypeStruct((2, tokens, width), jnp.bfloat16),
        in_specs=[
            pl.BlockSpec(memory_space=pltpu.SMEM),
            pl.BlockSpec(memory_space=pl.ANY),
            pl.BlockSpec(memory_space=pl.ANY),
        ],
        out_specs=pl.BlockSpec(memory_space=pltpu.VMEM),
        scratch_shapes=[
            pltpu.VMEM((tiles, rows, 2, width), jnp.bfloat16),
            pltpu.SemaphoreType.DMA((tiles,)),
        ],
        compiler_params=params(),
        cost_estimate=pl.CostEstimate(
            flops=8 * tokens * rows * width, bytes_accessed=8 * tokens * width, transcendentals=0
        ),
        name="resident",
    )(flags, fresh, cache)


def attend_kernel(heads, mask_ref, q_ref, own_ref, other_ref, out_ref, bias_ref):
    tiles = mask_ref.shape[0]
    rows = q_ref.shape[0] // tiles
    keys = own_ref.shape[1]
    for side in range(2):
        for query in range(tiles):
            for key in range(tiles):
                bias_ref[side, query * rows : (query + 1) * rows, key * rows : (key + 1) * rows] = (
                    jnp.full((rows, rows), mask_ref[query, side * tiles + key], jnp.float32)
                )
    scale = math.log2(math.e) / math.sqrt(HEAD_DIM)
    contract_last = (((1,), (1,)), ((), ()))
    for head in range(heads):
        cols = slice(head * HEAD_DIM, (head + 1) * HEAD_DIM)
        query_head = q_ref[:, cols]
        scores = [
            lax.dot_general(
                query_head, ref[0, :, cols], contract_last, preferred_element_type=jnp.float32
            )
            * scale
            + bias_ref[side]
            for side, ref in enumerate((own_ref, other_ref))
        ]
        row_max = jnp.max(jnp.maximum(scores[0], scores[1]), axis=1, keepdims=True)
        terms = [jnp.exp2(part - row_max) for part in scores]
        total = jnp.sum(terms[0] + terms[1], axis=1, keepdims=True)
        summed = jnp.dot(
            terms[0].astype(jnp.bfloat16), own_ref[1, :, cols], preferred_element_type=jnp.float32
        ) + jnp.dot(
            terms[1].astype(jnp.bfloat16), other_ref[1, :, cols], preferred_element_type=jnp.float32
        )
        out_ref[:, cols] = (summed / total).astype(jnp.bfloat16)


def attended_heads(mask, queries, own, other, first, count, step):
    tokens = queries.shape[0]
    start = first // step
    width = step * HEAD_DIM
    kv_spec = pl.BlockSpec((2, tokens, width), lambda i: (0, 0, start + i))
    return pl.pallas_call(
        functools.partial(attend_kernel, step),
        grid=(count // step,),
        out_shape=jax.ShapeDtypeStruct((tokens, count * HEAD_DIM), jnp.bfloat16),
        in_specs=[
            pl.BlockSpec(memory_space=pltpu.SMEM),
            pl.BlockSpec((tokens, width), lambda i: (0, start + i)),
            kv_spec,
            kv_spec,
        ],
        out_specs=pl.BlockSpec((tokens, width), lambda i: (0, i)),
        scratch_shapes=[pltpu.VMEM((2, tokens, tokens), jnp.float32)],
        compiler_params=params(),
        cost_estimate=pl.CostEstimate(
            flops=8 * tokens * tokens * count * HEAD_DIM,
            bytes_accessed=12 * tokens * count * HEAD_DIM,
            transcendentals=2 * tokens * tokens * count,
        ),
        name="attend",
    )(mask, queries, own, other)


def project_kernel(pieces, halves, blocks, *refs):
    offsets_ref = refs[0]
    piece_refs = refs[1 : 1 + pieces]
    row_refs = refs[1 + pieces : 1 + pieces + halves * blocks]
    out_refs = refs[1 + pieces + halves * blocks : -2]
    weight, sems = refs[-2:]

    def copy(index):
        rows = piece_refs[index].shape[0]
        start = pl.multiple_of(offsets_ref[index], 16)
        return pltpu.make_async_copy(
            piece_refs[index], weight.at[pl.ds(start, rows)], sems.at[index]
        )

    for index in range(pieces):
        copy(index).start()
    for index in range(pieces):
        copy(index).wait()
    depth = weight.shape[0] // halves

    def one_step(step, _):
        cols = pl.ds(pl.multiple_of(step * LANES, LANES), LANES)
        for block in range(blocks):
            total = None
            for half in range(halves):
                part = jnp.dot(
                    row_refs[block * halves + half][...],
                    weight[half * depth : (half + 1) * depth, cols],
                    preferred_element_type=jnp.float32,
                )
                total = part if total is None else total + part
            rows = total.shape[0]
            if len(out_refs) == 1:
                out_refs[0][block * rows : (block + 1) * rows, cols] = total.astype(
                    out_refs[0].dtype
                )
            else:
                out_refs[block][:, cols] = total.astype(out_refs[block].dtype)
        return 0

    lax.fori_loop(0, weight.shape[1] // LANES, one_step, 0)


def projected_rows(offsets, pieces, row_blocks, out_shapes):
    halves = len(row_blocks[0])
    depth = halves * row_blocks[0][0].shape[1]
    cols = pieces[0].shape[1]
    rows = sum(parts[0].shape[0] for parts in row_blocks)
    vmem = pl.BlockSpec(memory_space=pltpu.VMEM)
    single = len(out_shapes) == 1
    result = pl.pallas_call(
        functools.partial(project_kernel, len(pieces), halves, len(row_blocks)),
        out_shape=out_shapes,
        in_specs=[pl.BlockSpec(memory_space=pltpu.SMEM)]
        + [pl.BlockSpec(memory_space=pl.ANY)] * len(pieces)
        + [vmem] * (halves * len(row_blocks)),
        out_specs=[vmem] * len(out_shapes),
        scratch_shapes=[
            pltpu.VMEM((depth, cols), jnp.bfloat16),
            pltpu.SemaphoreType.DMA((len(pieces),)),
        ],
        compiler_params=params(),
        cost_estimate=pl.CostEstimate(
            flops=2 * rows * depth * cols,
            bytes_accessed=2 * depth * (rows + cols) + 2 * rows * cols,
            transcendentals=0,
        ),
        name="project",
    )(offsets, *pieces, *[part for parts in row_blocks for part in parts])
    return result[0] if single else result


def finish_kernel(places_ref, flags_ref, input_ref, gate_ref, *refs):
    sources, out_ref = refs[:4], refs[-1]
    source = pl.program_id(0)
    tiles = flags_ref.shape[0]
    rows = out_ref.shape[0] // tiles
    for index in range(4):

        @pl.when(source == index)
        def _(index=index):
            for tile in range(tiles):
                span = slice(tile * rows, (tile + 1) * rows)

                @pl.when(flags_ref[tile] != 0)
                def _(span=span):
                    out_ref[span] = (
                        input_ref[span].astype(jnp.float32)
                        + gate_ref[...] * sources[index][span].astype(jnp.float32)
                    ).astype(jnp.bfloat16)

                @pl.when(flags_ref[tile] == 0)
                def _(span=span):
                    out_ref[span] = input_ref[span]


def finished(places, flags, block_input, gate, sources, offset, width, earlier):
    tokens, total = block_input.shape
    per_quarter = total // 4 // LANES
    start, steps = offset // LANES, width // LANES

    def wide(source, step, places, flags):
        return (0, places[source] * per_quarter + start + step)

    def narrow(index):
        def at(source, step, places, flags):
            return (0, jnp.where(source == index, step, jnp.where(source < index, 0, steps - 1)))

        return at

    in_specs = [
        pl.BlockSpec((tokens, LANES), wide),
        pl.BlockSpec((1, LANES), wide),
    ] + [pl.BlockSpec((tokens, LANES), narrow(index)) for index in range(4)]
    args = [block_input, gate[None], *sources]
    aliases = {}
    if earlier is not None:
        in_specs.append(pl.BlockSpec(memory_space=pl.ANY))
        args.append(earlier)
        aliases = {len(args) + 1: 0}
    return pl.pallas_call(
        finish_kernel,
        grid_spec=pltpu.PrefetchScalarGridSpec(
            num_scalar_prefetch=2,
            grid=(4, steps),
            in_specs=in_specs,
            out_specs=pl.BlockSpec((tokens, LANES), wide),
        ),
        out_shape=jax.ShapeDtypeStruct((tokens, total), jnp.bfloat16),
        input_output_aliases=aliases,
        compiler_params=params(),
        cost_estimate=pl.CostEstimate(
            flops=8 * tokens * width, bytes_accessed=24 * tokens * width, transcendentals=0
        ),
        name="finish",
    )(places, flags, *args)


def gathered(columns, position, order):
    count, rows = len(order), columns.shape[0]
    place = [0] * count
    for index, device in enumerate(order):
        place[device] = index
    place = jnp.array(place, jnp.int32)[position]
    order_table = jnp.array(order, jnp.int32)
    ahead = [(order[index], order[(index + 1) % count]) for index in range(count)]
    behind = [(to, start) for start, to in ahead]
    pieces, offsets = [columns], [position * rows]
    from_behind = from_ahead = columns
    for step in range(1, (count + 1) // 2):
        from_behind = lax.ppermute(from_behind, "fsdp", ahead)
        from_ahead = lax.ppermute(from_ahead, "fsdp", behind)
        pieces += [from_behind, from_ahead]
        offsets += [
            order_table[(place - step + count) % count] * rows,
            order_table[(place + step) % count] * rows,
        ]
    if count % 2 == 0:
        half = rows // 2
        opposite = order_table[(place + count // 2) % count] * rows
        pieces += [
            lax.ppermute(from_behind[:half], "fsdp", ahead),
            lax.ppermute(from_ahead[half:], "fsdp", behind),
        ]
        offsets += [opposite, opposite + half]
    return pieces, jnp.stack(offsets).astype(jnp.int32)


def local(
    block_input, gate, q_fresh, kv_fresh, kv_cache, active_list, active_count, key_list, out_weight
):
    part, position, side = (lax.axis_index(axis) for axis in ("groups", "fsdp", "blk"))
    positions = lax.axis_size("fsdp")
    tiles = active_list.shape[2]
    tokens, total = block_input.shape
    depth = q_fresh.shape[1]
    heads = depth // HEAD_DIM
    quarter = total // 4

    splits = (quarter,)
    ringed = positions == 8 and out_weight.shape[0] % 32 == 0
    weights, offset = [], 0
    for width in splits:
        columns = lax.dynamic_slice_in_dim(
            out_weight, (part * 2 + side) * quarter + offset, width, 1
        )
        if ringed:
            weights.append(gathered(columns, position, ring_order(positions)))
        else:
            whole = lax.all_gather(columns, "fsdp", axis=0, tiled=True)
            weights.append(([whole], jnp.zeros((1,), jnp.int32)))
        offset += width

    own_list, own_count = active_list[0, side], active_count[0, side]
    slots = jnp.arange(tiles, dtype=jnp.int32)
    flags = jnp.any(
        (own_list[:, None] == slots[None, :]) & (slots[:, None] < own_count), axis=0
    ).astype(jnp.int32)
    listed = lax.dynamic_slice_in_dim(key_list[0], side * tiles, tiles, 0)
    tile_ids = jnp.concatenate([side * tiles + slots, (1 - side) * tiles + slots])
    allowed = jnp.any(listed[:, :, None] == tile_ids[None, None, :], axis=1)
    mask = jnp.where(allowed, 0.0, MASKED).astype(jnp.float32)

    own_kv = resident_planes(flags, kv_fresh, kv_cache)
    other_kv = exchanged(own_kv, "blk")
    own_rows = [
        attended_heads(mask, q_fresh, own_kv, other_kv, first, heads // 2, heads // 4)
        for first in (0, heads // 2)
    ]
    far_rows = [exchanged(rows, "groups") for rows in own_rows]
    near_rows = [exchanged(rows, "blk") for rows in own_rows]
    far_near_rows = [exchanged(rows, "blk") for rows in far_rows]

    places = jnp.stack(
        [
            part * 2 + side,
            part * 2 + 1 - side,
            (1 - part) * 2 + side,
            (1 - part) * 2 + 1 - side,
        ]
    ).astype(jnp.int32)
    result, offset = None, 0
    for width, (pieces, offsets) in zip(splits, weights):
        one = jax.ShapeDtypeStruct((tokens, width), jnp.bfloat16)
        two = jax.ShapeDtypeStruct((2 * tokens, width), jnp.bfloat16)
        away = projected_rows(offsets, pieces, [far_rows, far_near_rows], [two])
        back = exchanged(away, "groups")
        own_part, near_part = projected_rows(offsets, pieces, [own_rows, near_rows], [one, one])
        sources = [
            own_part,
            exchanged(near_part, "blk"),
            back[:tokens],
            exchanged(back[tokens:], "blk"),
        ]
        result = finished(places, flags, block_input, gate, sources, offset, width, result)
        offset += width
    return result


def solution(mesh):
    in_specs = (
        P(("groups", "fsdp", "blk"), None),
        P("groups"),
        P(("groups", "fsdp", "blk"), None),
        P(("groups", "fsdp", "blk"), None, None),
        P(("groups", "fsdp", "blk"), None, None),
        P(("groups", "fsdp"), None, None),
        P(("groups", "fsdp"), None),
        P(("groups", "fsdp"), None, None),
        P("fsdp", None),
    )
    out_specs = P(("groups", "fsdp", "blk"), None)
    return jax.shard_map(local, mesh=mesh, in_specs=in_specs, out_specs=out_specs, check_vma=False)
```

time: 246 us -> 147 us (0.60)
  Pallas kernels: 0 us -> 43.8 us
  matrix products: 39.6 us -> 0 us
  other arithmetic: 35.8 us -> 1 us
  waiting for transfers between devices: 94.8 us -> 62.2 us
  local copies, waits for them, and re-layouts: 42.6 us -> 17 us
  loops' own time: 17.6 us -> 0 us
  starting transfers between devices: 0.59 us -> 13.7 us
  between operations: 13.5 us -> 9.18 us
    all_gather x1 -> x0, waiting for transfers between devices: 91.8 us -> none  [local(): half_weight = lax.all_gather(own_cols, 'fsdp', axis=0, tiled=True)]
    ppermute x3 -> x18, waiting for transfers between devices: 2.97 us -> 62.2 us  [the longest x10 37.4 us: exchanged(): return lax.ppermute(block, axis, [(0, 1), (1, 0)])]
    pallas_call x0 -> x6, Pallas kernels: none -> 43.8 us  [the longest x2 18.4 us: projected_rows(): pl.pallas_call(functools.partial(project_kernel, len(pieces), halves, len...]
    dot_general x10 -> x0, matrix products: 39.6 us -> none  [the longest x4 16.6 us: block_partial(): jnp.einsum('hqk,khd->hqd', weights, value3, preferred_element_type=jnp.fl...]
    another operation x2 -> x0, loops' own time: 17.6 us -> none  [attend_block(): return lax.fori_loop(0, tile_count, one_slot, init_state)]
    select_n x8 -> x1, other arithmetic: 14.2 us -> 0.01 us  [local(): mask = jnp.where(allowed, 0.0, MASKED).astype(jnp.float32)]
    ppermute x3 -> x18, starting transfers between devices: 0.59 us -> 13.7 us  [the longest x10 5.37 us: exchanged(): return lax.ppermute(block, axis, [(0, 1), (1, 0)])]
    unnamed x19 -> x34, local copies, waits for them, and re-layouts: 17.4 us -> 9.67 us
  transfers between devices with their start and end apart: 4 -> 18, of which waited for: 2 -> 11; matrix products, arithmetic and copies ran while one was open for 33% -> 4% of each run, Pallas kernels for 0% -> 12%
where the time goes in v1:
time: 147 us
  waiting for transfers between devices  62.2 us (42%)
  Pallas kernels  43.8 us (30%)
  local copies, waits for them, and re-layouts  17 us (12%)
  starting transfers between devices  13.7 us (9%)
  between operations  9.18 us (6%)
    ppermute x10, waiting for transfers between devices, exchanged(): return lax.ppermute(block, axis, [(0, 1), (1, 0)])  37.4 us
    ppermute x3, waiting for transfers between devices, gathered(): from_behind = lax.ppermute(from_behind, 'fsdp', ahead)  24.2 us
    pallas_call x2, Pallas kernels, projected_rows(): pl.pallas_call(functools.partial(project_kernel, len(pieces), halves, len...  18.4 us
    pallas_call x1, Pallas kernels, finished(): pl.pallas_call(finish_kernel, grid_spec=pltpu.PrefetchScalarGridSpec(num_...  11.5 us
    unnamed x34, local copies, waits for them, and re-layouts  9.67 us
    pallas_call x2, Pallas kernels, attended_heads(): pl.pallas_call(functools.partial(attend_kernel, step), grid=(count // ste...  9.45 us
    ppermute x10, starting transfers between devices, exchanged(): return lax.ppermute(block, axis, [(0, 1), (1, 0)])  5.37 us
    pallas_call x1, Pallas kernels, resident_planes(): pl.pallas_call(resident_kernel, out_shape=jax.ShapeDtypeStruct((2, tokens...  4.43 us
  transfers between devices with their start and end apart: 18, of which 11 were waited for; matrix products, arithmetic and copies ran while one was open for 4% of the time, Pallas kernels for 12%

profile of v1, /device:TPU:0, one launch (start us, length us, event | category | flops | bytes accessed | tf_op | source)
XLA Modules:
  0.0 146.9 jit_solution(2484381605178394942)
XLA Ops:
  0.0 1.4 constant_dynamic-slice_fusion.2
  1.4 0.6 iota_compare_fusion
  2.0 0.7 fusion
  2.7 0.1 and_reduce_fusion
  2.8 1.7 %copy-done.2 = bf16[256,2,2560]{2,1,0:T(2,128)(2,1)S(1)} copy-done((bf16[256,2,2560]{2,1,0:T(2,128)(2,1)S(1)}, bf16[256,2,2560]{2,1,0:T(2,128)(2,1)}, u32[]{:S(2)}) %copy-start.2) | copy-done | bytes 2621464
  4.6 4.4 %resident.1.own_ref = bf16[2,256,2560]{2,1,0:T(8,128)(2,1)} custom-call(s32[2]{0:T(128)S(1)} %convert_element_type.3.flags_ref, bf16[256,2,2560]{2,1,0:T(2,128)(2,1)S(1)} %copy-done.2, bf16[256,2,2560]{2,1,0:T(2,128)(2,1)} %cache_ref.1), custom_call_target="tpu_custom_call" | custom-call | flops 671088640 | bytes 5242880 | tf_op jit(solution)/shard_map/resident/pallas_call | solution.py:65
  9.0 0.5 collective-permute-start.8
  9.5 1.0 constant_dynamic-slice_fusion.1.refs_1_
  10.5 1.5 %collective-permute-start = (bf16[320,1280]{1,0:T(8,128)(2,1)}, bf16[320,1280]{1,0:T(8,128)(2,1)}, u32[]{:S(2)}, u32[]{:S(2)}) collective-permute-start(bf16[320,1280]{1,0:T(8,128)(2,1)} %constant_dynamic-slice_fusion.1.refs_1_), channel_id=1, source_target_pairs={{0,4},{4,8},{8,12},{12,14},{14,10},{10,6},{6,2},{2,0},{1,5},{5,9},... | collective-permute-start | bytes 2457608 | tf_op jit(solution)/shard_map/ppermute | solution.py:297
  12.0 0.8 collective-permute-start.1
  12.8 19.0 %collective-permute-done.refs_2_ = bf16[320,1280]{1,0:T(8,128)(2,1)} collective-permute-done((bf16[320,1280]{1,0:T(8,128)(2,1)}, bf16[320,1280]{1,0:T(8,128)(2,1)}, u32[]{:S(2)}, u32[]{:S(2)}) %collective-permute-start) | collective-permute-done | bytes 819232 | tf_op jit(solution)/shard_map/ppermute | solution.py:297
  31.8 1.2 collective-permute-start.2
  32.9 0.1 collective-permute-done.1.refs_3_
  33.0 0.8 collective-permute-start.3
  33.8 0.1 constant_dynamic-slice_fusion
  33.9 0.1 copy.13
  34.0 0.1 pad_add_fusion.1
  34.1 0.1 compare_reduce_fusion
  34.2 0.0 collective-permute-done.8.other_ref
  34.2 0.0 copy-start.1
  34.2 1.3 copy-done.1
  35.5 4.7 %attend.2.refs_10_ = bf16[256,1280]{1,0:T(8,128)(2,1)S(1)} custom-call(f32[2,4]{1,0:T(2,128)S(1)} %broadcast_select_fusion.mask_ref, bf16[256,2560]{1,0:T(8,128)(2,1)S(1)} %copy-done.1, bf16[2,256,2560]{2,1,0:T(8,128)(2,1)} %resident.1.own_ref, bf16[2,256,2560]{2,1,0:T(8,128)(2,1)} %collective-permute-done.8.other_ref), custom_call_target="tpu_custom_call" | custom-call | flops 671088640 | bytes 3932160 | tf_op jit(solution)/shard_map/attend/pallas_call | solution.py:125
  40.2 0.0 copy-start.16
  40.3 0.0 copy-start.14
  40.3 2.0 %collective-permute-start.12 = (bf16[256,1280]{1,0:T(8,128)(2,1)S(1)}, bf16[256,1280]{1,0:T(8,128)(2,1)}, u32[]{:S(2)}, u32[]{:S(2)}) collective-permute-start(bf16[256,1280]{1,0:T(8,128)(2,1)S(1)} %attend.2.refs_10_), channel_id=1, source_target_pairs={{0,16},{16,0},{1,17},{17,1},{2,18},{18,2},{3,19},{19,3},{4,20},{20... | collective-permute-start | bytes 1966088 | tf_op jit(solution)/shard_map/ppermute | solution.py:22
  42.3 4.7 %attend.3.refs_11_ = bf16[256,1280]{1,0:T(8,128)(2,1)S(1)} custom-call(f32[2,4]{1,0:T(2,128)S(1)} %broadcast_select_fusion.mask_ref, bf16[256,2560]{1,0:T(8,128)(2,1)S(1)} %copy-done.1, bf16[2,256,2560]{2,1,0:T(8,128)(2,1)} %resident.1.own_ref, bf16[2,256,2560]{2,1,0:T(8,128)(2,1)} %collective-permute-done.8.other_ref), custom_call_target="tpu_custom_call" | custom-call | flops 671088640 | bytes 3932160 | tf_op jit(solution)/shard_map/attend/pallas_call | solution.py:125
  47.1 0.2 collective-permute-start.13
  47.3 4.7 %collective-permute-done.2.refs_4_ = bf16[320,1280]{1,0:T(8,128)(2,1)} collective-permute-done((bf16[320,1280]{1,0:T(8,128)(2,1)}, bf16[320,1280]{1,0:T(8,128)(2,1)}, u32[]{:S(2)}, u32[]{:S(2)}) %collective-permute-start.2) | collective-permute-done | bytes 819232 | tf_op jit(solution)/shard_map/ppermute | solution.py:297
  52.0 1.1 collective-permute-start.4
  53.1 0.0 collective-permute-done.3.refs_5_
  53.1 0.9 collective-permute-start.5
  54.0 4.1 %collective-permute-done.12.refs_10_ = bf16[256,1280]{1,0:T(8,128)(2,1)} collective-permute-done((bf16[256,1280]{1,0:T(8,128)(2,1)S(1)}, bf16[256,1280]{1,0:T(8,128)(2,1)}, u32[]{:S(2)}, u32[]{:S(2)}) %collective-permute-start.12) | collective-permute-done | bytes 655392 | tf_op jit(solution)/shard_map/ppermute | solution.py:22
  58.1 12.6 %collective-permute-done.13.refs_11_ = bf16[256,1280]{1,0:T(8,128)(2,1)} collective-permute-done((bf16[256,1280]{1,0:T(8,128)(2,1)S(1)}, bf16[256,1280]{1,0:T(8,128)(2,1)}, u32[]{:S(2)}, u32[]{:S(2)}) %collective-permute-start.13) | collective-permute-done | bytes 655392 | tf_op jit(solution)/shard_map/ppermute | solution.py:22
  70.7 0.0 collective-permute-start.15
  70.7 0.5 collective-permute-done.4.refs_6_
  71.2 0.9 copy-done.12
  72.1 0.8 slice.16
  72.9 1.1 collective-permute-start.6
  74.0 0.9 copy-done.13
  75.0 0.8 slice.17
  75.7 0.9 collective-permute-start.7
  76.7 0.6 dynamic_slice.38
  81.9 0.7 fusion.2
  87.0 0.1 stack.35.refs_0_
  87.1 0.0 collective-permute-done.6.refs_8_
  87.1 0.6 collective-permute-done.7.refs_9_
  87.7 9.9 %project.3 = bf16[512,1280]{1,0:T(8,128)(2,1)} custom-call(s32[9]{0:T(128)S(1)} %stack.35.refs_0_, bf16[320,1280]{1,0:T(8,128)(2,1)} %constant_dynamic-slice_fusion.1.refs_1_, bf16[320,1280]{1,0:T(8,128)(2,1)} %collective-permute-done.refs_2_, bf16[320,1280]{1,0:T(8,128)(2,1)} %collective-permute-done.1.refs_3_, ...), custom_call_target="tpu_custom_call" | custom-call | flops 3355443200 | bytes 10485760 | tf_op jit(solution)/shard_map/project/pallas_call | solution.py:197
  97.6 1.9 %collective-permute-start.16 = (bf16[512,1280]{1,0:T(8,128)(2,1)}, bf16[512,1280]{1,0:T(8,128)(2,1)S(1)}, u32[]{:S(2)}, u32[]{:S(2)}) collective-permute-start(bf16[512,1280]{1,0:T(8,128)(2,1)} %project.3), channel_id=1, source_target_pairs={{0,16},{16,0},{1,17},{17,1},{2,18},{18,2},{3,19},{19,3},{4,20},{20... | collective-permute-start | bytes 3932168 | tf_op jit(solution)/shard_map/ppermute | solution.py:22
  99.5 0.5 collective-permute-start.9
  100.0 1.6 %collective-permute-done.10.refs_13_ = bf16[256,1280]{1,0:T(8,128)(2,1)S(1)} collective-permute-done((bf16[256,1280]{1,0:T(8,128)(2,1)S(1)}, bf16[256,1280]{1,0:T(8,128)(2,1)S(1)}, u32[]{:S(2)}, u32[]{:S(2)}) %collective-permute-start.10) | collective-permute-done | bytes 655392 | tf_op jit(solution)/shard_map/ppermute | solution.py:22
  101.6 0.9 collective-permute-done.9.refs_12_
  102.5 8.5 %project.2 = (bf16[256,1280]{1,0:T(8,128)(2,1)S(1)}, bf16[256,1280]{1,0:T(8,128)(2,1)}) custom-call(s32[9]{0:T(128)S(1)} %stack.35.refs_0_, bf16[320,1280]{1,0:T(8,128)(2,1)} %constant_dynamic-slice_fusion.1.refs_1_, bf16[320,1280]{1,0:T(8,128)(2,1)} %collective-permute-done.refs_2_, bf16[320,1280]{1,0:T(8,128)(2,1)} %collective-permute-done.1.refs_3_, ...), custom_call_target="tpu_custom_call" | custom-call | flops 3355443200 | bytes 10485760 | tf_op jit(solution)/shard_map/project/pallas_call | solution.py:197
  111.1 0.8 copy-done.9
  111.9 0.1 collective-permute-start.11
  112.1 15.9 %collective-permute-done.16 = bf16[512,1280]{1,0:T(8,128)(2,1)S(1)} collective-permute-done((bf16[512,1280]{1,0:T(8,128)(2,1)}, bf16[512,1280]{1,0:T(8,128)(2,1)S(1)}, u32[]{:S(2)}, u32[]{:S(2)}) %collective-permute-start.16) | collective-permute-done | bytes 1310752 | tf_op jit(solution)/shard_map/ppermute | solution.py:22
  127.9 1.1 fusion.1
  129.1 0.0 collective-permute-start.17
  129.1 0.1 pad_add_fusion.places_ref
  129.2 0.0 collective-permute-done.11.refs_1_
  129.2 2.4 %collective-permute-done.17.refs_3_ = bf16[256,1280]{1,0:T(8,128)(2,1)} collective-permute-done((bf16[256,1280]{1,0:T(8,128)(2,1)}, bf16[256,1280]{1,0:T(8,128)(2,1)}, u32[]{:S(2)}, u32[]{:S(2)}) %collective-permute-start.17) | collective-permute-done | bytes 655392 | tf_op jit(solution)/shard_map/ppermute | solution.py:22
  131.5 1.7 %copy-done.3 = bf16[256,5120]{1,0:T(8,128)(2,1)S(1)} copy-done((bf16[256,5120]{1,0:T(8,128)(2,1)S(1)}, bf16[256,5120]{1,0:T(8,128)(2,1)}, u32[]{:S(2)}) %copy-start.3) | copy-done | bytes 2621464
  133.3 1.1 copy-done.4
  134.3 1.1 copy-done.10
  135.4 11.5 %finish.1 = bf16[256,5120]{1,0:T(8,128)(2,1)} custom-call(s32[4]{0:T(128)S(1)} %pad_add_fusion.places_ref, s32[2]{0:T(128)S(1)} %convert_element_type.3.flags_ref, bf16[256,5120]{1,0:T(8,128)(2,1)S(1)} %copy-done.3, f32[1,5120]{1,0:T(1,128)S(1)} %bitcast.17, bf16[256,1280]{1,0:T(8,128)(2,1)S(1)} %copy-done.10, ...), custom_call_target="tpu_custom_call" | custom-call | flops 2621440 | bytes 7864320 | tf_op jit(solution)/shard_map/finish/pallas_call | solution.py:267
  (31 shorter events, 0.1 us)
Async XLA Ops:
  0.0 9.5 %copy-start = (bf16[320,5120]{1,0:T(8,128)(2,1)S(1)}, bf16[320,5120]{1,0:T(8,128)(2,1)}, u32[]{:S(2)}) copy-start(bf16[320,5120]{1,0:T(8,128)(2,1)} %param.19) | copy-start | bytes 9830404
  2.8 1.7 %copy-start.2 = (bf16[256,2,2560]{2,1,0:T(2,128)(2,1)S(1)}, bf16[256,2,2560]{2,1,0:T(2,128)(2,1)}, u32[]{:S(2)}) copy-start(bf16[256,2,2560]{2,1,0:T(2,128)(2,1)} %fresh_ref.1) | copy-start | bytes 7864324
  4.6 29.3 %copy-start.15 = (s32[1,4,3]{1,0,2:T(1,128)S(1)}, s32[1,4,3]{1,0,2:T(1,128)}, u32[]{:S(2)}) copy-start(s32[1,4,3]{1,0,2:T(1,128)} %param.18) | copy-start | bytes 148
  9.0 25.2 %collective-permute-start.8 = (bf16[2,256,2560]{2,1,0:T(8,128)(2,1)}, bf16[2,256,2560]{2,1,0:T(8,128)(2,1)}, u32[]{:S(2)}, u32[]{:S(2)}) collective-permute-start(bf16[2,256,2560]{2,1,0:T(8,128)(2,1)} %resident.1.own_ref), channel_id=1, source_target_pairs={{0,1},{1,0},{2,3},{3,2},{4,5},{5,4},{6,7},{7,6},{8,9},{9,8},{10,11... | collective-permute-start | bytes 7864328 | tf_op jit(solution)/shard_map/ppermute | solution.py:22
  10.5 21.3 %collective-permute-start = (bf16[320,1280]{1,0:T(8,128)(2,1)}, bf16[320,1280]{1,0:T(8,128)(2,1)}, u32[]{:S(2)}, u32[]{:S(2)}) collective-permute-start(bf16[320,1280]{1,0:T(8,128)(2,1)} %constant_dynamic-slice_fusion.1.refs_1_), channel_id=1, source_target_pairs={{0,4},{4,8},{8,12},{12,14},{14,10},{10,6},{6,2},{2,0},{1,5},{5,9},... | collective-permute-start | bytes 2457608 | tf_op jit(solution)/shard_map/ppermute | solution.py:297
  12.0 21.0 %collective-permute-start.1 = (bf16[320,1280]{1,0:T(8,128)(2,1)}, bf16[320,1280]{1,0:T(8,128)(2,1)}, u32[]{:S(2)}, u32[]{:S(2)}) collective-permute-start(bf16[320,1280]{1,0:T(8,128)(2,1)} %constant_dynamic-slice_fusion.1.refs_1_), channel_id=1, source_target_pairs={{4,0},{8,4},{12,8},{14,12},{10,14},{6,10},{2,6},{0,2},{5,1},{9,5},... | collective-permute-start | bytes 2457608 | tf_op jit(solution)/shard_map/ppermute | solution.py:298
  31.8 20.2 %collective-permute-start.2 = (bf16[320,1280]{1,0:T(8,128)(2,1)}, bf16[320,1280]{1,0:T(8,128)(2,1)}, u32[]{:S(2)}, u32[]{:S(2)}) collective-permute-start(bf16[320,1280]{1,0:T(8,128)(2,1)} %collective-permute-done.refs_2_), channel_id=1, source_target_pairs={{0,4},{4,8},{8,12},{12,14},{14,10},{10,6},{6,2},{2,0},{1,5},{5,9},... | collective-permute-start | bytes 2457608 | tf_op jit(solution)/shard_map/ppermute | solution.py:297
  33.0 20.1 %collective-permute-start.3 = (bf16[320,1280]{1,0:T(8,128)(2,1)}, bf16[320,1280]{1,0:T(8,128)(2,1)}, u32[]{:S(2)}, u32[]{:S(2)}) collective-permute-start(bf16[320,1280]{1,0:T(8,128)(2,1)} %collective-permute-done.1.refs_3_), channel_id=1, source_target_pairs={{4,0},{8,4},{12,8},{14,12},{10,14},{6,10},{2,6},{0,2},{5,1},{9,5},... | collective-permute-start | bytes 2457608 | tf_op jit(solution)/shard_map/ppermute | solution.py:298
  34.2 1.3 copy-start.1
  40.2 6.8 %copy-start.5 = (bf16[256,1280]{1,0:T(8,128)(2,1)}, bf16[256,1280]{1,0:T(8,128)(2,1)S(1)}, u32[]{:S(2)}) copy-start(bf16[256,1280]{1,0:T(8,128)(2,1)S(1)} %attend.2.refs_10_) | copy-start | bytes 1966084
  40.2 36.4 %copy-start.16 = (s32[8]{0:T(128)S(1)}, s32[8]{0:T(128)}, u32[]{:S(2)}) copy-start(s32[8]{0:T(128)} %constant.105.clone) | copy-start | bytes 100
  40.3 41.6 %copy-start.14 = (s32[8]{0:T(128)S(1)}, s32[8]{0:T(128)}, u32[]{:S(2)}) copy-start(s32[8]{0:T(128)} %constant.106.clone) | copy-start | bytes 100
  40.3 17.8 %collective-permute-start.12 = (bf16[256,1280]{1,0:T(8,128)(2,1)S(1)}, bf16[256,1280]{1,0:T(8,128)(2,1)}, u32[]{:S(2)}, u32[]{:S(2)}) collective-permute-start(bf16[256,1280]{1,0:T(8,128)(2,1)S(1)} %attend.2.refs_10_), channel_id=1, source_target_pairs={{0,16},{16,0},{1,17},{17,1},{2,18},{18,2},{3,19},{19,3},{4,20},{20... | collective-permute-start | bytes 1966088 | tf_op jit(solution)/shard_map/ppermute | solution.py:22
  47.1 11.1 %copy-start.7 = (bf16[256,1280]{1,0:T(8,128)(2,1)}, bf16[256,1280]{1,0:T(8,128)(2,1)S(1)}, u32[]{:S(2)}) copy-start(bf16[256,1280]{1,0:T(8,128)(2,1)S(1)} %attend.3.refs_11_) | copy-start | bytes 1966084
  47.1 23.6 %collective-permute-start.13 = (bf16[256,1280]{1,0:T(8,128)(2,1)S(1)}, bf16[256,1280]{1,0:T(8,128)(2,1)}, u32[]{:S(2)}, u32[]{:S(2)}) collective-permute-start(bf16[256,1280]{1,0:T(8,128)(2,1)S(1)} %attend.3.refs_11_), channel_id=1, source_target_pairs={{0,16},{16,0},{1,17},{17,1},{2,18},{18,2},{3,19},{19,3},{4,20},{20... | collective-permute-start | bytes 1966088 | tf_op jit(solution)/shard_map/ppermute | solution.py:22
  52.0 19.2 %collective-permute-start.4 = (bf16[320,1280]{1,0:T(8,128)(2,1)}, bf16[320,1280]{1,0:T(8,128)(2,1)S(1)}, u32[]{:S(2)}, u32[]{:S(2)}) collective-permute-start(bf16[320,1280]{1,0:T(8,128)(2,1)} %collective-permute-done.2.refs_4_), channel_id=1, source_target_pairs={{0,4},{4,8},{8,12},{12,14},{14,10},{10,6},{6,2},{2,0},{1,5},{5,9},... | collective-permute-start | bytes 2457608 | tf_op jit(solution)/shard_map/ppermute | solution.py:297
  53.1 20.9 %collective-permute-start.5 = (bf16[320,1280]{1,0:T(8,128)(2,1)}, bf16[320,1280]{1,0:T(8,128)(2,1)S(1)}, u32[]{:S(2)}, u32[]{:S(2)}) collective-permute-start(bf16[320,1280]{1,0:T(8,128)(2,1)} %collective-permute-done.3.refs_5_), channel_id=1, source_target_pairs={{4,0},{8,4},{12,8},{14,12},{10,14},{6,10},{2,6},{0,2},{5,1},{9,5},... | collective-permute-start | bytes 2457608 | tf_op jit(solution)/shard_map/ppermute | solution.py:298
  58.1 29.6 %collective-permute-start.14 = (bf16[256,1280]{1,0:T(8,128)(2,1)}, bf16[256,1280]{1,0:T(8,128)(2,1)}, u32[]{:S(2)}, u32[]{:S(2)}) collective-permute-start(bf16[256,1280]{1,0:T(8,128)(2,1)} %collective-permute-done.12.refs_10_), channel_id=1, source_target_pairs={{0,1},{1,0},{2,3},{3,2},{4,5},{5,4},{6,7},{7,6},{8,9},{9,8},{10,11... | collective-permute-start | bytes 1966088 | tf_op jit(solution)/shard_map/ppermute | solution.py:22
  70.7 17.0 %collective-permute-start.15 = (bf16[256,1280]{1,0:T(8,128)(2,1)}, bf16[256,1280]{1,0:T(8,128)(2,1)}, u32[]{:S(2)}, u32[]{:S(2)}) collective-permute-start(bf16[256,1280]{1,0:T(8,128)(2,1)} %collective-permute-done.13.refs_11_), channel_id=1, source_target_pairs={{0,1},{1,0},{2,3},{3,2},{4,5},{5,4},{6,7},{7,6},{8,9},{9,8},{10,11... | collective-permute-start | bytes 1966088 | tf_op jit(solution)/shard_map/ppermute | solution.py:22
  71.2 0.9 copy-start.12
  72.9 14.2 %collective-permute-start.6 = (bf16[160,1280]{1,0:T(8,128)(2,1)}, bf16[160,1280]{1,0:T(8,128)(2,1)}, u32[]{:S(2)}, u32[]{:S(2)}) collective-permute-start(bf16[160,1280]{1,0:T(8,128)(2,1)} %slice.16), channel_id=1, source_target_pairs={{0,4},{4,8},{8,12},{12,14},{14,10},{10,6},{6,2},{2,0},{1,5},{5,9},... | collective-permute-start | bytes 1228808 | tf_op jit(solution)/shard_map/ppermute | solution.py:308
  74.0 0.9 copy-start.13
  75.7 11.9 %collective-permute-start.7 = (bf16[160,1280]{1,0:T(8,128)(2,1)}, bf16[160,1280]{1,0:T(8,128)(2,1)}, u32[]{:S(2)}, u32[]{:S(2)}) collective-permute-start(bf16[160,1280]{1,0:T(8,128)(2,1)} %slice.17), channel_id=1, source_target_pairs={{4,0},{8,4},{12,8},{14,12},{10,14},{6,10},{2,6},{0,2},{5,1},{9,5},... | collective-permute-start | bytes 1228808 | tf_op jit(solution)/shard_map/ppermute | solution.py:309
  87.1 12.4 %copy-start.8 = (bf16[256,1280]{1,0:T(8,128)(2,1)S(1)}, bf16[256,1280]{1,0:T(8,128)(2,1)}, u32[]{:S(2)}) copy-start(bf16[256,1280]{1,0:T(8,128)(2,1)} %copy-done.7) | copy-start | bytes 1966084
  87.1 12.4 %copy-start.6 = (bf16[256,1280]{1,0:T(8,128)(2,1)S(1)}, bf16[256,1280]{1,0:T(8,128)(2,1)}, u32[]{:S(2)}) copy-start(bf16[256,1280]{1,0:T(8,128)(2,1)} %copy-done.5) | copy-start | bytes 1966084
  97.6 30.4 %collective-permute-start.16 = (bf16[512,1280]{1,0:T(8,128)(2,1)}, bf16[512,1280]{1,0:T(8,128)(2,1)S(1)}, u32[]{:S(2)}, u32[]{:S(2)}) collective-permute-start(bf16[512,1280]{1,0:T(8,128)(2,1)} %project.3), channel_id=1, source_target_pairs={{0,16},{16,0},{1,17},{17,1},{2,18},{18,2},{3,19},{19,3},{4,20},{20... | collective-permute-start | bytes 3932168 | tf_op jit(solution)/shard_map/ppermute | solution.py:22
  99.5 2.1 %collective-permute-start.10 = (bf16[256,1280]{1,0:T(8,128)(2,1)S(1)}, bf16[256,1280]{1,0:T(8,128)(2,1)S(1)}, u32[]{:S(2)}, u32[]{:S(2)}) collective-permute-start(bf16[256,1280]{1,0:T(8,128)(2,1)S(1)} %copy-done.8), channel_id=1, source_target_pairs={{0,1},{1,0},{2,3},{3,2},{4,5},{5,4},{6,7},{7,6},{8,9},{9,8},{10,11... | collective-permute-start | bytes 1966088 | tf_op jit(solution)/shard_map/ppermute | solution.py:22
  99.5 3.0 %collective-permute-start.9 = (bf16[256,1280]{1,0:T(8,128)(2,1)S(1)}, bf16[256,1280]{1,0:T(8,128)(2,1)S(1)}, u32[]{:S(2)}, u32[]{:S(2)}) collective-permute-start(bf16[256,1280]{1,0:T(8,128)(2,1)S(1)} %copy-done.6), channel_id=1, source_target_pairs={{0,1},{1,0},{2,3},{3,2},{4,5},{5,4},{6,7},{7,6},{8,9},{9,8},{10,11... | collective-permute-start | bytes 1966088 | tf_op jit(solution)/shard_map/ppermute | solution.py:22
  111.1 0.8 copy-start.9
  111.9 19.6 %copy-start.11 = (f32[5120]{0:T(1024)S(1)}, f32[5120]{0:T(1024)}, u32[]{:S(2)}) copy-start(f32[5120]{0:T(1024)} %param.12) | copy-start | bytes 61444
  111.9 17.2 %collective-permute-start.11 = (bf16[256,1280]{1,0:T(8,128)(2,1)}, bf16[256,1280]{1,0:T(8,128)(2,1)}, u32[]{:S(2)}, u32[]{:S(2)}) collective-permute-start(bf16[256,1280]{1,0:T(8,128)(2,1)} %get-tuple-element.8), channel_id=1, source_target_pairs={{0,1},{1,0},{2,3},{3,2},{4,5},{5,4},{6,7},{7,6},{8,9},{9,8},{10,11... | collective-permute-start | bytes 1966088 | tf_op jit(solution)/shard_map/ppermute | solution.py:22
  129.1 2.4 %collective-permute-start.17 = (bf16[256,1280]{1,0:T(8,128)(2,1)}, bf16[256,1280]{1,0:T(8,128)(2,1)}, u32[]{:S(2)}, u32[]{:S(2)}) collective-permute-start(bf16[256,1280]{1,0:T(8,128)(2,1)} %get-tuple-element.9), channel_id=1, source_target_pairs={{0,1},{1,0},{2,3},{3,2},{4,5},{5,4},{6,7},{7,6},{8,9},{9,8},{10,11... | collective-permute-start | bytes 1966088 | tf_op jit(solution)/shard_map/ppermute | solution.py:22
  131.5 1.7 %copy-start.3 = (bf16[256,5120]{1,0:T(8,128)(2,1)S(1)}, bf16[256,5120]{1,0:T(8,128)(2,1)}, u32[]{:S(2)}) copy-start(bf16[256,5120]{1,0:T(8,128)(2,1)} %input_ref.1) | copy-start | bytes 7864324
  133.3 1.1 copy-start.4
  134.3 1.1 copy-start.10

commit v2 on v0

v2 whole, which is shorter than its diff:
```python
import functools
import math

import jax
import jax.numpy as jnp
from jax import lax
from jax.experimental import pallas as pl
from jax.experimental.pallas import tpu as pltpu
from jax.sharding import PartitionSpec as P

HEAD_DIM = 128
SPLIT = (3, 5)
MASKED = -1e30
ALL_VMEM = 62 << 20
SOME_VMEM = 24 << 20
SMEM = pl.BlockSpec(memory_space=pltpu.SMEM)
VMEM = pl.BlockSpec(memory_space=pltpu.VMEM)
HBM = pl.BlockSpec(memory_space=pltpu.HBM)


def params(limit):
    return pltpu.CompilerParams(vmem_limit_bytes=limit)


def exchanged(block, axis):
    return lax.ppermute(block, axis, [(0, 1), (1, 0)])


def ring_order(count):
    return list(range(0, count, 2)) + list(range(count - 1, 0, -2))


def ring_neighbour(position, shift, count):
    place = jnp.where(position % 2 == 0, position // 2, count - 1 - position // 2)
    place = (place + shift + count) % count
    return jnp.where(place < count // 2, 2 * place, 2 * (count - 1 - place) + 1)


def tile_active(list_ref, count_ref, side, tile):
    found = jnp.int32(0)
    for slot in range(list_ref.shape[2]):
        hit = (list_ref[0, side, slot] == tile) & (slot < count_ref[0, side])
        found = jnp.where(hit, 1, found)
    return found != 0


def attend_kernel(
    first,
    ids_ref,
    list_ref,
    count_ref,
    keys_ref,
    q_ref,
    own_fresh_ref,
    own_cache_ref,
    other_fresh_ref,
    other_cache_ref,
    out_ref,
    queries,
    pairs,
    key_rows,
    value_rows,
    bias,
    sems,
):
    spans, tokens, width = queries.shape
    tiles = list_ref.shape[2]
    rows = tokens // tiles
    own_side = ids_ref[2]
    sides = (own_side, 1 - own_side)
    sources = ((own_fresh_ref, own_cache_ref), (other_fresh_ref, other_cache_ref))

    def columns(span):
        return pl.ds(first + span * width, width)

    def load_queries(span):
        return pltpu.make_async_copy(
            q_ref.at[:, columns(span)], queries.at[span], sems.at[span, 2 * tiles]
        )

    def load_pairs(span, side, tile, source):
        index = side * tiles + tile
        return pltpu.make_async_copy(
            source.at[pl.ds(tile * rows, rows), :, columns(span)],
            pairs.at[span, index],
            sems.at[span, index],
        )

    for span in range(spans):
        load_queries(span).start()
        for side in range(2):
            for tile in range(tiles):
                active = tile_active(list_ref, count_ref, sides[side], tile)
                fresh, cache = sources[side]

                @pl.when(active)
                def _(span=span, side=side, tile=tile, source=fresh):
                    load_pairs(span, side, tile, source).start()

                @pl.when(jnp.logical_not(active))
                def _(span=span, side=side, tile=tile, source=cache):
                    load_pairs(span, side, tile, source).start()

    for query in range(tiles):
        for side in range(2):
            for key in range(tiles):
                allowed = jnp.int32(0)
                for slot in range(keys_ref.shape[2]):
                    hit = keys_ref[0, own_side * tiles + query, slot] == sides[side] * tiles + key
                    allowed = jnp.where(hit, 1, allowed)
                start = (side * tiles + key) * rows
                bias[query * rows : (query + 1) * rows, start : start + rows] = jnp.full(
                    (rows, rows), jnp.where(allowed != 0, 0.0, MASKED), jnp.float32
                )

    to_row = lax.broadcasted_iota(jnp.int32, (2 * rows, 2 * rows), 0)
    from_row = lax.broadcasted_iota(jnp.int32, (2 * rows, 2 * rows), 1)
    wanted = jnp.where(to_row < rows, 2 * to_row, 2 * (to_row - rows) + 1)
    order = (from_row == wanted).astype(jnp.bfloat16)
    scale = math.log2(math.e) / math.sqrt(HEAD_DIM)
    contract_last = (((1,), (1,)), ((), ()))
    for span in range(spans):
        for index in range(2 * tiles):
            load_pairs(span, index // tiles, index % tiles, own_fresh_ref).wait()
            sorted_rows = jnp.dot(
                order,
                pairs[span, index].reshape(2 * rows, width),
                preferred_element_type=jnp.float32,
            ).astype(jnp.bfloat16)
            key_rows[index * rows : (index + 1) * rows] = sorted_rows[:rows]
            value_rows[index * rows : (index + 1) * rows] = sorted_rows[rows:]
        load_queries(span).wait()
        for head in range(width // HEAD_DIM):
            cols = slice(head * HEAD_DIM, (head + 1) * HEAD_DIM)
            scores = lax.dot_general(
                queries[span, :, cols],
                key_rows[:, cols],
                contract_last,
                preferred_element_type=jnp.float32,
            )
            scores = scores * scale + bias[...]
            terms = jnp.exp2(scores - jnp.max(scores, axis=1, keepdims=True))
            total = jnp.sum(terms, axis=1, keepdims=True)
            summed = jnp.dot(
                terms.astype(jnp.bfloat16), value_rows[:, cols], preferred_element_type=jnp.float32
            )
            out_ref[:, span * width + cols.start : span * width + cols.stop] = (
                summed / total
            ).astype(jnp.bfloat16)


def attended_heads(ids, active_list, active_count, key_list, queries, pairs, first, width, spans):
    tokens = queries.shape[0]
    tiles = active_list.shape[2]
    rows = tokens // tiles
    span = width // spans
    return pl.pallas_call(
        functools.partial(attend_kernel, first),
        out_shape=jax.ShapeDtypeStruct((tokens, width), jnp.bfloat16),
        in_specs=[SMEM] * 4 + [HBM] * 5,
        out_specs=VMEM,
        scratch_shapes=[
            pltpu.VMEM((spans, tokens, span), jnp.bfloat16),
            pltpu.VMEM((spans, 2 * tiles, rows, 2, span), jnp.bfloat16),
            pltpu.VMEM((2 * tokens, span), jnp.bfloat16),
            pltpu.VMEM((2 * tokens, span), jnp.bfloat16),
            pltpu.VMEM((tokens, 2 * tokens), jnp.float32),
            pltpu.SemaphoreType.DMA((spans, 2 * tiles + 1)),
        ],
        compiler_params=params(ALL_VMEM),
        cost_estimate=pl.CostEstimate(flops=0, bytes_accessed=0, transcendentals=0),
        name="attend",
    )(ids, active_list, active_count, key_list, queries, *pairs)


def window(place, depth, columns):
    start = place * depth
    first = start // 128 * 128
    return pl.multiple_of(first, 128), pl.multiple_of(start - first, math.gcd(depth, 128))


def most_kernel(shifts, positions, splits, ids_ref, *refs):
    pieces, blocks = len(shifts), 4
    piece_refs, refs = refs[:pieces], refs[pieces:]
    row_refs, refs = refs[: blocks * len(splits)], refs[blocks * len(splits) :]
    sums, cuts, (weight, held, row_sems, sems) = refs[:2], refs[2:4], refs[4:]
    depth = piece_refs[0].shape[0]

    def load_piece(index):
        place = ring_neighbour(ids_ref[1], shifts[index], positions)
        start = pl.multiple_of(place * depth, math.gcd(depth, 64))
        return pltpu.make_async_copy(
            piece_refs[index], weight.at[pl.ds(start, depth)], sems.at[index]
        )

    def load_rows(block):
        copies, start = [], 0
        for index, width in enumerate(splits):
            copies.append(
                pltpu.make_async_copy(
                    row_refs[block * len(splits) + index],
                    held.at[block, :, pl.ds(start, width)],
                    row_sems.at[block, index],
                )
            )
            start += width
        return copies

    for copy in load_rows(0):
        copy.start()
    for index in range(pieces):
        load_piece(index).start()
    for block in range(1, blocks):
        for copy in load_rows(block):
            copy.start()
    missing = ring_neighbour(ids_ref[1], positions // 2, positions)
    start = pl.multiple_of(missing * depth, math.gcd(depth, 64))
    weight[pl.ds(start, depth)] = jnp.zeros((depth, weight.shape[1]), weight.dtype)
    for index in range(pieces):
        load_piece(index).wait()
    first, _ = window(missing, depth, held.shape[2])
    for block in range(blocks):
        for copy in load_rows(block):
            copy.wait()
        rows = held.shape[1]
        span = slice(block % 2 * rows, (block % 2 + 1) * rows)
        sums[block // 2][span] = jnp.dot(
            held[block], weight[...], preferred_element_type=jnp.float32
        )
        cuts[block // 2][span] = held[block, :, pl.ds(first, cuts[0].shape[1])]


def most_projected(ids, positions, pieces, shifts, row_blocks):
    rows, depth, cols = row_blocks[0][0].shape[0], pieces[0].shape[0], pieces[0].shape[1]
    splits = [part.shape[1] for part in row_blocks[0]]
    cut = -(-(depth + 64) // 128) * 128
    pair = jax.ShapeDtypeStruct((2 * rows, cols), jnp.float32)
    left = jax.ShapeDtypeStruct((2 * rows, cut), jnp.bfloat16)
    return pl.pallas_call(
        functools.partial(most_kernel, shifts, positions, splits),
        out_shape=[pair, pair, left, left],
        in_specs=[SMEM] + [HBM] * (len(pieces) + 4 * len(splits)),
        out_specs=[VMEM] * 4,
        scratch_shapes=[
            pltpu.VMEM((positions * depth, cols), jnp.bfloat16),
            pltpu.VMEM((4, rows, positions * depth), jnp.bfloat16),
            pltpu.SemaphoreType.DMA((4, len(splits))),
            pltpu.SemaphoreType.DMA((len(pieces),)),
        ],
        compiler_params=params(SOME_VMEM),
        cost_estimate=pl.CostEstimate(flops=0, bytes_accessed=0, transcendentals=0),
        name="project_most",
    )(ids, *pieces, *[part for block in row_blocks for part in block])


def last_kernel(positions, ids_ref, top_ref, bottom_ref, sums_ref, cut_ref, out_ref, weight):
    half = top_ref.shape[0]
    depth = 2 * half
    missing = ring_neighbour(ids_ref[1], positions // 2, positions)
    _, start = window(missing, depth, positions * depth)
    weight[...] = jnp.zeros(weight.shape, weight.dtype)
    weight[pl.ds(start, half)] = top_ref[...]
    weight[pl.ds(pl.multiple_of(start + half, math.gcd(half, 64)), half)] = bottom_ref[...]
    product = jnp.dot(cut_ref[...], weight[...], preferred_element_type=jnp.float32)
    out_ref[...] = (sums_ref[...] + product).astype(out_ref.dtype)


def last_projected(ids, positions, halves, sums, cut):
    return pl.pallas_call(
        functools.partial(last_kernel, positions),
        out_shape=jax.ShapeDtypeStruct(sums.shape, jnp.bfloat16),
        in_specs=[SMEM, VMEM, VMEM, VMEM, VMEM],
        out_specs=VMEM,
        scratch_shapes=[pltpu.VMEM((cut.shape[1], sums.shape[1]), jnp.bfloat16)],
        compiler_params=params(SOME_VMEM),
        cost_estimate=pl.CostEstimate(flops=0, bytes_accessed=0, transcendentals=0),
        name="project_last",
    )(ids, *halves, sums, cut)


def finish_kernel(
    from_parts, offset, firsts, ids_ref, list_ref, count_ref, gate_ref, input_ref, own_ref, near_ref, *refs
):
    out_ref, inputs, products, outputs, sems = refs[-5:]
    tokens, width = outputs.shape[1:]
    quarter = input_ref.shape[1] // 4
    tiles = list_ref.shape[2]
    rows = tokens // tiles
    part = ids_ref[0] if from_parts == 0 else 1 - ids_ref[0]
    side = ids_ref[2]

    def place(index):
        from_side = side if index == 0 else 1 - side
        start = (part * 2 + from_side) * quarter + offset
        return pl.ds(pl.multiple_of(start, 128), width)

    def loads(index):
        source, first = (own_ref, firsts[0]) if index == 0 else (near_ref, firsts[1])
        return (
            pltpu.make_async_copy(input_ref.at[:, place(index)], inputs.at[index], sems.at[0, index]),
            pltpu.make_async_copy(
                source.at[pl.ds(first, tokens)], products.at[index], sems.at[1, index]
            ),
        )

    def store(index):
        return pltpu.make_async_copy(outputs.at[index], out_ref.at[:, place(index)], sems.at[2, index])

    for index in range(2):
        for copy in loads(index):
            copy.start()
    for index in range(2):
        for copy in loads(index):
            copy.wait()
        gate = gate_ref[:, place(index)]
        for tile in range(tiles):
            span = slice(tile * rows, (tile + 1) * rows)
            active = tile_active(list_ref, count_ref, side, tile)

            @pl.when(active)
            def _(index=index, span=span, gate=gate):
                mixed = inputs[index, span].astype(jnp.float32)
                mixed = mixed + gate * products[index, span].astype(jnp.float32)
                outputs[index, span] = mixed.astype(jnp.bfloat16)

            @pl.when(jnp.logical_not(active))
            def _(index=index, span=span):
                outputs[index, span] = inputs[index, span]

        store(index).start()
    for index in range(2):
        store(index).wait()


def finished(ids, active_list, active_count, gate, block_input, own, near, firsts, from_parts, offset, earlier):
    tokens, total = block_input.shape
    width = own.shape[1]
    args = [ids, active_list, active_count, gate[None], block_input, own, near]
    in_specs = [SMEM, SMEM, SMEM, VMEM, HBM, HBM, HBM]
    aliases = {}
    if earlier is not None:
        aliases = {len(args): 0}
        args.append(earlier)
        in_specs.append(HBM)
    return pl.pallas_call(
        functools.partial(finish_kernel, from_parts, offset, firsts),
        in_specs=in_specs,
        out_specs=HBM,
        out_shape=jax.ShapeDtypeStruct((tokens, total), jnp.bfloat16),
        input_output_aliases=aliases,
        scratch_shapes=[pltpu.VMEM((2, tokens, width), jnp.bfloat16)] * 3
        + [pltpu.SemaphoreType.DMA((3, 2))],
        compiler_params=params(SOME_VMEM),
        cost_estimate=pl.CostEstimate(flops=0, bytes_accessed=0, transcendentals=0),
        name="finish",
    )(*args)


def after(value, *others):
    return lax.optimization_barrier((value, *others))[0]


def all_after(values, *others):
    return list(lax.optimization_barrier((*values, *others))[: len(values)])


def ring_steps(order):
    count = len(order)
    ahead = [(order[index], order[(index + 1) % count]) for index in range(count)]
    behind = [(to, start) for start, to in ahead]

    def step(held):
        return [lax.ppermute(held[0], "fsdp", ahead), lax.ppermute(held[1], "fsdp", behind)]

    def last_step(held):
        half = held[0].shape[0] // 2
        return step([held[0][:half], held[1][half:]])

    return step, last_step


def local(
    block_input, gate, q_fresh, kv_fresh, kv_cache, active_list, active_count, key_list, out_weight
):
    part, position, side = (lax.axis_index(axis) for axis in ("groups", "fsdp", "blk"))
    positions = lax.axis_size("fsdp")
    total = block_input.shape[1]
    heads = q_fresh.shape[1] // HEAD_DIM
    quarter = total // 4
    ids = jnp.stack([part, position, side]).astype(jnp.int32)

    first = quarter // 128 * SPLIT[0] // SPLIT[1] * 128
    widths = (first, quarter - first)
    ringed = positions == 8 and out_weight.shape[0] % 32 == 0
    columns = [
        lax.dynamic_slice_in_dim(out_weight, (part * 2 + side) * quarter + start, width, 1)
        for start, width in ((0, first), (first, quarter - first))
    ]

    pairs = [kv_fresh, kv_cache, exchanged(kv_fresh, "blk"), exchanged(kv_cache, "blk")]
    own_rows, start = [], 0
    for spans in (2, 2):
        width = heads // 4 * spans * HEAD_DIM
        own_rows.append(
            attended_heads(
                ids, active_list, active_count, key_list, q_fresh, pairs, start, width, spans
            )
        )
        start += width
    far_rows = [exchanged(rows, "groups") for rows in own_rows]

    def finish(index, own, near, from_parts, earlier):
        start = (0, first)[index]
        return finished(
            ids, active_list, active_count, gate, block_input, own, near, (0, tokens), from_parts, start, earlier
        )

    tokens = block_input.shape[0]
    if not ringed:
        near_rows = [exchanged(rows, "blk") for rows in own_rows]
        far_near_rows = [exchanged(rows, "blk") for rows in far_rows]
        result = None
        for index, block in enumerate(columns):
            whole = lax.all_gather(block, "fsdp", axis=0, tiled=True)
            for from_parts, row_blocks in enumerate(((own_rows, near_rows), (far_rows, far_near_rows))):
                rows = jnp.concatenate([jnp.concatenate(parts, axis=1) for parts in row_blocks])
                part_rows = jnp.dot(rows, whole, preferred_element_type=jnp.float32)
                part_rows = part_rows.astype(jnp.bfloat16)
                if from_parts == 1:
                    part_rows = exchanged(part_rows, "groups")
                result = finish(index, part_rows, exchanged(part_rows, "blk"), from_parts, result)
        return result

    step, last_step = ring_steps(ring_order(positions))

    def most(pieces):
        blocks = [far_rows, far_near_rows, own_rows, near_rows]
        return most_projected(ids, positions, pieces, (0, -1, 1, -2, 2, -3, 3), blocks)

    first_1, second_1 = step([columns[0]] * 2), step([columns[1]] * 2)
    first_2 = step(all_after(first_1, *second_1, own_rows[0]))
    first_3 = step(all_after(first_2, own_rows[1], far_rows[0]))
    first_4 = last_step(first_3)
    second_2 = step(all_after(second_1, *first_3))
    near_rows = [exchanged(rows, "blk") for rows in own_rows]
    far_near_rows = [exchanged(rows, "blk") for rows in far_rows]
    far_sums, own_sums, far_cut, own_cut = most([columns[0], *first_1, *first_2, *first_3])
    away = last_projected(ids, positions, first_4, far_sums, far_cut)
    back = exchanged(away, "groups")
    kept = last_projected(ids, positions, first_4, own_sums, own_cut)
    second_3 = step(all_after(second_2, away))
    second_4 = last_step(all_after(second_3, kept))
    far_sums, own_sums, far_cut, own_cut = most([columns[1], *second_1, *second_2, *second_3])
    away = last_projected(ids, positions, second_4, after(far_sums, back), far_cut)
    last_back = exchanged(away, "groups")
    result = finish(0, kept, exchanged(kept, "blk"), 0, None)
    kept = last_projected(ids, positions, second_4, own_sums, own_cut)
    result = finish(0, back, exchanged(back, "blk"), 1, result)
    result = finish(1, kept, exchanged(kept, "blk"), 0, result)
    last_back = after(last_back, result)
    return finish(1, last_back, exchanged(last_back, "blk"), 1, result)


def solution(mesh):
    in_specs = (
        P(("groups", "fsdp", "blk"), None),
        P("groups"),
        P(("groups", "fsdp", "blk"), None),
        P(("groups", "fsdp", "blk"), None, None),
        P(("groups", "fsdp", "blk"), None, None),
        P(("groups", "fsdp"), None, None),
        P(("groups", "fsdp"), None),
        P(("groups", "fsdp"), None, None),
        P("fsdp", None),
    )
    out_specs = P(("groups", "fsdp", "blk"), None)
    return jax.shard_map(local, mesh=mesh, in_specs=in_specs, out_specs=out_specs, check_vma=False)
```

time: 246 us -> 114 us (0.46)
  waiting for transfers between devices: 94.8 us -> 40.3 us
  Pallas kernels: 0 us -> 42.6 us
  matrix products: 39.6 us -> 0 us
  local copies, waits for them, and re-layouts: 42.6 us -> 5.35 us
  other arithmetic: 35.8 us -> 0.6 us
  starting transfers between devices: 0.59 us -> 24.7 us
  loops' own time: 17.6 us -> 0 us
  between operations: 13.5 us -> 0.45 us
    all_gather x1 -> x0, waiting for transfers between devices: 91.8 us -> none  [local(): half_weight = lax.all_gather(own_cols, 'fsdp', axis=0, tiled=True)]
    pallas_call x0 -> x12, Pallas kernels: none -> 42.6 us  [the longest x2 16.9 us: attended_heads(): pl.pallas_call(functools.partial(attend_kernel, first), out_shape=jax.Sha...]
    dot_general x10 -> x0, matrix products: 39.6 us -> none  [the longest x4 16.6 us: block_partial(): jnp.einsum('hqk,khd->hqd', weights, value3, preferred_element_type=jnp.fl...]
    ppermute x3 -> x30, waiting for transfers between devices: 2.97 us -> 40.3 us  [the longest x14 24.6 us: exchanged(): return lax.ppermute(block, axis, [(0, 1), (1, 0)])]
    ppermute x3 -> x30, starting transfers between devices: 0.59 us -> 24.7 us  [the longest x8 9.17 us: step(): lax.ppermute(held[1], 'fsdp', behind)]
    another operation x2 -> x0, loops' own time: 17.6 us -> none  [attend_block(): return lax.fori_loop(0, tile_count, one_slot, init_state)]
    unnamed x19 -> x17, local copies, waits for them, and re-layouts: 17.4 us -> 2.47 us
    select_n x8 -> x0, other arithmetic: 14.2 us -> none  [the longest x1 4.99 us: local(): jnp.where(row_flags[:, None], mixed.astype(jnp.bfloat16), block_input)]
  transfers between devices with their start and end apart: 4 -> 30, of which waited for: 2 -> 13; matrix products, arithmetic and copies ran while one was open for 33% -> 4% of each run, Pallas kernels for 0% -> 35%
where the time goes in v2:
time: 114 us
  Pallas kernels  42.6 us (37%)
  waiting for transfers between devices  40.3 us (35%)
  starting transfers between devices  24.7 us (22%)
  local copies, waits for them, and re-layouts  5.35 us (5%)
    ppermute x14, waiting for transfers between devices, exchanged(): return lax.ppermute(block, axis, [(0, 1), (1, 0)])  24.6 us
    pallas_call x2, Pallas kernels, attended_heads(): pl.pallas_call(functools.partial(attend_kernel, first), out_shape=jax.Sha...  16.9 us
    pallas_call x2, Pallas kernels, most_projected(): pl.pallas_call(functools.partial(most_kernel, shifts, positions, splits),...  14.2 us
    ppermute x8, starting transfers between devices, step(): lax.ppermute(held[1], 'fsdp', behind)  9.17 us
    ppermute x8, waiting for transfers between devices, step(): lax.ppermute(held[0], 'fsdp', ahead)  8.48 us
    ppermute x8, starting transfers between devices, step(): lax.ppermute(held[0], 'fsdp', ahead)  8.45 us
    ppermute x8, waiting for transfers between devices, step(): lax.ppermute(held[1], 'fsdp', behind)  7.29 us
    ppermute x14, starting transfers between devices, exchanged(): return lax.ppermute(block, axis, [(0, 1), (1, 0)])  7.1 us
  transfers between devices with their start and end apart: 30, of which 13 were waited for; matrix products, arithmetic and copies ran while one was open for 4% of the time, Pallas kernels for 35%

profile of v2, /device:TPU:0, one launch (start us, length us, event | category | flops | bytes accessed | tf_op | source)
XLA Modules:
  0.0 114.1 jit_solution(7679300868514643655)
XLA Ops:
  0.0 0.5 collective-permute-start.4
  0.5 0.1 collective-permute-start.5
  0.5 1.1 constant_dynamic-slice_fusion.refs_0_
  1.6 3.0 %collective-permute-start.3 = (bf16[320,768]{1,0:T(8,128)(2,1)S(1)}, bf16[320,768]{1,0:T(8,128)(2,1)}, u32[]{:S(2)}, u32[]{:S(2)}) collective-permute-start(bf16[320,768]{1,0:T(8,128)(2,1)S(1)} %constant_dynamic-slice_fusion.refs_0_), channel_id=1, source_target_pairs={{4,0},{8,4},{12,8},{14,12},{10,14},{6,10},{2,6},{0,2},{5,1},{9,5},... | collective-permute-start | bytes 1474568 | tf_op jit(solution)/shard_map/ppermute | solution.py:373
  4.6 0.2 collective-permute-start.2
  4.7 1.8 %constant_dynamic-slice_fusion.1.refs_0_ = bf16[320,512]{1,0:T(8,128)(2,1)} fusion(bf16[320,5120]{1,0:T(8,128)(2,1)} %param.17, s32[]{:T(128)S(6)} %select_n.6), kind=kLoop, calls=%fused_computation.2 | loop fusion | bytes 655364 | tf_op jit(solution)/shard_map/dynamic_slice | solution.py:396
  6.5 1.9 %collective-permute-start.1 = (bf16[320,512]{1,0:T(8,128)(2,1)}, bf16[320,512]{1,0:T(8,128)(2,1)}, u32[]{:S(2)}, u32[]{:S(2)}) collective-permute-start(bf16[320,512]{1,0:T(8,128)(2,1)} %constant_dynamic-slice_fusion.1.refs_0_), channel_id=1, source_target_pairs={{4,0},{8,4},{12,8},{14,12},{10,14},{6,10},{2,6},{0,2},{5,1},{9,5},... | collective-permute-start | bytes 983048 | tf_op jit(solution)/shard_map/ppermute | solution.py:373
  8.4 0.2 collective-permute-start
  8.5 1.4 %copy.13.keys_ref = s32[1,4,3]{2,1,0:T(4,128)} copy(s32[1,4,3]{1,0,2:T(1,128)} %param.16) | data formatting | bytes 96 | tf_op args[7]
  9.9 0.6 pad_add_fusion.ids_ref
  10.5 0.0 collective-permute-done.5.other_cache_ref
  10.5 8.4 %attend.2.refs_11_ = bf16[256,1280]{1,0:T(8,128)(2,1)} custom-call(s32[3]{0:T(128)} %pad_add_fusion.ids_ref, s32[1,2,2]{2,1,0:T(2,128)} %list_ref.11, s32[1,2]{1,0:T(1,128)} %count_ref.11, s32[1,4,3]{2,1,0:T(4,128)} %copy.13.keys_ref, bf16[256,2560]{1,0:T(8,128)(2,1)} %q_ref.3, bf16[256,2,2560]{2,1,0:T(2,128)(2,1)} %own_fresh_ref.3, ...), custom_call_target="tpu_custom_call" | custom-call | tf_op jit(solution)/shard_map/attend/pallas_call | solution.py:157
  18.9 0.0 copy-start.1
  18.9 2.0 %collective-permute-start.8 = (bf16[256,1280]{1,0:T(8,128)(2,1)}, bf16[256,1280]{1,0:T(8,128)(2,1)S(1)}, u32[]{:S(2)}, u32[]{:S(2)}) collective-permute-start(bf16[256,1280]{1,0:T(8,128)(2,1)} %attend.2.refs_11_), channel_id=1, source_target_pairs={{0,16},{16,0},{1,17},{17,1},{2,18},{18,2},{3,19},{19,3},{4,20},{20... | collective-permute-start | bytes 1966088 | tf_op jit(solution)/shard_map/ppermute | solution.py:26
  20.9 2.3 %collective-permute-done.1.refs_2_ = bf16[320,512]{1,0:T(8,128)(2,1)} collective-permute-done((bf16[320,512]{1,0:T(8,128)(2,1)}, bf16[320,512]{1,0:T(8,128)(2,1)}, u32[]{:S(2)}, u32[]{:S(2)}) %collective-permute-start.1) | collective-permute-done | bytes 327712 | tf_op jit(solution)/shard_map/ppermute | solution.py:373
  23.2 1.4 %collective-permute-done.refs_1_ = bf16[320,512]{1,0:T(8,128)(2,1)} collective-permute-done((bf16[320,512]{1,0:T(8,128)(2,1)}, bf16[320,512]{1,0:T(8,128)(2,1)}, u32[]{:S(2)}, u32[]{:S(2)}) %collective-permute-start) | collective-permute-done | bytes 327712 | tf_op jit(solution)/shard_map/ppermute | solution.py:373
  24.6 0.4 collective-permute-start.6
  25.0 1.6 %collective-permute-start.7 = (bf16[320,768]{1,0:T(8,128)(2,1)}, bf16[320,768]{1,0:T(8,128)(2,1)}, u32[]{:S(2)}, u32[]{:S(2)}) collective-permute-start(bf16[320,768]{1,0:T(8,128)(2,1)} %collective-permute-done.3.refs_2_), channel_id=1, source_target_pairs={{4,0},{8,4},{12,8},{14,12},{10,14},{6,10},{2,6},{0,2},{5,1},{9,5},... | collective-permute-start | bytes 1474568 | tf_op jit(solution)/shard_map/ppermute | solution.py:373
  26.6 8.5 %attend.3.refs_12_ = bf16[256,1280]{1,0:T(8,128)(2,1)} custom-call(s32[3]{0:T(128)} %pad_add_fusion.ids_ref, s32[1,2,2]{2,1,0:T(2,128)} %list_ref.11, s32[1,2]{1,0:T(1,128)} %count_ref.11, s32[1,4,3]{2,1,0:T(4,128)} %copy.13.keys_ref, bf16[256,2560]{1,0:T(8,128)(2,1)} %q_ref.3, bf16[256,2,2560]{2,1,0:T(2,128)(2,1)} %own_fresh_ref.3, ...), custom_call_target="tpu_custom_call" | custom-call | tf_op jit(solution)/shard_map/attend/pallas_call | solution.py:157
  35.0 1.6 %collective-permute-start.15 = (bf16[256,1280]{1,0:T(8,128)(2,1)}, bf16[256,1280]{1,0:T(8,128)(2,1)S(1)}, u32[]{:S(2)}, u32[]{:S(2)}) collective-permute-start(bf16[256,1280]{1,0:T(8,128)(2,1)} %attend.3.refs_12_), channel_id=1, source_target_pairs={{0,16},{16,0},{1,17},{17,1},{2,18},{18,2},{3,19},{19,3},{4,20},{20... | collective-permute-start | bytes 1966088 | tf_op jit(solution)/shard_map/ppermute | solution.py:26
  36.6 0.2 collective-permute-done.6.refs_3_
  36.8 0.5 collective-permute-done.7.refs_4_
  37.3 0.0 collective-permute-done.8.refs_7_
  37.3 1.6 %collective-permute-start.9 = (bf16[320,768]{1,0:T(8,128)(2,1)}, bf16[320,768]{1,0:T(8,128)(2,1)S(1)}, u32[]{:S(2)}, u32[]{:S(2)}) collective-permute-start(bf16[320,768]{1,0:T(8,128)(2,1)} %collective-permute-done.6.refs_3_), channel_id=1, source_target_pairs={{0,4},{4,8},{8,12},{12,14},{14,10},{10,6},{6,2},{2,0},{1,5},{5,9},... | collective-permute-start | bytes 1474568 | tf_op jit(solution)/shard_map/ppermute | solution.py:373
  38.9 0.0 collective-permute-start.18
  38.9 0.5 collective-permute-start.10
  39.4 0.2 collective-permute-start.19
  39.6 10.6 %collective-permute-done.15.refs_8_ = bf16[256,1280]{1,0:T(8,128)(2,1)S(1)} collective-permute-done((bf16[256,1280]{1,0:T(8,128)(2,1)}, bf16[256,1280]{1,0:T(8,128)(2,1)S(1)}, u32[]{:S(2)}, u32[]{:S(2)}) %collective-permute-start.15) | collective-permute-done | bytes 655392 | tf_op jit(solution)/shard_map/ppermute | solution.py:26
  50.2 0.5 collective-permute-start.17
  50.8 2.0 %collective-permute-done.10.refs_6_ = bf16[320,768]{1,0:T(8,128)(2,1)S(1)} collective-permute-done((bf16[320,768]{1,0:T(8,128)(2,1)}, bf16[320,768]{1,0:T(8,128)(2,1)S(1)}, u32[]{:S(2)}, u32[]{:S(2)}) %collective-permute-start.10) | collective-permute-done | bytes 491552 | tf_op jit(solution)/shard_map/ppermute | solution.py:373
  52.7 1.6 %collective-permute-start.13 = (bf16[160,768]{1,0:T(8,128)(2,1)S(1)}, bf16[160,768]{1,0:T(8,128)(2,1)S(1)}, u32[]{:S(2)}, u32[]{:S(2)}) collective-permute-start(bf16[160,768]{1,0:T(8,128)(2,1)S(1)} %slice.16), channel_id=1, source_target_pairs={{0,4},{4,8},{8,12},{12,14},{14,10},{10,6},{6,2},{2,0},{1,5},{5,9},... | collective-permute-start | bytes 737288 | tf_op jit(solution)/shard_map/ppermute | solution.py:373
  54.3 0.7 collective-permute-start.14
  55.0 1.1 copy-done.2
  56.1 8.8 %project_most.2 = (f32[512,768]{1,0:T(8,128)S(1)}, f32[512,768]{1,0:T(8,128)S(1)}, bf16[512,384]{1,0:T(8,128)(2,1)S(1)}, bf16[512,384]{1,0:T(8,128)(2,1)S(1)}) custom-call(s32[3]{0:T(128)S(1)} %copy-done.5, bf16[320,768]{1,0:T(8,128)(2,1)S(1)} %constant_dynamic-slice_fusion.refs_0_, bf16[320,768]{1,0:T(8,128)(2,1)} %collective-permute-done.2.refs_1_, ...), custom_call_target="tpu_custom_call" | custom-call | tf_op jit(solution)/shard_map/project_most/pallas_call | solution.py:239
  65.0 1.2 %project_last.4 = bf16[512,768]{1,0:T(8,128)(2,1)S(1)} custom-call(s32[3]{0:T(128)S(1)} %copy-done.5, bf16[160,768]{1,0:T(8,128)(2,1)S(1)} %collective-permute-done.13.top_ref, bf16[160,768]{1,0:T(8,128)(2,1)S(1)} %collective-permute-done.14.bottom_ref, f32[512,768]{1,0:T(8,128)S(1)} %get-tuple-element.31.sums_ref, ...), custom_call_target="tpu_custom_call" | custom-call | tf_op jit(solution)/shard_map/project_last/pallas_call | solution.py:269
  66.2 1.6 %collective-permute-start.24 = (bf16[512,768]{1,0:T(8,128)(2,1)S(1)}, bf16[512,768]{1,0:T(8,128)(2,1)S(1)}, u32[]{:S(2)}, u32[]{:S(2)}) collective-permute-start(bf16[512,768]{1,0:T(8,128)(2,1)S(1)} %project_last.4), channel_id=1, source_target_pairs={{0,16},{16,0},{1,17},{17,1},{2,18},{18,2},{3,19},{19,3},{4,20},{20... | collective-permute-start | bytes 2359304 | tf_op jit(solution)/shard_map/ppermute | solution.py:26
  67.8 1.6 %collective-permute-start.11 = (bf16[320,512]{1,0:T(8,128)(2,1)}, bf16[320,512]{1,0:T(8,128)(2,1)S(1)}, u32[]{:S(2)}, u32[]{:S(2)}) collective-permute-start(bf16[320,512]{1,0:T(8,128)(2,1)} %collective-permute-done.refs_1_), channel_id=1, source_target_pairs={{0,4},{4,8},{8,12},{12,14},{14,10},{10,6},{6,2},{2,0},{1,5},{5,9},... | collective-permute-start | bytes 983048 | tf_op jit(solution)/shard_map/ppermute | solution.py:373
  69.3 0.4 collective-permute-start.12
  69.8 6.7 %collective-permute-done.11.refs_3_ = bf16[320,512]{1,0:T(8,128)(2,1)S(1)} collective-permute-done((bf16[320,512]{1,0:T(8,128)(2,1)}, bf16[320,512]{1,0:T(8,128)(2,1)S(1)}, u32[]{:S(2)}, u32[]{:S(2)}) %collective-permute-start.11) | collective-permute-done | bytes 327712 | tf_op jit(solution)/shard_map/ppermute | solution.py:373
  76.5 1.3 %collective-permute-done.12.refs_4_ = bf16[320,512]{1,0:T(8,128)(2,1)S(1)} collective-permute-done((bf16[320,512]{1,0:T(8,128)(2,1)}, bf16[320,512]{1,0:T(8,128)(2,1)S(1)}, u32[]{:S(2)}, u32[]{:S(2)}) %collective-permute-start.12) | collective-permute-done | bytes 327712 | tf_op jit(solution)/shard_map/ppermute | solution.py:373
  77.8 1.5 %collective-permute-start.20 = (bf16[320,512]{1,0:T(8,128)(2,1)S(1)}, bf16[320,512]{1,0:T(8,128)(2,1)S(1)}, u32[]{:S(2)}, u32[]{:S(2)}) collective-permute-start(bf16[320,512]{1,0:T(8,128)(2,1)S(1)} %collective-permute-done.11.refs_3_), channel_id=1, source_target_pairs={{0,4},{4,8},{8,12},{12,14},{14,10},{10,6},{6,2},{2,0},{1,5},{5,9},... | collective-permute-start | bytes 983048 | tf_op jit(solution)/shard_map/ppermute | solution.py:373
  79.3 0.5 collective-permute-start.21
  79.8 1.2 %project_last.5.own_ref = bf16[512,768]{1,0:T(8,128)(2,1)S(1)} custom-call(s32[3]{0:T(128)S(1)} %copy-done.5, bf16[160,768]{1,0:T(8,128)(2,1)S(1)} %collective-permute-done.13.top_ref, bf16[160,768]{1,0:T(8,128)(2,1)S(1)} %collective-permute-done.14.bottom_ref, f32[512,768]{1,0:T(8,128)S(1)} %get-tuple-element.35.sums_ref, ...), custom_call_target="tpu_custom_call" | custom-call | tf_op jit(solution)/shard_map/project_last/pallas_call | solution.py:269
  81.0 0.1 collective-permute-start.28
  81.1 3.8 %collective-permute-done.24.own_ref = bf16[512,768]{1,0:T(8,128)(2,1)S(1)} collective-permute-done((bf16[512,768]{1,0:T(8,128)(2,1)S(1)}, bf16[512,768]{1,0:T(8,128)(2,1)S(1)}, u32[]{:S(2)}, u32[]{:S(2)}) %collective-permute-start.24) | collective-permute-done | bytes 786464 | tf_op jit(solution)/shard_map/ppermute | solution.py:26
  84.8 0.2 collective-permute-done.20.refs_5_
  85.1 1.3 %collective-permute-done.21.refs_6_ = bf16[320,512]{1,0:T(8,128)(2,1)S(1)} collective-permute-done((bf16[320,512]{1,0:T(8,128)(2,1)S(1)}, bf16[320,512]{1,0:T(8,128)(2,1)S(1)}, u32[]{:S(2)}, u32[]{:S(2)}) %collective-permute-start.21) | collective-permute-done | bytes 327712 | tf_op jit(solution)/shard_map/ppermute | solution.py:373
  86.4 0.6 collective-permute-start.23
  87.0 1.5 %collective-permute-start.22 = (bf16[160,512]{1,0:T(8,128)(2,1)S(1)}, bf16[160,512]{1,0:T(8,128)(2,1)S(1)}, u32[]{:S(2)}, u32[]{:S(2)}) collective-permute-start(bf16[160,512]{1,0:T(8,128)(2,1)S(1)} %slice.14), channel_id=1, source_target_pairs={{0,4},{4,8},{8,12},{12,14},{14,10},{10,6},{6,2},{2,0},{1,5},{5,9},... | collective-permute-start | bytes 491528 | tf_op jit(solution)/shard_map/ppermute | solution.py:373
  88.4 5.4 %project_most.3 = (f32[512,512]{1,0:T(8,128)S(1)}, f32[512,512]{1,0:T(8,128)S(1)}, bf16[512,384]{1,0:T(8,128)(2,1)S(1)}, bf16[512,384]{1,0:T(8,128)(2,1)S(1)}) custom-call(s32[3]{0:T(128)S(1)} %copy-done.5, bf16[320,512]{1,0:T(8,128)(2,1)} %constant_dynamic-slice_fusion.1.refs_0_, bf16[320,512]{1,0:T(8,128)(2,1)} %collective-permute-done.refs_1_, ...), custom_call_target="tpu_custom_call" | custom-call | tf_op jit(solution)/shard_map/project_most/pallas_call | solution.py:239
  93.9 0.0 copy-start
  93.9 0.0 copy-start.4
  93.9 0.0 copy-start.6
  93.9 0.0 copy-start.7
  93.9 1.0 project_last.7.own_ref
  95.0 0.1 collective-permute-start.26
  95.0 1.0 project_last.6
  96.1 0.6 collective-permute-start.25
  96.7 2.0 %finish.4.refs_0_ = bf16[256,5120]{1,0:T(8,128)(2,1)} custom-call(s32[3]{0:T(128)S(1)} %copy-done.5, s32[1,2,2]{2,1,0:T(2,128)S(1)} %copy-done.6, s32[1,2]{1,0:T(1,128)S(1)} %copy-done.7, f32[1,5120]{1,0:T(1,128)S(1)} %bitcast.4, bf16[256,5120]{1,0:T(8,128)(2,1)S(1)} %copy-done, bf16[512,768]{1,0:T(8,128)(2,1)S(1)} %project_last.5.own_ref, ...), custom_call_target="tpu_custom_call" | custom-call | tf_op jit(solution)/shard_map/finish/pallas_call | solution.py:345
  98.7 2.0 %finish.5.refs_0_ = bf16[256,5120]{1,0:T(8,128)(2,1)} custom-call(s32[3]{0:T(128)S(1)} %copy-done.5, s32[1,2,2]{2,1,0:T(2,128)S(1)} %copy-done.6, s32[1,2]{1,0:T(1,128)S(1)} %copy-done.7, f32[1,5120]{1,0:T(1,128)S(1)} %bitcast.5, bf16[256,5120]{1,0:T(8,128)(2,1)S(1)} %copy-done, ...), custom_call_target="tpu_custom_call", output_to_operand_aliasing={{}: (7, {})} | custom-call | tf_op jit(solution)/shard_map/finish/pallas_call | solution.py:345
  100.7 1.5 %finish.6.refs_0_ = bf16[256,5120]{1,0:T(8,128)(2,1)} custom-call(s32[3]{0:T(128)S(1)} %copy-done.5, s32[1,2,2]{2,1,0:T(2,128)S(1)} %copy-done.6, s32[1,2]{1,0:T(1,128)S(1)} %copy-done.7, f32[1,5120]{1,0:T(1,128)S(1)} %bitcast.6, bf16[256,5120]{1,0:T(8,128)(2,1)S(1)} %copy-done, ...), custom_call_target="tpu_custom_call", output_to_operand_aliasing={{}: (7, {})} | custom-call | tf_op jit(solution)/shard_map/finish/pallas_call | solution.py:345
  102.3 8.2 %collective-permute-done.25.own_ref = bf16[512,512]{1,0:T(8,128)(2,1)S(1)} collective-permute-done((bf16[512,512]{1,0:T(8,128)(2,1)S(1)}, bf16[512,512]{1,0:T(8,128)(2,1)S(1)}, u32[]{:S(2)}, u32[]{:S(2)}) %collective-permute-start.25) | collective-permute-done | bytes 524320 | tf_op jit(solution)/shard_map/ppermute | solution.py:26
  110.5 1.9 %collective-permute-done.29.near_ref = bf16[512,512]{1,0:T(8,128)(2,1)S(1)} collective-permute-done((bf16[512,512]{1,0:T(8,128)(2,1)S(1)}, bf16[512,512]{1,0:T(8,128)(2,1)S(1)}, u32[]{:S(2)}, u32[]{:S(2)}) %collective-permute-start.29) | collective-permute-done | bytes 524320 | tf_op jit(solution)/shard_map/ppermute | solution.py:26
  112.4 1.5 %finish.7 = bf16[256,5120]{1,0:T(8,128)(2,1)} custom-call(s32[3]{0:T(128)S(1)} %copy-done.5, s32[1,2,2]{2,1,0:T(2,128)S(1)} %copy-done.6, s32[1,2]{1,0:T(1,128)S(1)} %copy-done.7, f32[1,5120]{1,0:T(1,128)S(1)} %bitcast.7, bf16[256,5120]{1,0:T(8,128)(2,1)S(1)} %copy-done, ...), custom_call_target="tpu_custom_call", output_to_operand_aliasing={{}: (7, {})} | custom-call | tf_op jit(solution)/shard_map/finish/pallas_call | solution.py:345
  (32 shorter events, 0.1 us)
Async XLA Ops:
  0.0 8.4 %collective-permute-start.4 = (bf16[256,2,2560]{2,1,0:T(2,128)(2,1)}, bf16[256,2,2560]{2,1,0:T(2,128)(2,1)}, u32[]{:S(2)}, u32[]{:S(2)}) collective-permute-start(bf16[256,2,2560]{2,1,0:T(2,128)(2,1)} %own_fresh_ref.3), channel_id=1, source_target_pairs={{0,1},{1,0},{2,3},{3,2},{4,5},{5,4},{6,7},{7,6},{8,9},{9,8},{10,11... | collective-permute-start | bytes 7864328 | tf_op jit(solution)/shard_map/ppermute | solution.py:26
  0.5 10.0 %collective-permute-start.5 = (bf16[256,2,2560]{2,1,0:T(2,128)(2,1)}, bf16[256,2,2560]{2,1,0:T(2,128)(2,1)}, u32[]{:S(2)}, u32[]{:S(2)}) collective-permute-start(bf16[256,2,2560]{2,1,0:T(2,128)(2,1)} %own_cache_ref.3), channel_id=1, source_target_pairs={{0,1},{1,0},{2,3},{3,2},{4,5},{5,4},{6,7},{7,6},{8,9},{9,8},{10,11... | collective-permute-start | bytes 7864328 | tf_op jit(solution)/shard_map/ppermute | solution.py:26
  1.6 23.0 %collective-permute-start.3 = (bf16[320,768]{1,0:T(8,128)(2,1)S(1)}, bf16[320,768]{1,0:T(8,128)(2,1)}, u32[]{:S(2)}, u32[]{:S(2)}) collective-permute-start(bf16[320,768]{1,0:T(8,128)(2,1)S(1)} %constant_dynamic-slice_fusion.refs_0_), channel_id=1, source_target_pairs={{4,0},{8,4},{12,8},{14,12},{10,14},{6,10},{2,6},{0,2},{5,1},{9,5},... | collective-permute-start | bytes 1474568 | tf_op jit(solution)/shard_map/ppermute | solution.py:373
  4.6 20.0 %collective-permute-start.2 = (bf16[320,768]{1,0:T(8,128)(2,1)S(1)}, bf16[320,768]{1,0:T(8,128)(2,1)}, u32[]{:S(2)}, u32[]{:S(2)}) collective-permute-start(bf16[320,768]{1,0:T(8,128)(2,1)S(1)} %constant_dynamic-slice_fusion.refs_0_), channel_id=1, source_target_pairs={{0,4},{4,8},{8,12},{12,14},{14,10},{10,6},{6,2},{2,0},{1,5},{5,9},... | collective-permute-start | bytes 1474568 | tf_op jit(solution)/shard_map/ppermute | solution.py:373
  6.5 16.7 %collective-permute-start.1 = (bf16[320,512]{1,0:T(8,128)(2,1)}, bf16[320,512]{1,0:T(8,128)(2,1)}, u32[]{:S(2)}, u32[]{:S(2)}) collective-permute-start(bf16[320,512]{1,0:T(8,128)(2,1)} %constant_dynamic-slice_fusion.1.refs_0_), channel_id=1, source_target_pairs={{4,0},{8,4},{12,8},{14,12},{10,14},{6,10},{2,6},{0,2},{5,1},{9,5},... | collective-permute-start | bytes 983048 | tf_op jit(solution)/shard_map/ppermute | solution.py:373
  8.4 16.2 %collective-permute-start = (bf16[320,512]{1,0:T(8,128)(2,1)}, bf16[320,512]{1,0:T(8,128)(2,1)}, u32[]{:S(2)}, u32[]{:S(2)}) collective-permute-start(bf16[320,512]{1,0:T(8,128)(2,1)} %constant_dynamic-slice_fusion.1.refs_0_), channel_id=1, source_target_pairs={{0,4},{4,8},{8,12},{12,14},{14,10},{10,6},{6,2},{2,0},{1,5},{5,9},... | collective-permute-start | bytes 983048 | tf_op jit(solution)/shard_map/ppermute | solution.py:373
  18.9 20.0 %copy-start.1 = (bf16[256,1280]{1,0:T(8,128)(2,1)S(1)}, bf16[256,1280]{1,0:T(8,128)(2,1)}, u32[]{:S(2)}) copy-start(bf16[256,1280]{1,0:T(8,128)(2,1)} %attend.2.refs_11_) | copy-start | bytes 1966084
  18.9 36.1 %copy-start.5 = (s32[3]{0:T(128)S(1)}, s32[3]{0:T(128)}, u32[]{:S(2)}) copy-start(s32[3]{0:T(128)} %pad_add_fusion.ids_ref) | copy-start | bytes 40
  18.9 18.4 %collective-permute-start.8 = (bf16[256,1280]{1,0:T(8,128)(2,1)}, bf16[256,1280]{1,0:T(8,128)(2,1)S(1)}, u32[]{:S(2)}, u32[]{:S(2)}) collective-permute-start(bf16[256,1280]{1,0:T(8,128)(2,1)} %attend.2.refs_11_), channel_id=1, source_target_pairs={{0,16},{16,0},{1,17},{17,1},{2,18},{18,2},{3,19},{19,3},{4,20},{20... | collective-permute-start | bytes 1966088 | tf_op jit(solution)/shard_map/ppermute | solution.py:26
  24.6 12.3 %collective-permute-start.6 = (bf16[320,768]{1,0:T(8,128)(2,1)}, bf16[320,768]{1,0:T(8,128)(2,1)}, u32[]{:S(2)}, u32[]{:S(2)}) collective-permute-start(bf16[320,768]{1,0:T(8,128)(2,1)} %collective-permute-done.2.refs_1_), channel_id=1, source_target_pairs={{0,4},{4,8},{8,12},{12,14},{14,10},{10,6},{6,2},{2,0},{1,5},{5,9},... | collective-permute-start | bytes 1474568 | tf_op jit(solution)/shard_map/ppermute | solution.py:373
  25.0 12.3 %collective-permute-start.7 = (bf16[320,768]{1,0:T(8,128)(2,1)}, bf16[320,768]{1,0:T(8,128)(2,1)}, u32[]{:S(2)}, u32[]{:S(2)}) collective-permute-start(bf16[320,768]{1,0:T(8,128)(2,1)} %collective-permute-done.3.refs_2_), channel_id=1, source_target_pairs={{4,0},{8,4},{12,8},{14,12},{10,14},{6,10},{2,6},{0,2},{5,1},{9,5},... | collective-permute-start | bytes 1474568 | tf_op jit(solution)/shard_map/ppermute | solution.py:373
  35.0 15.2 %collective-permute-start.15 = (bf16[256,1280]{1,0:T(8,128)(2,1)}, bf16[256,1280]{1,0:T(8,128)(2,1)S(1)}, u32[]{:S(2)}, u32[]{:S(2)}) collective-permute-start(bf16[256,1280]{1,0:T(8,128)(2,1)} %attend.3.refs_12_), channel_id=1, source_target_pairs={{0,16},{16,0},{1,17},{17,1},{2,18},{18,2},{3,19},{19,3},{4,20},{20... | collective-permute-start | bytes 1966088 | tf_op jit(solution)/shard_map/ppermute | solution.py:26
  37.3 12.9 %collective-permute-start.9 = (bf16[320,768]{1,0:T(8,128)(2,1)}, bf16[320,768]{1,0:T(8,128)(2,1)S(1)}, u32[]{:S(2)}, u32[]{:S(2)}) collective-permute-start(bf16[320,768]{1,0:T(8,128)(2,1)} %collective-permute-done.6.refs_3_), channel_id=1, source_target_pairs={{0,4},{4,8},{8,12},{12,14},{14,10},{10,6},{6,2},{2,0},{1,5},{5,9},... | collective-permute-start | bytes 1474568 | tf_op jit(solution)/shard_map/ppermute | solution.py:373
  38.9 15.4 %collective-permute-start.18 = (bf16[256,1280]{1,0:T(8,128)(2,1)S(1)}, bf16[256,1280]{1,0:T(8,128)(2,1)S(1)}, u32[]{:S(2)}, u32[]{:S(2)}) collective-permute-start(bf16[256,1280]{1,0:T(8,128)(2,1)S(1)} %copy-done.1), channel_id=1, source_target_pairs={{0,1},{1,0},{2,3},{3,2},{4,5},{5,4},{6,7},{7,6},{8,9},{9,8},{10,11... | collective-permute-start | bytes 1966088 | tf_op jit(solution)/shard_map/ppermute | solution.py:26
  38.9 13.8 %collective-permute-start.10 = (bf16[320,768]{1,0:T(8,128)(2,1)}, bf16[320,768]{1,0:T(8,128)(2,1)S(1)}, u32[]{:S(2)}, u32[]{:S(2)}) collective-permute-start(bf16[320,768]{1,0:T(8,128)(2,1)} %collective-permute-done.7.refs_4_), channel_id=1, source_target_pairs={{4,0},{8,4},{12,8},{14,12},{10,14},{6,10},{2,6},{0,2},{5,1},{9,5},... | collective-permute-start | bytes 1474568 | tf_op jit(solution)/shard_map/ppermute | solution.py:373
  39.4 15.7 %collective-permute-start.19 = (bf16[256,1280]{1,0:T(8,128)(2,1)}, bf16[256,1280]{1,0:T(8,128)(2,1)S(1)}, u32[]{:S(2)}, u32[]{:S(2)}) collective-permute-start(bf16[256,1280]{1,0:T(8,128)(2,1)} %attend.3.refs_12_), channel_id=1, source_target_pairs={{0,1},{1,0},{2,3},{3,2},{4,5},{5,4},{6,7},{7,6},{8,9},{9,8},{10,11... | collective-permute-start | bytes 1966088 | tf_op jit(solution)/shard_map/ppermute | solution.py:26
  50.2 4.8 %collective-permute-start.16 = (bf16[256,1280]{1,0:T(8,128)(2,1)S(1)}, bf16[256,1280]{1,0:T(8,128)(2,1)S(1)}, u32[]{:S(2)}, u32[]{:S(2)}) collective-permute-start(bf16[256,1280]{1,0:T(8,128)(2,1)S(1)} %collective-permute-done.8.refs_7_), channel_id=1, source_target_pairs={{0,1},{1,0},{2,3},{3,2},{4,5},{5,4},{6,7},{7,6},{8,9},{9,8},{10,11... | collective-permute-start | bytes 1966088 | tf_op jit(solution)/shard_map/ppermute | solution.py:26
  50.2 4.8 %collective-permute-start.17 = (bf16[256,1280]{1,0:T(8,128)(2,1)S(1)}, bf16[256,1280]{1,0:T(8,128)(2,1)S(1)}, u32[]{:S(2)}, u32[]{:S(2)}) collective-permute-start(bf16[256,1280]{1,0:T(8,128)(2,1)S(1)} %collective-permute-done.15.refs_8_), channel_id=1, source_target_pairs={{0,1},{1,0},{2,3},{3,2},{4,5},{5,4},{6,7},{7,6},{8,9},{9,8},{10,11... | collective-permute-start | bytes 1966088 | tf_op jit(solution)/shard_map/ppermute | solution.py:26
  52.7 12.2 %collective-permute-start.13 = (bf16[160,768]{1,0:T(8,128)(2,1)S(1)}, bf16[160,768]{1,0:T(8,128)(2,1)S(1)}, u32[]{:S(2)}, u32[]{:S(2)}) collective-permute-start(bf16[160,768]{1,0:T(8,128)(2,1)S(1)} %slice.16), channel_id=1, source_target_pairs={{0,4},{4,8},{8,12},{12,14},{14,10},{10,6},{6,2},{2,0},{1,5},{5,9},... | collective-permute-start | bytes 737288 | tf_op jit(solution)/shard_map/ppermute | solution.py:373
  54.3 10.6 %collective-permute-start.14 = (bf16[160,768]{1,0:T(8,128)(2,1)S(1)}, bf16[160,768]{1,0:T(8,128)(2,1)S(1)}, u32[]{:S(2)}, u32[]{:S(2)}) collective-permute-start(bf16[160,768]{1,0:T(8,128)(2,1)S(1)} %slice.17), channel_id=1, source_target_pairs={{4,0},{8,4},{12,8},{14,12},{10,14},{6,10},{2,6},{0,2},{5,1},{9,5},... | collective-permute-start | bytes 737288 | tf_op jit(solution)/shard_map/ppermute | solution.py:373
  55.0 1.1 copy-start.2
  66.2 22.3 %copy-start.3 = (bf16[256,1280]{1,0:T(8,128)(2,1)S(1)}, bf16[256,1280]{1,0:T(8,128)(2,1)}, u32[]{:S(2)}) copy-start(bf16[256,1280]{1,0:T(8,128)(2,1)} %attend.3.refs_12_) | copy-start | bytes 1966084
  66.2 18.7 %collective-permute-start.24 = (bf16[512,768]{1,0:T(8,128)(2,1)S(1)}, bf16[512,768]{1,0:T(8,128)(2,1)S(1)}, u32[]{:S(2)}, u32[]{:S(2)}) collective-permute-start(bf16[512,768]{1,0:T(8,128)(2,1)S(1)} %project_last.4), channel_id=1, source_target_pairs={{0,16},{16,0},{1,17},{17,1},{2,18},{18,2},{3,19},{19,3},{4,20},{20... | collective-permute-start | bytes 2359304 | tf_op jit(solution)/shard_map/ppermute | solution.py:26
  67.8 8.7 %collective-permute-start.11 = (bf16[320,512]{1,0:T(8,128)(2,1)}, bf16[320,512]{1,0:T(8,128)(2,1)S(1)}, u32[]{:S(2)}, u32[]{:S(2)}) collective-permute-start(bf16[320,512]{1,0:T(8,128)(2,1)} %collective-permute-done.refs_1_), channel_id=1, source_target_pairs={{0,4},{4,8},{8,12},{12,14},{14,10},{10,6},{6,2},{2,0},{1,5},{5,9},... | collective-permute-start | bytes 983048 | tf_op jit(solution)/shard_map/ppermute | solution.py:373
  69.3 8.4 %collective-permute-start.12 = (bf16[320,512]{1,0:T(8,128)(2,1)}, bf16[320,512]{1,0:T(8,128)(2,1)S(1)}, u32[]{:S(2)}, u32[]{:S(2)}) collective-permute-start(bf16[320,512]{1,0:T(8,128)(2,1)} %collective-permute-done.1.refs_2_), channel_id=1, source_target_pairs={{4,0},{8,4},{12,8},{14,12},{10,14},{6,10},{2,6},{0,2},{5,1},{9,5},... | collective-permute-start | bytes 983048 | tf_op jit(solution)/shard_map/ppermute | solution.py:373
  77.8 7.3 %collective-permute-start.20 = (bf16[320,512]{1,0:T(8,128)(2,1)S(1)}, bf16[320,512]{1,0:T(8,128)(2,1)S(1)}, u32[]{:S(2)}, u32[]{:S(2)}) collective-permute-start(bf16[320,512]{1,0:T(8,128)(2,1)S(1)} %collective-permute-done.11.refs_3_), channel_id=1, source_target_pairs={{0,4},{4,8},{8,12},{12,14},{14,10},{10,6},{6,2},{2,0},{1,5},{5,9},... | collective-permute-start | bytes 983048 | tf_op jit(solution)/shard_map/ppermute | solution.py:373
  79.3 7.1 %collective-permute-start.21 = (bf16[320,512]{1,0:T(8,128)(2,1)S(1)}, bf16[320,512]{1,0:T(8,128)(2,1)S(1)}, u32[]{:S(2)}, u32[]{:S(2)}) collective-permute-start(bf16[320,512]{1,0:T(8,128)(2,1)S(1)} %collective-permute-done.12.refs_4_), channel_id=1, source_target_pairs={{4,0},{8,4},{12,8},{14,12},{10,14},{6,10},{2,6},{0,2},{5,1},{9,5},... | collective-permute-start | bytes 983048 | tf_op jit(solution)/shard_map/ppermute | solution.py:373
  81.0 15.7 %collective-permute-start.28 = (bf16[512,768]{1,0:T(8,128)(2,1)S(1)}, bf16[512,768]{1,0:T(8,128)(2,1)S(1)}, u32[]{:S(2)}, u32[]{:S(2)}) collective-permute-start(bf16[512,768]{1,0:T(8,128)(2,1)S(1)} %project_last.5.own_ref), channel_id=1, source_target_pairs={{0,1},{1,0},{2,3},{3,2},{4,5},{5,4},{6,7},{7,6},{8,9},{9,8},{10,11... | collective-permute-start | bytes 2359304 | tf_op jit(solution)/shard_map/ppermute | solution.py:26
  84.8 13.8 %collective-permute-start.27 = (bf16[512,768]{1,0:T(8,128)(2,1)S(1)}, bf16[512,768]{1,0:T(8,128)(2,1)S(1)}, u32[]{:S(2)}, u32[]{:S(2)}) collective-permute-start(bf16[512,768]{1,0:T(8,128)(2,1)S(1)} %collective-permute-done.24.own_ref), channel_id=1, source_target_pairs={{0,1},{1,0},{2,3},{3,2},{4,5},{5,4},{6,7},{7,6},{8,9},{9,8},{10,11... | collective-permute-start | bytes 2359304 | tf_op jit(solution)/shard_map/ppermute | solution.py:26
  86.4 7.6 %collective-permute-start.23 = (bf16[160,512]{1,0:T(8,128)(2,1)S(1)}, bf16[160,512]{1,0:T(8,128)(2,1)S(1)}, u32[]{:S(2)}, u32[]{:S(2)}) collective-permute-start(bf16[160,512]{1,0:T(8,128)(2,1)S(1)} %slice.15), channel_id=1, source_target_pairs={{4,0},{8,4},{12,8},{14,12},{10,14},{6,10},{2,6},{0,2},{5,1},{9,5},... | collective-permute-start | bytes 491528 | tf_op jit(solution)/shard_map/ppermute | solution.py:373
  87.0 7.0 %collective-permute-start.22 = (bf16[160,512]{1,0:T(8,128)(2,1)S(1)}, bf16[160,512]{1,0:T(8,128)(2,1)S(1)}, u32[]{:S(2)}, u32[]{:S(2)}) collective-permute-start(bf16[160,512]{1,0:T(8,128)(2,1)S(1)} %slice.14), channel_id=1, source_target_pairs={{0,4},{4,8},{8,12},{12,14},{14,10},{10,6},{6,2},{2,0},{1,5},{5,9},... | collective-permute-start | bytes 491528 | tf_op jit(solution)/shard_map/ppermute | solution.py:373
  93.9 2.8 %copy-start = (bf16[256,5120]{1,0:T(8,128)(2,1)S(1)}, bf16[256,5120]{1,0:T(8,128)(2,1)}, u32[]{:S(2)}) copy-start(bf16[256,5120]{1,0:T(8,128)(2,1)} %input_ref.7) | copy-start | bytes 7864324
  93.9 2.8 %copy-start.4 = (f32[5120]{0:T(1024)S(1)}, f32[5120]{0:T(1024)}, u32[]{:S(2)}) copy-start(f32[5120]{0:T(1024)} %param.10) | copy-start | bytes 61444
  93.9 2.8 %copy-start.6 = (s32[1,2,2]{2,1,0:T(2,128)S(1)}, s32[1,2,2]{2,1,0:T(2,128)}, u32[]{:S(2)}) copy-start(s32[1,2,2]{2,1,0:T(2,128)} %list_ref.11) | copy-start | bytes 52
  93.9 2.8 %copy-start.7 = (s32[1,2]{1,0:T(1,128)S(1)}, s32[1,2]{1,0:T(1,128)}, u32[]{:S(2)}) copy-start(s32[1,2]{1,0:T(1,128)} %count_ref.11) | copy-start | bytes 28
  95.0 5.7 %collective-permute-start.26 = (bf16[512,512]{1,0:T(8,128)(2,1)S(1)}, bf16[512,512]{1,0:T(8,128)(2,1)S(1)}, u32[]{:S(2)}, u32[]{:S(2)}) collective-permute-start(bf16[512,512]{1,0:T(8,128)(2,1)S(1)} %project_last.7.own_ref), channel_id=1, source_target_pairs={{0,1},{1,0},{2,3},{3,2},{4,5},{5,4},{6,7},{7,6},{8,9},{9,8},{10,11... | collective-permute-start | bytes 1572872 | tf_op jit(solution)/shard_map/ppermute | solution.py:26
  96.1 14.4 %collective-permute-start.25 = (bf16[512,512]{1,0:T(8,128)(2,1)S(1)}, bf16[512,512]{1,0:T(8,128)(2,1)S(1)}, u32[]{:S(2)}, u32[]{:S(2)}) collective-permute-start(bf16[512,512]{1,0:T(8,128)(2,1)S(1)} %project_last.6), channel_id=1, source_target_pairs={{0,16},{16,0},{1,17},{17,1},{2,18},{18,2},{3,19},{19,3},{4,20},{20... | collective-permute-start | bytes 1572872 | tf_op jit(solution)/shard_map/ppermute | solution.py:26
  110.5 1.9 %collective-permute-start.29 = (bf16[512,512]{1,0:T(8,128)(2,1)S(1)}, bf16[512,512]{1,0:T(8,128)(2,1)S(1)}, u32[]{:S(2)}, u32[]{:S(2)}) collective-permute-start(bf16[512,512]{1,0:T(8,128)(2,1)S(1)} %collective-permute-done.25.own_ref), channel_id=1, source_target_pairs={{0,1},{1,0},{2,3},{3,2},{4,5},{5,4},{6,7},{7,6},{8,9},{9,8},{10,11... | collective-permute-start | bytes 1572872 | tf_op jit(solution)/shard_map/ppermute | solution.py:26

commit v3 on v2

v3 whole, which is shorter than its diff:
```python
import functools
import math

import jax
import jax.numpy as jnp
from jax import lax
from jax.experimental import pallas as pl
from jax.experimental.pallas import tpu as pltpu
from jax.sharding import PartitionSpec as P

HEAD_DIM = 128
SPLIT = (7, 10)
MASKED = -1e30
ALL_VMEM = 62 << 20
SOME_VMEM = 24 << 20
SMEM = pl.BlockSpec(memory_space=pltpu.SMEM)
VMEM = pl.BlockSpec(memory_space=pltpu.VMEM)
HBM = pl.BlockSpec(memory_space=pltpu.HBM)


def params(limit):
    return pltpu.CompilerParams(vmem_limit_bytes=limit)


def exchanged(block, axis):
    return lax.ppermute(block, axis, [(0, 1), (1, 0)])


def ring_order(count):
    return list(range(0, count, 2)) + list(range(count - 1, 0, -2))


def ring_neighbour(position, shift, count):
    place = jnp.where(position % 2 == 0, position // 2, count - 1 - position // 2)
    place = (place + shift + count) % count
    return jnp.where(place < count // 2, 2 * place, 2 * (count - 1 - place) + 1)


def tile_active(list_ref, count_ref, side, tile):
    found = jnp.int32(0)
    for slot in range(list_ref.shape[2]):
        hit = (list_ref[0, side, slot] == tile) & (slot < count_ref[0, side])
        found = jnp.where(hit, 1, found)
    return found != 0


def attend_kernel(
    ids_ref,
    list_ref,
    count_ref,
    keys_ref,
    own_q_ref,
    other_q_ref,
    own_fresh_ref,
    own_cache_ref,
    other_fresh_ref,
    other_cache_ref,
    out_ref,
    queries,
    pairs,
    key_rows,
    value_rows,
    bias,
    sems,
):
    spans, _, tokens, width = queries.shape
    tiles = list_ref.shape[2]
    rows = tokens // tiles
    own_side = ids_ref[2]
    sides = (own_side, 1 - own_side)
    first = own_side * (spans * width)

    def columns(span):
        return pl.ds(pl.multiple_of(first + span * width, 128), width)

    def load_queries(span, side):
        source = (own_q_ref, other_q_ref)[side]
        return pltpu.make_async_copy(
            source.at[:, columns(span)], queries.at[span, side], sems.at[span, 2 * tiles + side]
        )

    def load_pairs(span, index, ref):
        return pltpu.make_async_copy(
            ref.at[pl.ds(index % tiles * rows, rows), :, columns(span)],
            pairs.at[span, index],
            sems.at[span, index],
        )

    for span in range(spans):
        for index in range(2 * tiles):
            active = tile_active(list_ref, count_ref, sides[index // tiles], index % tiles)
            fresh, cache = (
                (own_fresh_ref, own_cache_ref) if index < tiles else (other_fresh_ref, other_cache_ref)
            )

            @pl.when(active)
            def _(span=span, index=index, source=fresh):
                load_pairs(span, index, source).start()

            @pl.when(jnp.logical_not(active))
            def _(span=span, index=index, source=cache):
                load_pairs(span, index, source).start()

        for side in range(2):
            load_queries(span, side).start()

    for asking in range(2):
        for query in range(tiles):
            for side in range(2):
                for key in range(tiles):
                    allowed = jnp.int32(0)
                    for slot in range(keys_ref.shape[2]):
                        listed = keys_ref[0, sides[asking] * tiles + query, slot]
                        allowed = jnp.where(listed == sides[side] * tiles + key, 1, allowed)
                    start = (side * tiles + key) * rows
                    bias[asking, query * rows : (query + 1) * rows, start : start + rows] = jnp.full(
                        (rows, rows), jnp.where(allowed != 0, 0.0, MASKED), jnp.float32
                    )

    to_row = lax.broadcasted_iota(jnp.int32, (2 * rows, 2 * rows), 0)
    from_row = lax.broadcasted_iota(jnp.int32, (2 * rows, 2 * rows), 1)
    wanted = jnp.where(to_row < rows, 2 * to_row, 2 * (to_row - rows) + 1)
    order = (from_row == wanted).astype(jnp.bfloat16)
    scale = math.log2(math.e) / math.sqrt(HEAD_DIM)
    contract_last = (((1,), (1,)), ((), ()))
    for span in range(spans):
        for index in range(2 * tiles):
            load_pairs(span, index, own_fresh_ref).wait()
            sorted_rows = jnp.dot(
                order,
                pairs[span, index].reshape(2 * rows, width),
                preferred_element_type=jnp.float32,
            ).astype(jnp.bfloat16)
            key_rows[index * rows : (index + 1) * rows] = sorted_rows[:rows]
            value_rows[index * rows : (index + 1) * rows] = sorted_rows[rows:]
        for asking in range(2):
            load_queries(span, asking).wait()
            for head in range(width // HEAD_DIM):
                cols = slice(head * HEAD_DIM, (head + 1) * HEAD_DIM)
                scores = lax.dot_general(
                    queries[span, asking, :, cols],
                    key_rows[:, cols],
                    contract_last,
                    preferred_element_type=jnp.float32,
                )
                scores = scores * scale + bias[asking]
                terms = jnp.exp2(scores - jnp.max(scores, axis=1, keepdims=True))
                total = jnp.sum(terms, axis=1, keepdims=True)
                summed = jnp.dot(
                    terms.astype(jnp.bfloat16),
                    value_rows[:, cols],
                    preferred_element_type=jnp.float32,
                )
                out_ref[
                    asking * tokens : (asking + 1) * tokens,
                    span * width + cols.start : span * width + cols.stop,
                ] = (summed / total).astype(jnp.bfloat16)


def attended_heads(ids, active_list, active_count, key_list, queries, pairs):
    tokens, width = queries[0].shape[0], queries[0].shape[1] // 2
    tiles = active_list.shape[2]
    rows, spans = tokens // tiles, 2
    span = width // spans
    return pl.pallas_call(
        attend_kernel,
        out_shape=jax.ShapeDtypeStruct((2 * tokens, width), jnp.bfloat16),
        in_specs=[SMEM] * 4 + [HBM] * 6,
        out_specs=VMEM,
        scratch_shapes=[
            pltpu.VMEM((spans, 2, tokens, span), jnp.bfloat16),
            pltpu.VMEM((spans, 2 * tiles, rows, 2, span), jnp.bfloat16),
            pltpu.VMEM((2 * tokens, span), jnp.bfloat16),
            pltpu.VMEM((2 * tokens, span), jnp.bfloat16),
            pltpu.VMEM((2, tokens, 2 * tokens), jnp.float32),
            pltpu.SemaphoreType.DMA((spans, 2 * tiles + 2)),
        ],
        compiler_params=params(ALL_VMEM),
        cost_estimate=pl.CostEstimate(flops=0, bytes_accessed=0, transcendentals=0),
        name="attend",
    )(ids, active_list, active_count, key_list, *queries, *pairs)


def window(place, depth):
    start = place * depth
    first = start // 128 * 128
    return pl.multiple_of(first, 128), pl.multiple_of(start - first, math.gcd(depth, 128))


def most_kernel(shifts, starts, pairs, positions, ids_ref, *refs):
    pieces = len(shifts)
    piece_refs, row_refs, refs = refs[:pieces], refs[pieces:][: 2 * pairs], refs[pieces + 2 * pairs :]
    sums, cuts, (weight, held, row_sems, sems) = refs[:pairs], refs[pairs:][:pairs], refs[2 * pairs :]
    depth = piece_refs[0].shape[0]
    blocks, rows, width = held.shape
    side = ids_ref[2]
    halves = [pl.ds(pl.multiple_of(at * (width // 2), 128), width // 2) for at in (side, 1 - side)]

    def load_piece(index):
        place = ring_neighbour(ids_ref[1], shifts[index], positions)
        start = pl.multiple_of(place * depth, math.gcd(depth, 64))
        return pltpu.make_async_copy(
            piece_refs[index].at[:, pl.ds(starts[index], weight.shape[1])],
            weight.at[pl.ds(start, depth)],
            sems.at[index],
        )

    def load_rows(block):
        refs = row_refs[block // 2 * 2 : block // 2 * 2 + 2]
        places = (block % 2, 1 - block % 2)
        return [
            pltpu.make_async_copy(
                ref.at[pl.ds(place * rows, rows)], held.at[block, :, half], row_sems.at[block, index]
            )
            for index, (ref, place, half) in enumerate(zip(refs, places, halves))
        ]

    for copy in load_rows(0):
        copy.start()
    for index in range(pieces):
        load_piece(index).start()
    for block in range(1, blocks):
        for copy in load_rows(block):
            copy.start()
    missing = ring_neighbour(ids_ref[1], positions // 2, positions)
    start = pl.multiple_of(missing * depth, math.gcd(depth, 64))
    weight[pl.ds(start, depth)] = jnp.zeros((depth, weight.shape[1]), weight.dtype)
    for index in range(pieces):
        load_piece(index).wait()
    first, _ = window(missing, depth)
    for block in range(blocks):
        for copy in load_rows(block):
            copy.wait()
        span = slice(block % 2 * rows, (block % 2 + 1) * rows)
        sums[block // 2][span] = jnp.dot(
            held[block], weight[...], preferred_element_type=jnp.float32
        )
        cuts[block // 2][span] = held[block, :, pl.ds(first, cuts[0].shape[1])]


def most_projected(ids, positions, pieces, shifts, starts, cols, row_halves):
    depth, pairs = pieces[0].shape[0], len(row_halves) // 2
    rows = row_halves[0].shape[0] // 2
    cut = -(-(depth + 64) // 128) * 128
    return pl.pallas_call(
        functools.partial(most_kernel, shifts, starts, pairs, positions),
        out_shape=[jax.ShapeDtypeStruct((2 * rows, cols), jnp.float32)] * pairs
        + [jax.ShapeDtypeStruct((2 * rows, cut), jnp.bfloat16)] * pairs,
        in_specs=[SMEM] + [HBM] * (len(pieces) + 2 * pairs),
        out_specs=[VMEM] * (2 * pairs),
        scratch_shapes=[
            pltpu.VMEM((positions * depth, cols), jnp.bfloat16),
            pltpu.VMEM((2 * pairs, rows, positions * depth), jnp.bfloat16),
            pltpu.SemaphoreType.DMA((2 * pairs, 2)),
            pltpu.SemaphoreType.DMA((len(pieces),)),
        ],
        compiler_params=params(SOME_VMEM),
        cost_estimate=pl.CostEstimate(
            flops=4 * rows * pairs * depth * positions * cols, bytes_accessed=0, transcendentals=0
        ),
        name="project_most",
    )(ids, *pieces, *row_halves)


def last_kernel(positions, ids_ref, top_ref, bottom_ref, sums_ref, cut_ref, out_ref, weight):
    half = top_ref.shape[0]
    depth = 2 * half
    missing = ring_neighbour(ids_ref[1], positions // 2, positions)
    _, start = window(missing, depth)
    weight[...] = jnp.zeros(weight.shape, weight.dtype)
    weight[pl.ds(start, half)] = top_ref[...]
    weight[pl.ds(pl.multiple_of(start + half, math.gcd(half, 64)), half)] = bottom_ref[...]
    product = jnp.dot(cut_ref[...], weight[...], preferred_element_type=jnp.float32)
    out_ref[...] = (sums_ref[...] + product).astype(out_ref.dtype)


def last_projected(ids, positions, halves, sums, cut, flops):
    return pl.pallas_call(
        functools.partial(last_kernel, positions),
        out_shape=jax.ShapeDtypeStruct(sums.shape, jnp.bfloat16),
        in_specs=[SMEM, VMEM, VMEM, VMEM, VMEM],
        out_specs=VMEM,
        scratch_shapes=[pltpu.VMEM((cut.shape[1], sums.shape[1]), jnp.bfloat16)],
        compiler_params=params(SOME_VMEM),
        cost_estimate=pl.CostEstimate(flops=flops, bytes_accessed=0, transcendentals=0),
        name="project_last",
    )(ids, *halves, sums, cut)


def finish_kernel(
    from_parts, offset, firsts, ids_ref, list_ref, count_ref, gate_ref, input_ref, own_ref, near_ref, *refs
):
    out_ref, inputs, products, outputs, sems = refs[-5:]
    tokens, width = outputs.shape[1:]
    quarter = input_ref.shape[1] // 4
    tiles = list_ref.shape[2]
    rows = tokens // tiles
    part = ids_ref[0] if from_parts == 0 else 1 - ids_ref[0]
    side = ids_ref[2]

    def place(index):
        from_side = side if index == 0 else 1 - side
        start = (part * 2 + from_side) * quarter + offset
        return pl.ds(pl.multiple_of(start, 128), width)

    def loads(index):
        source, first = (own_ref, firsts[0]) if index == 0 else (near_ref, firsts[1])
        return (
            pltpu.make_async_copy(input_ref.at[:, place(index)], inputs.at[index], sems.at[0, index]),
            pltpu.make_async_copy(
                source.at[pl.ds(first, tokens)], products.at[index], sems.at[1, index]
            ),
        )

    def store(index):
        return pltpu.make_async_copy(outputs.at[index], out_ref.at[:, place(index)], sems.at[2, index])

    for index in range(2):
        for copy in loads(index):
            copy.start()
    for index in range(2):
        for copy in loads(index):
            copy.wait()
        gate = gate_ref[:, place(index)]
        for tile in range(tiles):
            span = slice(tile * rows, (tile + 1) * rows)
            active = tile_active(list_ref, count_ref, side, tile)

            @pl.when(active)
            def _(index=index, span=span, gate=gate):
                mixed = inputs[index, span].astype(jnp.float32)
                mixed = mixed + gate * products[index, span].astype(jnp.float32)
                outputs[index, span] = mixed.astype(jnp.bfloat16)

            @pl.when(jnp.logical_not(active))
            def _(index=index, span=span):
                outputs[index, span] = inputs[index, span]

        store(index).start()
    for index in range(2):
        store(index).wait()


def finished(ids, active_list, active_count, gate, block_input, own, near, firsts, from_parts, offset, earlier):
    tokens, total = block_input.shape
    width = own.shape[1]
    args = [ids, active_list, active_count, gate[None], block_input, own, near]
    in_specs = [SMEM, SMEM, SMEM, VMEM, HBM, HBM, HBM]
    aliases = {}
    if earlier is not None:
        aliases = {len(args): 0}
        args.append(earlier)
        in_specs.append(HBM)
    return pl.pallas_call(
        functools.partial(finish_kernel, from_parts, offset, firsts),
        in_specs=in_specs,
        out_specs=HBM,
        out_shape=jax.ShapeDtypeStruct((tokens, total), jnp.bfloat16),
        input_output_aliases=aliases,
        scratch_shapes=[pltpu.VMEM((2, tokens, width), jnp.bfloat16)] * 3
        + [pltpu.SemaphoreType.DMA((3, 2))],
        compiler_params=params(SOME_VMEM),
        cost_estimate=pl.CostEstimate(flops=3_000_000_000, bytes_accessed=0, transcendentals=0),
        name="finish",
    )(*args)


def after(value, *others):
    return lax.optimization_barrier((value, *others))[0]


def all_after(values, *others):
    return list(lax.optimization_barrier((*values, *others))[: len(values)])


def ring_steps(order):
    count = len(order)
    ahead = [(order[index], order[(index + 1) % count]) for index in range(count)]
    behind = [(to, start) for start, to in ahead]

    def step(held):
        return [lax.ppermute(held[0], "fsdp", ahead), lax.ppermute(held[1], "fsdp", behind)]

    def last_step(held):
        half = held[0].shape[0] // 2
        return step([held[0][:half], held[1][half:]])

    return step, last_step


def local(
    block_input, gate, q_fresh, kv_fresh, kv_cache, active_list, active_count, key_list, out_weight
):
    part, position, side = (lax.axis_index(axis) for axis in ("groups", "fsdp", "blk"))
    positions = lax.axis_size("fsdp")
    total = block_input.shape[1]
    heads = q_fresh.shape[1] // HEAD_DIM
    quarter = total // 4
    ids = jnp.stack([part, position, side]).astype(jnp.int32)

    first = quarter // 128 * SPLIT[0] // SPLIT[1] * 128
    ringed = positions == 8 and out_weight.shape[0] % 32 == 0
    columns = lax.dynamic_slice_in_dim(out_weight, (part * 2 + side) * quarter, quarter, 1)
    pairs = [kv_fresh, kv_cache, exchanged(kv_fresh, "blk"), exchanged(kv_cache, "blk")]
    queries = [q_fresh, exchanged(q_fresh, "blk")]
    own_rows = attended_heads(ids, active_list, active_count, key_list, queries, pairs)

    def finish(index, own, near, from_parts, earlier):
        start = (0, first)[index]
        return finished(
            ids, active_list, active_count, gate, block_input, own, near, (0, tokens), from_parts, start, earlier
        )

    tokens = block_input.shape[0]
    if not ringed:
        far_rows = exchanged(own_rows, "groups")
        near_rows, far_near_rows = exchanged(own_rows, "blk"), exchanged(far_rows, "blk")
        result = None
        for index, block in enumerate((columns[:, :first], columns[:, first:])):
            whole = lax.all_gather(block, "fsdp", axis=0, tiled=True)
            for from_parts, (mine, theirs) in enumerate(
                ((own_rows, near_rows), (far_rows, far_near_rows))
            ):
                theirs = jnp.concatenate([theirs[tokens:], theirs[:tokens]])
                low, high = jnp.where(side == 0, mine, theirs), jnp.where(side == 0, theirs, mine)
                rows = jnp.concatenate([low, high], axis=1)
                rows = jnp.dot(rows, whole, preferred_element_type=jnp.float32)
                rows = rows.astype(jnp.bfloat16)
                if from_parts == 1:
                    rows = exchanged(rows, "groups")
                result = finish(index, rows, exchanged(rows, "blk"), from_parts, result)
        return result

    step, last_step = ring_steps(ring_order(positions))

    def most(pieces, start, width, *row_halves):
        shifts, starts = (0, -1, 1, -2, 2, -3, 3), (start,) * 3 + (0,) * 4
        return most_projected(ids, positions, pieces, shifts, starts, width, row_halves)

    both_1 = step([columns] * 2)
    first_1 = [block[:, :first] for block in all_after(both_1, own_rows)]
    first_2 = step(first_1)
    first_3 = step(first_2)
    first_4 = last_step(first_3)
    far_rows = exchanged(own_rows, "groups")
    near_rows = exchanged(own_rows, "blk")
    far_near_rows = exchanged(after(far_rows, near_rows, *first_3), "blk")
    second_1 = [block[:, first:] for block in all_after(both_1, far_near_rows)]
    second_2 = step(second_1)
    pieces = [columns, *both_1, *first_2, *first_3]
    far_sums, far_cut = most(pieces, 0, first, far_rows, far_near_rows)
    away = last_projected(ids, positions, first_4, far_sums, far_cut, 0)
    back = exchanged(away, "groups")
    own_sums, own_cut = most(pieces, 0, first, after(own_rows, away), near_rows)
    kept = last_projected(ids, positions, first_4, own_sums, own_cut, 20_000_000_000)
    second_3 = step(all_after(second_2, away))
    second_4 = last_step(all_after(second_3, kept))
    result = finish(0, kept, exchanged(kept, "blk"), 0, None)
    pieces, rest = [columns, *both_1, *second_2, *second_3], quarter - first
    far_sums, own_sums, far_cut, own_cut = most(
        pieces, first, rest, far_rows, far_near_rows, own_rows, near_rows
    )
    away = last_projected(ids, positions, second_4, far_sums, far_cut, 0)
    last_back = exchanged(away, "groups")
    kept = last_projected(ids, positions, second_4, after(own_sums, away), own_cut, 20_000_000_000)
    back = after(back, *second_4)
    result = finish(0, back, exchanged(back, "blk"), 1, result)
    result = finish(1, kept, exchanged(kept, "blk"), 0, result)
    last_back = after(last_back, result)
    return finish(1, last_back, exchanged(last_back, "blk"), 1, result)


def solution(mesh):
    in_specs = (
        P(("groups", "fsdp", "blk"), None),
        P("groups"),
        P(("groups", "fsdp", "blk"), None),
        P(("groups", "fsdp", "blk"), None, None),
        P(("groups", "fsdp", "blk"), None, None),
        P(("groups", "fsdp"), None, None),
        P(("groups", "fsdp"), None),
        P(("groups", "fsdp"), None, None),
        P("fsdp", None),
    )
    out_specs = P(("groups", "fsdp", "blk"), None)
    return jax.shard_map(local, mesh=mesh, in_specs=in_specs, out_specs=out_specs, check_vma=False)
```

time: 114 us -> 107 us (0.939)
  waiting for transfers between devices: 40.3 us -> 37.2 us
  starting transfers between devices: 24.7 us -> 22.2 us
  Pallas kernels: 42.6 us -> 40.9 us
    ppermute x14 -> x12, waiting for transfers between devices: 24.6 us -> 6.31 us  [exchanged(): return lax.ppermute(block, axis, [(0, 1), (1, 0)])]
    ppermute x8 -> x7, waiting for transfers between devices: 7.29 us -> 24.3 us  [step(): lax.ppermute(held[1], 'fsdp', behind)]
    ppermute x8 -> x7, starting transfers between devices: 8.45 us -> 4.75 us  [step(): lax.ppermute(held[0], 'fsdp', ahead)]
    pallas_call x4, Pallas kernels: 31.1 us -> 27.9 us  [the longest x3 16 us: most_projected(): pl.pallas_call(functools.partial(most_kernel, shifts, starts, pairs, posi...]
    slice x0 -> x4, local copies, waits for them, and re-layouts: none -> 2.15 us  [the longest x2 1.15 us: local(): first_1 = [block[:, :first] for block in all_after(both_1, own_rows)]]
    ppermute x8 -> x7, waiting for transfers between devices: 8.48 us -> 6.61 us  [step(): lax.ppermute(held[0], 'fsdp', ahead)]
    dynamic_slice x2 -> x1, local copies, waits for them, and re-layouts: 2.82 us -> 1.2 us  [local(): lax.dynamic_slice_in_dim(out_weight, (part * 2 + side) * quarter, quarter...]
    pallas_call x4, Pallas kernels: 7.06 us -> 8.41 us  [finished(): pl.pallas_call(functools.partial(finish_kernel, from_parts, offset, first...]
  transfers between devices with their start and end apart: 30 -> 26, of which waited for: 13 -> 10; matrix products, arithmetic and copies ran while one was open for 4% -> 5% of each run, Pallas kernels for 35% -> 37%
where the time goes in v3:
time: 107 us; the launch traced here: 106 us
  Pallas kernels  40.9 us (38%)
  waiting for transfers between devices  37.2 us (35%)
  starting transfers between devices  22.2 us (21%)
  local copies, waits for them, and re-layouts  4.97 us (5%)
    ppermute x7, waiting for transfers between devices, step(): lax.ppermute(held[1], 'fsdp', behind)  24.3 us
    pallas_call x3, Pallas kernels, most_projected(): pl.pallas_call(functools.partial(most_kernel, shifts, starts, pairs, posi...  16 us
    pallas_call x1, Pallas kernels, attended_heads(): pl.pallas_call(attend_kernel, out_shape=jax.ShapeDtypeStruct((2 * tokens,...  11.9 us
    ppermute x7, starting transfers between devices, step(): lax.ppermute(held[1], 'fsdp', behind)  10.5 us
    pallas_call x4, Pallas kernels, finished(): pl.pallas_call(functools.partial(finish_kernel, from_parts, offset, first...  8.41 us
    ppermute x12, starting transfers between devices, exchanged(): return lax.ppermute(block, axis, [(0, 1), (1, 0)])  7 us
    ppermute x7, waiting for transfers between devices, step(): lax.ppermute(held[0], 'fsdp', ahead)  6.61 us
    ppermute x12, waiting for transfers between devices, exchanged(): return lax.ppermute(block, axis, [(0, 1), (1, 0)])  6.31 us
  transfers between devices with their start and end apart: 26, of which 10 were waited for; matrix products, arithmetic and copies ran while one was open for 5% of the time, Pallas kernels for 37%

profile of v3, /device:TPU:0, one launch (start us, length us, event | category | flops | bytes accessed | tf_op | source)
XLA Modules:
  0.0 106.4 jit_solution(1530539371438008421)
XLA Ops:
  0.0 0.5 collective-permute-start.3
  0.5 0.1 collective-permute-start.4
  0.5 0.5 collective-permute-start.2
  1.0 1.2 %constant_dynamic-slice_fusion.refs_0_ = bf16[320,1280]{1,0:T(8,128)(2,1)S(1)} fusion(bf16[320,5120]{1,0:T(8,128)(2,1)} %param.17, s32[]{:T(128)S(6)} %select_n.3), kind=kLoop, calls=%fused_computation.1 | loop fusion | bytes 1638404 | tf_op jit(solution)/shard_map/dynamic_slice | solution.py:403
  2.2 2.5 %collective-permute-start.1 = (bf16[320,1280]{1,0:T(8,128)(2,1)S(1)}, bf16[320,1280]{1,0:T(8,128)(2,1)S(1)}, u32[]{:S(2)}, u32[]{:S(2)}) collective-permute-start(bf16[320,1280]{1,0:T(8,128)(2,1)S(1)} %constant_dynamic-slice_fusion.refs_0_), channel_id=1, source_target_pairs={{4,0},{8,4},{12,8},{14,12},{10,14},{6,10},{2,6},{0,2},{5,1},{9,5},... | collective-permute-start | bytes 2457608 | tf_op jit(solution)/shard_map/ppermute | solution.py:382
  4.7 0.2 collective-permute-start
  4.9 1.3 %copy.13.keys_ref = s32[1,4,3]{2,1,0:T(4,128)} copy(s32[1,4,3]{1,0,2:T(1,128)} %param.16) | data formatting | bytes 96 | tf_op args[7]
  6.2 0.7 pad_add_fusion.ids_ref
  6.9 4.1 %collective-permute-done.2.other_q_ref = bf16[256,2560]{1,0:T(8,128)(2,1)} collective-permute-done((bf16[256,2560]{1,0:T(8,128)(2,1)}, bf16[256,2560]{1,0:T(8,128)(2,1)}, u32[]{:S(2)}, u32[]{:S(2)}) %collective-permute-start.2) | collective-permute-done | bytes 1310752 | tf_op jit(solution)/shard_map/ppermute | solution.py:26
  11.0 0.0 collective-permute-done.3.other_fresh_ref
  11.0 0.0 collective-permute-done.4.other_cache_ref
  11.0 11.9 %attend.1.refs_7_.refs_9_ = bf16[512,1280]{1,0:T(8,128)(2,1)} custom-call(s32[3]{0:T(128)} %pad_add_fusion.ids_ref, s32[1,2,2]{2,1,0:T(2,128)} %list_ref.9, s32[1,2]{1,0:T(1,128)} %count_ref.9, s32[1,4,3]{2,1,0:T(4,128)} %copy.13.keys_ref, bf16[256,2560]{1,0:T(8,128)(2,1)} %own_q_ref.1, bf16[256,2560]{1,0:T(8,128)(2,1)} %collective-permute-done.2.other_q_ref, ...), custom_call_target="tpu_custom_call" | custom-call | tf_op jit(solution)/shard_map/attend/pallas_call | solution.py:165
  22.9 0.5 collective-permute-start.6
  23.4 2.6 %collective-permute-start.5 = (bf16[512,1280]{1,0:T(8,128)(2,1)}, bf16[512,1280]{1,0:T(8,128)(2,1)S(1)}, u32[]{:S(2)}, u32[]{:S(2)}) collective-permute-start(bf16[512,1280]{1,0:T(8,128)(2,1)} %attend.1.refs_7_.refs_9_), channel_id=1, source_target_pairs={{0,16},{16,0},{1,17},{17,1},{2,18},{18,2},{3,19},{19,3},{4,20},{20... | collective-permute-start | bytes 3932168 | tf_op jit(solution)/shard_map/ppermute | solution.py:26
  26.0 0.0 collective-permute-done.1.refs_2_
  26.0 0.0 collective-permute-done.refs_1_
  26.0 1.6 %collective-permute-start.9 = (bf16[320,896]{1,0:T(8,128)(2,1)S(1)}, bf16[320,896]{1,0:T(8,128)(2,1)S(1)}, u32[]{:S(2)}, u32[]{:S(2)}) collective-permute-start(bf16[320,896]{1,0:T(8,128)(2,1)S(1)} %slice.25), channel_id=1, source_target_pairs={{4,0},{8,4},{12,8},{14,12},{10,14},{6,10},{2,6},{0,2},{5,1},{9,5},... | collective-permute-start | bytes 1720328 | tf_op jit(solution)/shard_map/ppermute | solution.py:382
  27.6 1.1 %slice.24 = bf16[320,896]{1,0:T(8,128)(2,1)S(1)} slice(bf16[320,1280]{1,0:T(8,128)(2,1)} %collective-permute-done.refs_1_), slice={[0:320], [0:896]} | slice | bytes 1146880 | tf_op jit(solution)/shard_map/slice | solution.py:441
  28.7 0.6 collective-permute-start.7
  29.3 11.8 %collective-permute-done.9.refs_4_ = bf16[320,896]{1,0:T(8,128)(2,1)S(1)} collective-permute-done((bf16[320,896]{1,0:T(8,128)(2,1)S(1)}, bf16[320,896]{1,0:T(8,128)(2,1)S(1)}, u32[]{:S(2)}, u32[]{:S(2)}) %collective-permute-start.9) | collective-permute-done | bytes 573472 | tf_op jit(solution)/shard_map/ppermute | solution.py:382
  41.1 1.4 %collective-permute-start.10 = (bf16[320,896]{1,0:T(8,128)(2,1)S(1)}, bf16[320,896]{1,0:T(8,128)(2,1)S(1)}, u32[]{:S(2)}, u32[]{:S(2)}) collective-permute-start(bf16[320,896]{1,0:T(8,128)(2,1)S(1)} %collective-permute-done.9.refs_4_), channel_id=1, source_target_pairs={{4,0},{8,4},{12,8},{14,12},{10,14},{6,10},{2,6},{0,2},{5,1},{9,5},... | collective-permute-start | bytes 1720328 | tf_op jit(solution)/shard_map/ppermute | solution.py:382
  42.6 0.9 collective-permute-done.7.refs_3_
  43.4 0.6 collective-permute-start.8
  44.0 11.3 %collective-permute-done.10.refs_6_ = bf16[320,896]{1,0:T(8,128)(2,1)S(1)} collective-permute-done((bf16[320,896]{1,0:T(8,128)(2,1)S(1)}, bf16[320,896]{1,0:T(8,128)(2,1)S(1)}, u32[]{:S(2)}, u32[]{:S(2)}) %collective-permute-start.10) | collective-permute-done | bytes 573472 | tf_op jit(solution)/shard_map/ppermute | solution.py:382
  55.3 1.9 %collective-permute-done.8.refs_5_ = bf16[320,896]{1,0:T(8,128)(2,1)S(1)} collective-permute-done((bf16[320,896]{1,0:T(8,128)(2,1)S(1)}, bf16[320,896]{1,0:T(8,128)(2,1)S(1)}, u32[]{:S(2)}, u32[]{:S(2)}) %collective-permute-start.8) | collective-permute-done | bytes 573472 | tf_op jit(solution)/shard_map/ppermute | solution.py:382
  57.2 0.0 collective-permute-done.5.refs_7_
  57.2 0.0 collective-permute-start.11
  57.3 1.7 %collective-permute-start.15 = (bf16[160,896]{1,0:T(8,128)(2,1)S(1)}, bf16[160,896]{1,0:T(8,128)(2,1)S(1)}, u32[]{:S(2)}, u32[]{:S(2)}) collective-permute-start(bf16[160,896]{1,0:T(8,128)(2,1)S(1)} %slice.33), channel_id=1, source_target_pairs={{4,0},{8,4},{12,8},{14,12},{10,14},{6,10},{2,6},{0,2},{5,1},{9,5},... | collective-permute-start | bytes 860168 | tf_op jit(solution)/shard_map/ppermute | solution.py:382
  59.0 0.5 collective-permute-start.14
  59.4 0.8 collective-permute-done.11.refs_8_
  60.3 1.0 slice.26
  61.3 1.7 %collective-permute-start.13 = (bf16[320,384]{1,0:T(8,128)(2,1)S(1)}, bf16[320,384]{1,0:T(8,128)(2,1)S(1)}, u32[]{:S(2)}, u32[]{:S(2)}) collective-permute-start(bf16[320,384]{1,0:T(8,128)(2,1)S(1)} %slice.27), channel_id=1, source_target_pairs={{4,0},{8,4},{12,8},{14,12},{10,14},{6,10},{2,6},{0,2},{5,1},{9,5},... | collective-permute-start | bytes 737288 | tf_op jit(solution)/shard_map/ppermute | solution.py:382
  63.0 0.4 collective-permute-start.12
  63.4 5.0 %project_most.3 = (f32[512,896]{1,0:T(8,128)S(1)}, bf16[512,384]{1,0:T(8,128)(2,1)S(1)}) custom-call(s32[3]{0:T(128)S(1)} %copy-done.1, bf16[320,1280]{1,0:T(8,128)(2,1)S(1)} %constant_dynamic-slice_fusion.refs_0_, bf16[320,1280]{1,0:T(8,128)(2,1)} %collective-permute-done.refs_1_, bf16[320,1280]{1,0:T(8,128)(2,1)S(1)} %collective-permute-done.1.refs_2_, ...), custom_call_target="tpu_custom_call" | custom-call | flops 2348810240 | tf_op jit(solution)/shard_map/project_most/pallas_call | solution.py:245
  68.4 0.0 copy-start
  68.4 0.3 collective-permute-done.14.top_ref
  68.7 1.3 %project_last.4 = bf16[512,896]{1,0:T(8,128)(2,1)S(1)} custom-call(s32[3]{0:T(128)S(1)} %copy-done.1, bf16[160,896]{1,0:T(8,128)(2,1)S(1)} %collective-permute-done.14.top_ref, bf16[160,896]{1,0:T(8,128)(2,1)S(1)} %collective-permute-done.15.bottom_ref, f32[512,896]{1,0:T(8,128)S(1)} %get-tuple-element.31.sums_ref, ...), custom_call_target="tpu_custom_call" | custom-call | tf_op jit(solution)/shard_map/project_last/pallas_call | solution.py:278
  70.0 0.3 collective-permute-start.22
  70.3 5.0 %project_most.4 = (f32[512,896]{1,0:T(8,128)S(1)}, bf16[512,384]{1,0:T(8,128)(2,1)S(1)}) custom-call(s32[3]{0:T(128)S(1)} %copy-done.1, bf16[320,1280]{1,0:T(8,128)(2,1)S(1)} %constant_dynamic-slice_fusion.refs_0_, bf16[320,1280]{1,0:T(8,128)(2,1)} %collective-permute-done.refs_1_, bf16[320,1280]{1,0:T(8,128)(2,1)S(1)} %collective-permute-done.1.refs_2_, ...), custom_call_target="tpu_custom_call" | custom-call | flops 2348810240 | tf_op jit(solution)/shard_map/project_most/pallas_call | solution.py:245
  75.3 0.0 collective-permute-done.13.refs_4_
  75.3 1.2 %collective-permute-start.16 = (bf16[320,384]{1,0:T(8,128)(2,1)S(1)}, bf16[320,384]{1,0:T(8,128)(2,1)S(1)}, u32[]{:S(2)}, u32[]{:S(2)}) collective-permute-start(bf16[320,384]{1,0:T(8,128)(2,1)S(1)} %collective-permute-done.12.refs_3_), channel_id=1, source_target_pairs={{0,4},{4,8},{8,12},{12,14},{14,10},{10,6},{6,2},{2,0},{1,5},{5,9},... | collective-permute-start | bytes 737288 | tf_op jit(solution)/shard_map/ppermute | solution.py:382
  76.5 0.9 collective-permute-start.17
  77.4 1.3 %project_last.5.own_ref = bf16[512,896]{1,0:T(8,128)(2,1)S(1)} custom-call(s32[3]{0:T(128)S(1)} %copy-done.1, bf16[160,896]{1,0:T(8,128)(2,1)S(1)} %collective-permute-done.14.top_ref, bf16[160,896]{1,0:T(8,128)(2,1)S(1)} %collective-permute-done.15.bottom_ref, f32[512,896]{1,0:T(8,128)S(1)} %get-tuple-element.36.sums_ref, ...), custom_call_target="tpu_custom_call" | custom-call | flops 20000000000 | tf_op jit(solution)/shard_map/project_last/pallas_call | solution.py:278
  78.7 0.1 collective-permute-start.24
  78.8 3.5 %collective-permute-done.16.refs_5_ = bf16[320,384]{1,0:T(8,128)(2,1)S(1)} collective-permute-done((bf16[320,384]{1,0:T(8,128)(2,1)S(1)}, bf16[320,384]{1,0:T(8,128)(2,1)S(1)}, u32[]{:S(2)}, u32[]{:S(2)}) %collective-permute-start.16) | collective-permute-done | bytes 245792 | tf_op jit(solution)/shard_map/ppermute | solution.py:382
  82.3 1.1 %collective-permute-done.17.refs_6_ = bf16[320,384]{1,0:T(8,128)(2,1)S(1)} collective-permute-done((bf16[320,384]{1,0:T(8,128)(2,1)S(1)}, bf16[320,384]{1,0:T(8,128)(2,1)S(1)}, u32[]{:S(2)}, u32[]{:S(2)}) %collective-permute-start.17) | collective-permute-done | bytes 245792 | tf_op jit(solution)/shard_map/ppermute | solution.py:382
  83.5 0.7 collective-permute-start.19
  84.2 1.4 %collective-permute-start.18 = (bf16[160,384]{1,0:T(8,128)(2,1)S(1)}, bf16[160,384]{1,0:T(8,128)(2,1)S(1)}, u32[]{:S(2)}, u32[]{:S(2)}) collective-permute-start(bf16[160,384]{1,0:T(8,128)(2,1)S(1)} %slice.30), channel_id=1, source_target_pairs={{0,4},{4,8},{8,12},{12,14},{14,10},{10,6},{6,2},{2,0},{1,5},{5,9},... | collective-permute-start | bytes 368648 | tf_op jit(solution)/shard_map/ppermute | solution.py:382
  85.6 6.0 %project_most.5 = (f32[512,384]{1,0:T(8,128)S(1)}, f32[512,384]{1,0:T(8,128)S(1)}, bf16[512,384]{1,0:T(8,128)(2,1)S(1)}, bf16[512,384]{1,0:T(8,128)(2,1)S(1)}) custom-call(s32[3]{0:T(128)S(1)} %copy-done.1, bf16[320,1280]{1,0:T(8,128)(2,1)S(1)} %constant_dynamic-slice_fusion.refs_0_, bf16[320,1280]{1,0:T(8,128)(2,1)} %collective-permute-done.refs_1_, ...), custom_call_target="tpu_custom_call" | custom-call | flops 2013265920 | tf_op jit(solution)/shard_map/project_most/pallas_call | solution.py:245
  91.6 0.0 collective-permute-done.18.top_ref
  91.6 1.0 project_last.6
  92.6 1.1 %collective-permute-start.20 = (bf16[512,384]{1,0:T(8,128)(2,1)S(1)}, bf16[512,384]{1,0:T(8,128)(2,1)S(1)}, u32[]{:S(2)}, u32[]{:S(2)}) collective-permute-start(bf16[512,384]{1,0:T(8,128)(2,1)S(1)} %project_last.6), channel_id=1, source_target_pairs={{0,16},{16,0},{1,17},{17,1},{2,18},{18,2},{3,19},{19,3},{4,20},{20... | collective-permute-start | bytes 1179656 | tf_op jit(solution)/shard_map/ppermute | solution.py:26
  93.8 0.0 copy-start.3
  93.8 0.0 copy-start.4
  93.8 0.0 copy-start.5
  93.8 1.0 project_last.7.own_ref
  94.8 0.5 collective-permute-start.21
  95.3 0.2 copy-done.4
  95.5 2.2 %finish.4.refs_0_ = bf16[256,5120]{1,0:T(8,128)(2,1)} custom-call(s32[3]{0:T(128)S(1)} %copy-done.1, s32[1,2,2]{2,1,0:T(2,128)S(1)} %copy-done.2, s32[1,2]{1,0:T(1,128)S(1)} %copy-done.3, f32[1,5120]{1,0:T(1,128)S(1)} %bitcast.4, bf16[256,5120]{1,0:T(8,128)(2,1)S(1)} %copy-done.4, bf16[512,896]{1,0:T(8,128)(2,1)S(1)} %project_last.5.own_ref, ...), custom_call_target="tpu_custom_call" | custom-call | flops 3000000000 | tf_op jit(solution)/shard_map/finish/pallas_call | solution.py:354
  97.8 2.2 %finish.5.refs_0_ = bf16[256,5120]{1,0:T(8,128)(2,1)} custom-call(s32[3]{0:T(128)S(1)} %copy-done.1, s32[1,2,2]{2,1,0:T(2,128)S(1)} %copy-done.2, s32[1,2]{1,0:T(1,128)S(1)} %copy-done.3, f32[1,5120]{1,0:T(1,128)S(1)} %bitcast.5, bf16[256,5120]{1,0:T(8,128)(2,1)S(1)} %copy-done.4, ...), custom_call_target="tpu_custom_call", output_to_operand_aliasing={{}: (7, {})} | custom-call | flops 3000000000 | tf_op jit(solution)/shard_map/finish/pallas_call | solution.py:354
  100.0 2.0 %finish.6.refs_0_ = bf16[256,5120]{1,0:T(8,128)(2,1)} custom-call(s32[3]{0:T(128)S(1)} %copy-done.1, s32[1,2,2]{2,1,0:T(2,128)S(1)} %copy-done.2, s32[1,2]{1,0:T(1,128)S(1)} %copy-done.3, f32[1,5120]{1,0:T(1,128)S(1)} %bitcast.6, bf16[256,5120]{1,0:T(8,128)(2,1)S(1)} %copy-done.4, ...), custom_call_target="tpu_custom_call", output_to_operand_aliasing={{}: (7, {})} | custom-call | flops 3000000000 | tf_op jit(solution)/shard_map/finish/pallas_call | solution.py:354
  102.0 0.9 collective-permute-start.25
  102.9 1.3 %collective-permute-done.25.near_ref = bf16[512,384]{1,0:T(8,128)(2,1)S(1)} collective-permute-done((bf16[512,384]{1,0:T(8,128)(2,1)S(1)}, bf16[512,384]{1,0:T(8,128)(2,1)S(1)}, u32[]{:S(2)}, u32[]{:S(2)}) %collective-permute-start.25) | collective-permute-done | bytes 393248 | tf_op jit(solution)/shard_map/ppermute | solution.py:26
  104.3 2.0 %finish.7 = bf16[256,5120]{1,0:T(8,128)(2,1)} custom-call(s32[3]{0:T(128)S(1)} %copy-done.1, s32[1,2,2]{2,1,0:T(2,128)S(1)} %copy-done.2, s32[1,2]{1,0:T(1,128)S(1)} %copy-done.3, f32[1,5120]{1,0:T(1,128)S(1)} %bitcast.7, bf16[256,5120]{1,0:T(8,128)(2,1)S(1)} %copy-done.4, ...), custom_call_target="tpu_custom_call", output_to_operand_aliasing={{}: (7, {})} | custom-call | flops 3000000000 | tf_op jit(solution)/shard_map/finish/pallas_call | solution.py:354
  (23 shorter events, 0.2 us)
Async XLA Ops:
  0.0 11.0 %collective-permute-start.3 = (bf16[256,2,2560]{2,1,0:T(2,128)(2,1)}, bf16[256,2,2560]{2,1,0:T(2,128)(2,1)}, u32[]{:S(2)}, u32[]{:S(2)}) collective-permute-start(bf16[256,2,2560]{2,1,0:T(2,128)(2,1)} %own_fresh_ref.1), channel_id=1, source_target_pairs={{0,1},{1,0},{2,3},{3,2},{4,5},{5,4},{6,7},{7,6},{8,9},{9,8},{10,11... | collective-permute-start | bytes 7864328 | tf_op jit(solution)/shard_map/ppermute | solution.py:26
  0.5 10.5 %collective-permute-start.4 = (bf16[256,2,2560]{2,1,0:T(2,128)(2,1)}, bf16[256,2,2560]{2,1,0:T(2,128)(2,1)}, u32[]{:S(2)}, u32[]{:S(2)}) collective-permute-start(bf16[256,2,2560]{2,1,0:T(2,128)(2,1)} %own_cache_ref.1), channel_id=1, source_target_pairs={{0,1},{1,0},{2,3},{3,2},{4,5},{5,4},{6,7},{7,6},{8,9},{9,8},{10,11... | collective-permute-start | bytes 7864328 | tf_op jit(solution)/shard_map/ppermute | solution.py:26
  0.5 10.4 %collective-permute-start.2 = (bf16[256,2560]{1,0:T(8,128)(2,1)}, bf16[256,2560]{1,0:T(8,128)(2,1)}, u32[]{:S(2)}, u32[]{:S(2)}) collective-permute-start(bf16[256,2560]{1,0:T(8,128)(2,1)} %own_q_ref.1), channel_id=1, source_target_pairs={{0,1},{1,0},{2,3},{3,2},{4,5},{5,4},{6,7},{7,6},{8,9},{9,8},{10,11... | collective-permute-start | bytes 3932168 | tf_op jit(solution)/shard_map/ppermute | solution.py:26
  2.2 23.8 %collective-permute-start.1 = (bf16[320,1280]{1,0:T(8,128)(2,1)S(1)}, bf16[320,1280]{1,0:T(8,128)(2,1)S(1)}, u32[]{:S(2)}, u32[]{:S(2)}) collective-permute-start(bf16[320,1280]{1,0:T(8,128)(2,1)S(1)} %constant_dynamic-slice_fusion.refs_0_), channel_id=1, source_target_pairs={{4,0},{8,4},{12,8},{14,12},{10,14},{6,10},{2,6},{0,2},{5,1},{9,5},... | collective-permute-start | bytes 2457608 | tf_op jit(solution)/shard_map/ppermute | solution.py:382
  4.7 21.3 %collective-permute-start = (bf16[320,1280]{1,0:T(8,128)(2,1)S(1)}, bf16[320,1280]{1,0:T(8,128)(2,1)}, u32[]{:S(2)}, u32[]{:S(2)}) collective-permute-start(bf16[320,1280]{1,0:T(8,128)(2,1)S(1)} %constant_dynamic-slice_fusion.refs_0_), channel_id=1, source_target_pairs={{0,4},{4,8},{8,12},{12,14},{14,10},{10,6},{6,2},{2,0},{1,5},{5,9},... | collective-permute-start | bytes 2457608 | tf_op jit(solution)/shard_map/ppermute | solution.py:382
  22.9 40.5 %copy-start.1 = (s32[3]{0:T(128)S(1)}, s32[3]{0:T(128)}, u32[]{:S(2)}) copy-start(s32[3]{0:T(128)} %pad_add_fusion.ids_ref) | copy-start | bytes 40
  22.9 34.3 %collective-permute-start.6 = (bf16[512,1280]{1,0:T(8,128)(2,1)}, bf16[512,1280]{1,0:T(8,128)(2,1)S(1)}, u32[]{:S(2)}, u32[]{:S(2)}) collective-permute-start(bf16[512,1280]{1,0:T(8,128)(2,1)} %attend.1.refs_7_.refs_9_), channel_id=1, source_target_pairs={{0,1},{1,0},{2,3},{3,2},{4,5},{5,4},{6,7},{7,6},{8,9},{9,8},{10,11... | collective-permute-start | bytes 3932168 | tf_op jit(solution)/shard_map/ppermute | solution.py:26
  23.4 33.9 %collective-permute-start.5 = (bf16[512,1280]{1,0:T(8,128)(2,1)}, bf16[512,1280]{1,0:T(8,128)(2,1)S(1)}, u32[]{:S(2)}, u32[]{:S(2)}) collective-permute-start(bf16[512,1280]{1,0:T(8,128)(2,1)} %attend.1.refs_7_.refs_9_), channel_id=1, source_target_pairs={{0,16},{16,0},{1,17},{17,1},{2,18},{18,2},{3,19},{19,3},{4,20},{20... | collective-permute-start | bytes 3932168 | tf_op jit(solution)/shard_map/ppermute | solution.py:26
  26.0 15.1 %collective-permute-start.9 = (bf16[320,896]{1,0:T(8,128)(2,1)S(1)}, bf16[320,896]{1,0:T(8,128)(2,1)S(1)}, u32[]{:S(2)}, u32[]{:S(2)}) collective-permute-start(bf16[320,896]{1,0:T(8,128)(2,1)S(1)} %slice.25), channel_id=1, source_target_pairs={{4,0},{8,4},{12,8},{14,12},{10,14},{6,10},{2,6},{0,2},{5,1},{9,5},... | collective-permute-start | bytes 1720328 | tf_op jit(solution)/shard_map/ppermute | solution.py:382
  28.7 14.7 %collective-permute-start.7 = (bf16[320,896]{1,0:T(8,128)(2,1)S(1)}, bf16[320,896]{1,0:T(8,128)(2,1)S(1)}, u32[]{:S(2)}, u32[]{:S(2)}) collective-permute-start(bf16[320,896]{1,0:T(8,128)(2,1)S(1)} %slice.24), channel_id=1, source_target_pairs={{0,4},{4,8},{8,12},{12,14},{14,10},{10,6},{6,2},{2,0},{1,5},{5,9},... | collective-permute-start | bytes 1720328 | tf_op jit(solution)/shard_map/ppermute | solution.py:382
  41.1 14.2 %collective-permute-start.10 = (bf16[320,896]{1,0:T(8,128)(2,1)S(1)}, bf16[320,896]{1,0:T(8,128)(2,1)S(1)}, u32[]{:S(2)}, u32[]{:S(2)}) collective-permute-start(bf16[320,896]{1,0:T(8,128)(2,1)S(1)} %collective-permute-done.9.refs_4_), channel_id=1, source_target_pairs={{4,0},{8,4},{12,8},{14,12},{10,14},{6,10},{2,6},{0,2},{5,1},{9,5},... | collective-permute-start | bytes 1720328 | tf_op jit(solution)/shard_map/ppermute | solution.py:382
  43.4 13.8 %collective-permute-start.8 = (bf16[320,896]{1,0:T(8,128)(2,1)S(1)}, bf16[320,896]{1,0:T(8,128)(2,1)S(1)}, u32[]{:S(2)}, u32[]{:S(2)}) collective-permute-start(bf16[320,896]{1,0:T(8,128)(2,1)S(1)} %collective-permute-done.7.refs_3_), channel_id=1, source_target_pairs={{0,4},{4,8},{8,12},{12,14},{14,10},{10,6},{6,2},{2,0},{1,5},{5,9},... | collective-permute-start | bytes 1720328 | tf_op jit(solution)/shard_map/ppermute | solution.py:382
  57.2 3.0 %collective-permute-start.11 = (bf16[512,1280]{1,0:T(8,128)(2,1)S(1)}, bf16[512,1280]{1,0:T(8,128)(2,1)S(1)}, u32[]{:S(2)}, u32[]{:S(2)}) collective-permute-start(bf16[512,1280]{1,0:T(8,128)(2,1)S(1)} %collective-permute-done.5.refs_7_), channel_id=1, source_target_pairs={{0,1},{1,0},{2,3},{3,2},{4,5},{5,4},{6,7},{7,6},{8,9},{9,8},{10,11... | collective-permute-start | bytes 3932168 | tf_op jit(solution)/shard_map/ppermute | solution.py:26
  57.3 11.1 %collective-permute-start.15 = (bf16[160,896]{1,0:T(8,128)(2,1)S(1)}, bf16[160,896]{1,0:T(8,128)(2,1)S(1)}, u32[]{:S(2)}, u32[]{:S(2)}) collective-permute-start(bf16[160,896]{1,0:T(8,128)(2,1)S(1)} %slice.33), channel_id=1, source_target_pairs={{4,0},{8,4},{12,8},{14,12},{10,14},{6,10},{2,6},{0,2},{5,1},{9,5},... | collective-permute-start | bytes 860168 | tf_op jit(solution)/shard_map/ppermute | solution.py:382
  59.0 9.7 %collective-permute-start.14 = (bf16[160,896]{1,0:T(8,128)(2,1)S(1)}, bf16[160,896]{1,0:T(8,128)(2,1)S(1)}, u32[]{:S(2)}, u32[]{:S(2)}) collective-permute-start(bf16[160,896]{1,0:T(8,128)(2,1)S(1)} %slice.32), channel_id=1, source_target_pairs={{0,4},{4,8},{8,12},{12,14},{14,10},{10,6},{6,2},{2,0},{1,5},{5,9},... | collective-permute-start | bytes 860168 | tf_op jit(solution)/shard_map/ppermute | solution.py:382
  61.3 14.0 %collective-permute-start.13 = (bf16[320,384]{1,0:T(8,128)(2,1)S(1)}, bf16[320,384]{1,0:T(8,128)(2,1)S(1)}, u32[]{:S(2)}, u32[]{:S(2)}) collective-permute-start(bf16[320,384]{1,0:T(8,128)(2,1)S(1)} %slice.27), channel_id=1, source_target_pairs={{4,0},{8,4},{12,8},{14,12},{10,14},{6,10},{2,6},{0,2},{5,1},{9,5},... | collective-permute-start | bytes 737288 | tf_op jit(solution)/shard_map/ppermute | solution.py:382
  63.0 12.4 %collective-permute-start.12 = (bf16[320,384]{1,0:T(8,128)(2,1)S(1)}, bf16[320,384]{1,0:T(8,128)(2,1)S(1)}, u32[]{:S(2)}, u32[]{:S(2)}) collective-permute-start(bf16[320,384]{1,0:T(8,128)(2,1)S(1)} %slice.26), channel_id=1, source_target_pairs={{0,4},{4,8},{8,12},{12,14},{14,10},{10,6},{6,2},{2,0},{1,5},{5,9},... | collective-permute-start | bytes 737288 | tf_op jit(solution)/shard_map/ppermute | solution.py:382
  68.4 2.0 %copy-start = (bf16[512,1280]{1,0:T(8,128)(2,1)S(1)}, bf16[512,1280]{1,0:T(8,128)(2,1)}, u32[]{:S(2)}) copy-start(bf16[512,1280]{1,0:T(8,128)(2,1)} %attend.1.refs_7_.refs_9_) | copy-start | bytes 3932164
  70.0 23.7 %collective-permute-start.22 = (bf16[512,896]{1,0:T(8,128)(2,1)S(1)}, bf16[512,896]{1,0:T(8,128)(2,1)S(1)}, u32[]{:S(2)}, u32[]{:S(2)}) collective-permute-start(bf16[512,896]{1,0:T(8,128)(2,1)S(1)} %project_last.4), channel_id=1, source_target_pairs={{0,16},{16,0},{1,17},{17,1},{2,18},{18,2},{3,19},{19,3},{4,20},{20... | collective-permute-start | bytes 2752520 | tf_op jit(solution)/shard_map/ppermute | solution.py:26
  75.3 7.0 %collective-permute-start.16 = (bf16[320,384]{1,0:T(8,128)(2,1)S(1)}, bf16[320,384]{1,0:T(8,128)(2,1)S(1)}, u32[]{:S(2)}, u32[]{:S(2)}) collective-permute-start(bf16[320,384]{1,0:T(8,128)(2,1)S(1)} %collective-permute-done.12.refs_3_), channel_id=1, source_target_pairs={{0,4},{4,8},{8,12},{12,14},{14,10},{10,6},{6,2},{2,0},{1,5},{5,9},... | collective-permute-start | bytes 737288 | tf_op jit(solution)/shard_map/ppermute | solution.py:382
  76.5 7.0 %collective-permute-start.17 = (bf16[320,384]{1,0:T(8,128)(2,1)S(1)}, bf16[320,384]{1,0:T(8,128)(2,1)S(1)}, u32[]{:S(2)}, u32[]{:S(2)}) collective-permute-start(bf16[320,384]{1,0:T(8,128)(2,1)S(1)} %collective-permute-done.13.refs_4_), channel_id=1, source_target_pairs={{4,0},{8,4},{12,8},{14,12},{10,14},{6,10},{2,6},{0,2},{5,1},{9,5},... | collective-permute-start | bytes 737288 | tf_op jit(solution)/shard_map/ppermute | solution.py:382
  78.7 16.6 %collective-permute-start.24 = (bf16[512,896]{1,0:T(8,128)(2,1)S(1)}, bf16[512,896]{1,0:T(8,128)(2,1)S(1)}, u32[]{:S(2)}, u32[]{:S(2)}) collective-permute-start(bf16[512,896]{1,0:T(8,128)(2,1)S(1)} %project_last.5.own_ref), channel_id=1, source_target_pairs={{0,1},{1,0},{2,3},{3,2},{4,5},{5,4},{6,7},{7,6},{8,9},{9,8},{10,11... | collective-permute-start | bytes 2752520 | tf_op jit(solution)/shard_map/ppermute | solution.py:26
  83.5 8.1 %collective-permute-start.19 = (bf16[160,384]{1,0:T(8,128)(2,1)S(1)}, bf16[160,384]{1,0:T(8,128)(2,1)S(1)}, u32[]{:S(2)}, u32[]{:S(2)}) collective-permute-start(bf16[160,384]{1,0:T(8,128)(2,1)S(1)} %slice.31), channel_id=1, source_target_pairs={{4,0},{8,4},{12,8},{14,12},{10,14},{6,10},{2,6},{0,2},{5,1},{9,5},... | collective-permute-start | bytes 368648 | tf_op jit(solution)/shard_map/ppermute | solution.py:382
  84.2 7.4 %collective-permute-start.18 = (bf16[160,384]{1,0:T(8,128)(2,1)S(1)}, bf16[160,384]{1,0:T(8,128)(2,1)S(1)}, u32[]{:S(2)}, u32[]{:S(2)}) collective-permute-start(bf16[160,384]{1,0:T(8,128)(2,1)S(1)} %slice.30), channel_id=1, source_target_pairs={{0,4},{4,8},{8,12},{12,14},{14,10},{10,6},{6,2},{2,0},{1,5},{5,9},... | collective-permute-start | bytes 368648 | tf_op jit(solution)/shard_map/ppermute | solution.py:382
  92.6 9.4 %collective-permute-start.20 = (bf16[512,384]{1,0:T(8,128)(2,1)S(1)}, bf16[512,384]{1,0:T(8,128)(2,1)S(1)}, u32[]{:S(2)}, u32[]{:S(2)}) collective-permute-start(bf16[512,384]{1,0:T(8,128)(2,1)S(1)} %project_last.6), channel_id=1, source_target_pairs={{0,16},{16,0},{1,17},{17,1},{2,18},{18,2},{3,19},{19,3},{4,20},{20... | collective-permute-start | bytes 1179656 | tf_op jit(solution)/shard_map/ppermute | solution.py:26
  93.8 4.0 %collective-permute-start.23 = (bf16[512,896]{1,0:T(8,128)(2,1)S(1)}, bf16[512,896]{1,0:T(8,128)(2,1)S(1)}, u32[]{:S(2)}, u32[]{:S(2)}) collective-permute-start(bf16[512,896]{1,0:T(8,128)(2,1)S(1)} %collective-permute-done.22.own_ref), channel_id=1, source_target_pairs={{0,1},{1,0},{2,3},{3,2},{4,5},{5,4},{6,7},{7,6},{8,9},{9,8},{10,11... | collective-permute-start | bytes 2752520 | tf_op jit(solution)/shard_map/ppermute | solution.py:26
  93.8 1.6 %copy-start.2 = (s32[1,2,2]{2,1,0:T(2,128)S(1)}, s32[1,2,2]{2,1,0:T(2,128)}, u32[]{:S(2)}) copy-start(s32[1,2,2]{2,1,0:T(2,128)} %list_ref.9) | copy-start | bytes 52
  93.8 1.6 %copy-start.3 = (s32[1,2]{1,0:T(1,128)S(1)}, s32[1,2]{1,0:T(1,128)}, u32[]{:S(2)}) copy-start(s32[1,2]{1,0:T(1,128)} %count_ref.9) | copy-start | bytes 28
  93.8 1.8 %copy-start.4 = (bf16[256,5120]{1,0:T(8,128)(2,1)S(1)}, bf16[256,5120]{1,0:T(8,128)(2,1)}, u32[]{:S(2)}) copy-start(bf16[256,5120]{1,0:T(8,128)(2,1)} %input_ref.7) | copy-start | bytes 7864324
  93.8 1.7 %copy-start.5 = (f32[5120]{0:T(1024)S(1)}, f32[5120]{0:T(1024)}, u32[]{:S(2)}) copy-start(f32[5120]{0:T(1024)} %param.10) | copy-start | bytes 61444
  94.8 5.2 %collective-permute-start.21 = (bf16[512,384]{1,0:T(8,128)(2,1)S(1)}, bf16[512,384]{1,0:T(8,128)(2,1)S(1)}, u32[]{:S(2)}, u32[]{:S(2)}) collective-permute-start(bf16[512,384]{1,0:T(8,128)(2,1)S(1)} %project_last.7.own_ref), channel_id=1, source_target_pairs={{0,1},{1,0},{2,3},{3,2},{4,5},{5,4},{6,7},{7,6},{8,9},{9,8},{10,11... | collective-permute-start | bytes 1179656 | tf_op jit(solution)/shard_map/ppermute | solution.py:26
  102.0 2.3 %collective-permute-start.25 = (bf16[512,384]{1,0:T(8,128)(2,1)S(1)}, bf16[512,384]{1,0:T(8,128)(2,1)S(1)}, u32[]{:S(2)}, u32[]{:S(2)}) collective-permute-start(bf16[512,384]{1,0:T(8,128)(2,1)S(1)} %collective-permute-done.20.own_ref), channel_id=1, source_target_pairs={{0,1},{1,0},{2,3},{3,2},{4,5},{5,4},{6,7},{7,6},{8,9},{9,8},{10,11... | collective-permute-start | bytes 1179656 | tf_op jit(solution)/shard_map/ppermute | solution.py:26

commit v4 on v3

--- a/solution.py
+++ b/solution.py
@@ -74,9 +74,12 @@
         return pl.ds(pl.multiple_of(first + span * width, 128), width)
 
     def load_queries(span, side):
-        source = (own_q_ref, other_q_ref)[side]
+        if side == 0:
+            source = own_q_ref.at[:, columns(span)]
+        else:
+            source = other_q_ref.at[:, pl.ds(span * width, width)]
         return pltpu.make_async_copy(
-            source.at[:, columns(span)], queries.at[span, side], sems.at[span, 2 * tiles + side]
+            source, queries.at[span, side], sems.at[span, 2 * tiles + side]
         )
 
     def load_pairs(span, index, ref):
@@ -262,7 +265,8 @@
     )(ids, *pieces, *row_halves)
 
 
-def last_kernel(positions, ids_ref, top_ref, bottom_ref, sums_ref, cut_ref, out_ref, weight):
+def last_kernel(positions, ids_ref, top_ref, bottom_ref, sums_ref, cut_ref, *refs):
+    out_refs, weight = refs[:-1], refs[-1]
     half = top_ref.shape[0]
     depth = 2 * half
     missing = ring_neighbour(ids_ref[1], positions // 2, positions)
@@ -270,58 +274,68 @@
     weight[...] = jnp.zeros(weight.shape, weight.dtype)
     weight[pl.ds(start, half)] = top_ref[...]
     weight[pl.ds(pl.multiple_of(start + half, math.gcd(half, 64)), half)] = bottom_ref[...]
-    product = jnp.dot(cut_ref[...], weight[...], preferred_element_type=jnp.float32)
-    out_ref[...] = (sums_ref[...] + product).astype(out_ref.dtype)
-
-
-def last_projected(ids, positions, halves, sums, cut, flops):
-    return pl.pallas_call(
+    rows = out_refs[0].shape[0]
+    for index, out_ref in enumerate(out_refs):
+        span = slice(index * rows, (index + 1) * rows)
+        product = jnp.dot(cut_ref[span], weight[...], preferred_element_type=jnp.float32)
+        out_ref[...] = (sums_ref[span] + product).astype(out_ref.dtype)
+
+
+def last_projected(ids, positions, halves, sums, cut, flops, count=1):
+    result = pl.pallas_call(
         functools.partial(last_kernel, positions),
-        out_shape=jax.ShapeDtypeStruct(sums.shape, jnp.bfloat16),
+        out_shape=[jax.ShapeDtypeStruct((sums.shape[0] // count, sums.shape[1]), jnp.bfloat16)]
+        * count,
         in_specs=[SMEM, VMEM, VMEM, VMEM, VMEM],
-        out_specs=VMEM,
+        out_specs=[VMEM] * count,
         scratch_shapes=[pltpu.VMEM((cut.shape[1], sums.shape[1]), jnp.bfloat16)],
         compiler_params=params(SOME_VMEM),
         cost_estimate=pl.CostEstimate(flops=flops, bytes_accessed=0, transcendentals=0),
         name="project_last",
     )(ids, *halves, sums, cut)
-
-
-def finish_kernel(
-    from_parts, offset, firsts, ids_ref, list_ref, count_ref, gate_ref, input_ref, own_ref, near_ref, *refs
-):
+    return result[0] if count == 1 else result
+
+
+def finish_kernel(offset, places, ids_ref, list_ref, count_ref, gate_ref, input_ref, *refs):
+    sources = refs[: len(places)]
     out_ref, inputs, products, outputs, sems = refs[-5:]
     tokens, width = outputs.shape[1:]
     quarter = input_ref.shape[1] // 4
     tiles = list_ref.shape[2]
     rows = tokens // tiles
-    part = ids_ref[0] if from_parts == 0 else 1 - ids_ref[0]
     side = ids_ref[2]
 
-    def place(index):
-        from_side = side if index == 0 else 1 - side
-        start = (part * 2 + from_side) * quarter + offset
+    def columns(index):
+        far, other, _ = places[index]
+        of_part = 1 - ids_ref[0] if far else ids_ref[0]
+        of_side = 1 - side if other else side
+        start = (of_part * 2 + of_side) * quarter + offset
         return pl.ds(pl.multiple_of(start, 128), width)
 
     def loads(index):
-        source, first = (own_ref, firsts[0]) if index == 0 else (near_ref, firsts[1])
         return (
-            pltpu.make_async_copy(input_ref.at[:, place(index)], inputs.at[index], sems.at[0, index]),
             pltpu.make_async_copy(
-                source.at[pl.ds(first, tokens)], products.at[index], sems.at[1, index]
+                input_ref.at[:, columns(index)], inputs.at[index], sems.at[0, index]
             ),
+            pltpu.make_async_copy(
+                sources[index].at[pl.ds(places[index][2], tokens)],
+                products.at[index],
+                sems.at[1, index],
+            ),
         )
 
     def store(index):
-        return pltpu.make_async_copy(outputs.at[index], out_ref.at[:, place(index)], sems.at[2, index])
-
-    for index in range(2):
+        return pltpu.make_async_copy(
+            outputs.at[index], out_ref.at[:, columns(index)], sems.at[2, index]
+        )
+
+    for index in range(len(places)):
         for copy in loads(index):
             copy.start()
-    for index in range(2):
+    for index in range(len(places)):
         for copy in loads(index):
             copy.wait()
-        gate = gate_ref[:, place(index)]
+        gate = gate_ref[:, columns(index)]
         for tile in range(tiles):
             span = slice(tile * rows, (tile + 1) * rows)
             active = tile_active(list_ref, count_ref, side, tile)
@@ -337,30 +351,32 @@
                 outputs[index, span] = inputs[index, span]
 
         store(index).start()
-    for index in range(2):
+    for index in range(len(places)):
         store(index).wait()
 
 
-def finished(ids, active_list, active_count, gate, block_input, own, near, firsts, from_parts, offset, earlier):
+def finished(ids, active_list, active_count, gate, block_input, sources, places, offset, earlier):
     tokens, total = block_input.shape
-    width = own.shape[1]
-    args = [ids, active_list, active_count, gate[None], block_input, own, near]
-    in_specs = [SMEM, SMEM, SMEM, VMEM, HBM, HBM, HBM]
+    width, count = sources[0].shape[1], len(sources)
+    args = [ids, active_list, active_count, gate[None], block_input, *sources]
+    in_specs = [SMEM, SMEM, SMEM, VMEM, HBM] + [HBM] * count
     aliases = {}
     if earlier is not None:
         aliases = {len(args): 0}
         args.append(earlier)
         in_specs.append(HBM)
     return pl.pallas_call(
-        functools.partial(finish_kernel, from_parts, offset, firsts),
+        functools.partial(finish_kernel, offset, places),
         in_specs=in_specs,
         out_specs=HBM,
         out_shape=jax.ShapeDtypeStruct((tokens, total), jnp.bfloat16),
         input_output_aliases=aliases,
-        scratch_shapes=[pltpu.VMEM((2, tokens, width), jnp.bfloat16)] * 3
-        + [pltpu.SemaphoreType.DMA((3, 2))],
+        scratch_shapes=[pltpu.VMEM((count, tokens, width), jnp.bfloat16)] * 3
+        + [pltpu.SemaphoreType.DMA((3, count))],
         compiler_params=params(SOME_VMEM),
-        cost_estimate=pl.CostEstimate(flops=3_000_000_000, bytes_accessed=0, transcendentals=0),
+        cost_estimate=pl.CostEstimate(
+            flops=1_500_000_000 * count, bytes_accessed=0, transcendentals=0
+        ),
         name="finish",
     )(*args)
 
@@ -402,13 +418,17 @@
     ringed = positions == 8 and out_weight.shape[0] % 32 == 0
     columns = lax.dynamic_slice_in_dim(out_weight, (part * 2 + side) * quarter, quarter, 1)
     pairs = [kv_fresh, kv_cache, exchanged(kv_fresh, "blk"), exchanged(kv_cache, "blk")]
-    queries = [q_fresh, exchanged(q_fresh, "blk")]
+    half = q_fresh.shape[1] // 2
+    queries = [
+        q_fresh,
+        exchanged(lax.dynamic_slice_in_dim(q_fresh, (1 - side) * half, half, 1), "blk"),
+    ]
     own_rows = attended_heads(ids, active_list, active_count, key_list, queries, pairs)
 
-    def finish(index, own, near, from_parts, earlier):
+    def finish(index, sources, places, earlier):
         start = (0, first)[index]
         return finished(
-            ids, active_list, active_count, gate, block_input, own, near, (0, tokens), from_parts, start, earlier
+            ids, active_list, active_count, gate, block_input, sources, places, start, earlier
         )
 
     tokens = block_input.shape[0]
@@ -428,7 +448,9 @@
                 rows = rows.astype(jnp.bfloat16)
                 if from_parts == 1:
                     rows = exchanged(rows, "groups")
-                result = finish(index, rows, exchanged(rows, "blk"), from_parts, result)
+                sources = [rows, exchanged(rows, "blk")]
+                places = ((from_parts, 0, 0), (from_parts, 1, tokens))
+                result = finish(index, sources, places, result)
         return result
 
     step, last_step = ring_steps(ring_order(positions))
@@ -437,6 +459,7 @@
         shifts, starts = (0, -1, 1, -2, 2, -3, 3), (start,) * 3 + (0,) * 4
         return most_projected(ids, positions, pieces, shifts, starts, width, row_halves)
 
+    much = 20_000_000_000
     both_1 = step([columns] * 2)
     first_1 = [block[:, :first] for block in all_after(both_1, own_rows)]
     first_2 = step(first_1)
@@ -445,29 +468,37 @@
     far_rows = exchanged(own_rows, "groups")
     near_rows = exchanged(own_rows, "blk")
     far_near_rows = exchanged(after(far_rows, near_rows, *first_3), "blk")
-    second_1 = [block[:, first:] for block in all_after(both_1, far_near_rows)]
-    second_2 = step(second_1)
+    second_1 = [block[:, first:] for block in both_1]
+    second_2 = step(all_after(second_1, far_rows))
     pieces = [columns, *both_1, *first_2, *first_3]
     far_sums, far_cut = most(pieces, 0, first, far_rows, far_near_rows)
     away = last_projected(ids, positions, first_4, far_sums, far_cut, 0)
     back = exchanged(away, "groups")
-    own_sums, own_cut = most(pieces, 0, first, after(own_rows, away), near_rows)
-    kept = last_projected(ids, positions, first_4, own_sums, own_cut, 20_000_000_000)
+    own_sums, own_cut = most(pieces, 0, first, after(own_rows, away, *second_2), near_rows)
+    kept = last_projected(ids, positions, first_4, own_sums, own_cut, much)
     second_3 = step(all_after(second_2, away))
     second_4 = last_step(all_after(second_3, kept))
-    result = finish(0, kept, exchanged(kept, "blk"), 0, None)
+    kept_near = exchanged(kept, "blk")
     pieces, rest = [columns, *both_1, *second_2, *second_3], quarter - first
-    far_sums, own_sums, far_cut, own_cut = most(
-        pieces, first, rest, far_rows, far_near_rows, own_rows, near_rows
-    )
+    far_sums, far_cut = most(pieces, first, rest, far_rows, far_near_rows)
     away = last_projected(ids, positions, second_4, far_sums, far_cut, 0)
     last_back = exchanged(away, "groups")
-    kept = last_projected(ids, positions, second_4, after(own_sums, away), own_cut, 20_000_000_000)
+    own_sums, own_cut = most(pieces, first, rest, after(own_rows, away), near_rows)
+    rest_kept = last_projected(ids, positions, second_4, own_sums, own_cut, much)
     back = after(back, *second_4)
-    result = finish(0, back, exchanged(back, "blk"), 1, result)
-    result = finish(1, kept, exchanged(kept, "blk"), 0, result)
+    result = finish(
+        0,
+        [kept, kept_near, back, exchanged(back, "blk")],
+        ((0, 0, 0), (0, 1, tokens), (1, 0, 0), (1, 1, tokens)),
+        None,
+    )
+    result = finish(
+        1, [rest_kept, exchanged(rest_kept, "blk")], ((0, 0, 0), (0, 1, tokens)), result
+    )
     last_back = after(last_back, result)
-    return finish(1, last_back, exchanged(last_back, "blk"), 1, result)
+    last_near = exchanged(last_back, "blk")
+    result = finish(1, [last_back], ((1, 0, 0),), result)
+    return finish(1, [last_near], ((1, 1, tokens),), result)
 
 
 def solution(mesh):

time: 107 us -> 105 us (0.981)
  waiting for transfers between devices: 37.2 us -> 34 us
  Pallas kernels: 40.9 us -> 43.5 us
  starting transfers between devices: 22.2 us -> 20.4 us
    ppermute x12, waiting for transfers between devices: 6.31 us -> 3.35 us  [exchanged(): return lax.ppermute(block, axis, [(0, 1), (1, 0)])]
    ppermute x12, starting transfers between devices: 7 us -> 4.83 us  [exchanged(): return lax.ppermute(block, axis, [(0, 1), (1, 0)])]
    pallas_call x3 -> x4, Pallas kernels: 16 us -> 18.1 us  [most_projected(): pl.pallas_call(functools.partial(most_kernel, shifts, starts, pairs, posi...]
    ppermute x7, starting transfers between devices: 10.5 us -> 12.4 us  [step(): lax.ppermute(held[1], 'fsdp', behind)]
    ppermute x7, starting transfers between devices: 4.75 us -> 3.23 us  [step(): lax.ppermute(held[0], 'fsdp', ahead)]
    dynamic_slice x0 -> x1, local copies, waits for them, and re-layouts: none -> 1.13 us  [local(): lax.dynamic_slice_in_dim(q_fresh, (1 - side) * half, half, 1)]
    ppermute x7, waiting for transfers between devices: 24.3 us -> 23.2 us  [step(): lax.ppermute(held[1], 'fsdp', behind)]
  transfers between devices with their start and end apart: 26 -> 26, of which waited for: 10 -> 9; matrix products, arithmetic and copies ran while one was open for 5% -> 6% of each run, Pallas kernels for 37% -> 40%
where the time goes in v4:
time: 105 us; the launch traced here: 104 us
  Pallas kernels  43.5 us (41%)
  waiting for transfers between devices  34 us (32%)
  starting transfers between devices  20.4 us (19%)
  local copies, waits for them, and re-layouts  5.26 us (5%)
    ppermute x7, waiting for transfers between devices, step(): lax.ppermute(held[1], 'fsdp', behind)  23.2 us
    pallas_call x4, Pallas kernels, most_projected(): pl.pallas_call(functools.partial(most_kernel, shifts, starts, pairs, posi...  18.1 us
    ppermute x7, starting transfers between devices, step(): lax.ppermute(held[1], 'fsdp', behind)  12.4 us
    pallas_call x1, Pallas kernels, attended_heads(): pl.pallas_call(attend_kernel, out_shape=jax.ShapeDtypeStruct((2 * tokens,...  11.9 us
    pallas_call x4, Pallas kernels, finished(): pl.pallas_call(functools.partial(finish_kernel, offset, places), in_specs...  8.8 us
    ppermute x7, waiting for transfers between devices, step(): lax.ppermute(held[0], 'fsdp', ahead)  7.53 us
    ppermute x12, starting transfers between devices, exchanged(): return lax.ppermute(block, axis, [(0, 1), (1, 0)])  4.83 us
    pallas_call x4, Pallas kernels, last_projected(): pl.pallas_call(functools.partial(last_kernel, positions), out_shape=[jax....  4.63 us
  transfers between devices with their start and end apart: 26, of which 9 were waited for; matrix products, arithmetic and copies ran while one was open for 6% of the time, Pallas kernels for 40%

profile of v4, /device:TPU:0, one launch (start us, length us, event | category | flops | bytes accessed | tf_op | source)
XLA Modules:
  0.0 104.4 jit_solution(2447880966360667622)
XLA Ops:
  0.0 0.5 collective-permute-start.3
  0.5 0.1 collective-permute-start.4
  0.5 1.2 %constant_dynamic-slice_fusion.1.refs_0_ = bf16[320,1280]{1,0:T(8,128)(2,1)S(1)} fusion(bf16[320,5120]{1,0:T(8,128)(2,1)} %param.17, s32[]{:T(128)S(6)} %select_n.6), kind=kLoop, calls=%fused_computation.2 | loop fusion | bytes 1638404 | tf_op jit(solution)/shard_map/dynamic_slice | solution.py:419
  1.7 3.0 %collective-permute-start.1 = (bf16[320,1280]{1,0:T(8,128)(2,1)S(1)}, bf16[320,1280]{1,0:T(8,128)(2,1)S(1)}, u32[]{:S(2)}, u32[]{:S(2)}) collective-permute-start(bf16[320,1280]{1,0:T(8,128)(2,1)S(1)} %constant_dynamic-slice_fusion.1.refs_0_), channel_id=1, source_target_pairs={{4,0},{8,4},{12,8},{14,12},{10,14},{6,10},{2,6},{0,2},{5,1},{9,5},... | collective-permute-start | bytes 2457608 | tf_op jit(solution)/shard_map/ppermute | solution.py:398
  4.7 0.2 collective-permute-start
  4.9 1.1 %constant_dynamic-slice_fusion = bf16[256,1280]{1,0:T(8,128)(2,1)S(1)} fusion(bf16[256,2560]{1,0:T(8,128)(2,1)} %own_q_ref.1, s32[]{:T(128)S(6)} %select_n.7), kind=kLoop, calls=%fused_computation.1 | loop fusion | bytes 1310724 | tf_op jit(solution)/shard_map/dynamic_slice | solution.py:424
  6.0 0.1 collective-permute-start.2
  6.1 0.7 copy.13.keys_ref
  6.8 0.7 pad_add_fusion.ids_ref
  7.4 2.4 %collective-permute-done.2.other_q_ref = bf16[256,1280]{1,0:T(8,128)(2,1)} collective-permute-done((bf16[256,1280]{1,0:T(8,128)(2,1)S(1)}, bf16[256,1280]{1,0:T(8,128)(2,1)}, u32[]{:S(2)}, u32[]{:S(2)}) %collective-permute-start.2) | collective-permute-done | bytes 655392 | tf_op jit(solution)/shard_map/ppermute | solution.py:26
  9.8 0.0 collective-permute-done.3.other_fresh_ref
  9.8 0.0 collective-permute-done.4.other_cache_ref
  9.8 11.9 %attend.1.refs_7_ = bf16[512,1280]{1,0:T(8,128)(2,1)} custom-call(s32[3]{0:T(128)} %pad_add_fusion.ids_ref, s32[1,2,2]{2,1,0:T(2,128)} %list_ref.9, s32[1,2]{1,0:T(1,128)} %count_ref.9, s32[1,4,3]{2,1,0:T(4,128)} %copy.13.keys_ref, bf16[256,2560]{1,0:T(8,128)(2,1)} %own_q_ref.1, bf16[256,1280]{1,0:T(8,128)(2,1)} %collective-permute-done.2.other_q_ref, ...), custom_call_target="tpu_custom_call" | custom-call | tf_op jit(solution)/shard_map/attend/pallas_call | solution.py:168
  21.8 0.5 collective-permute-start.14
  22.2 2.6 %collective-permute-start.5 = (bf16[512,1280]{1,0:T(8,128)(2,1)}, bf16[512,1280]{1,0:T(8,128)(2,1)S(1)}, u32[]{:S(2)}, u32[]{:S(2)}) collective-permute-start(bf16[512,1280]{1,0:T(8,128)(2,1)} %attend.1.refs_7_), channel_id=1, source_target_pairs={{0,16},{16,0},{1,17},{17,1},{2,18},{18,2},{3,19},{19,3},{4,20},{20... | collective-permute-start | bytes 3932168 | tf_op jit(solution)/shard_map/ppermute | solution.py:26
  24.8 0.0 collective-permute-done.1.refs_2_
  24.8 0.0 collective-permute-done.refs_1_
  24.9 1.6 %collective-permute-start.11 = (bf16[320,896]{1,0:T(8,128)(2,1)S(1)}, bf16[320,896]{1,0:T(8,128)(2,1)S(1)}, u32[]{:S(2)}, u32[]{:S(2)}) collective-permute-start(bf16[320,896]{1,0:T(8,128)(2,1)S(1)} %slice.28), channel_id=1, source_target_pairs={{4,0},{8,4},{12,8},{14,12},{10,14},{6,10},{2,6},{0,2},{5,1},{9,5},... | collective-permute-start | bytes 1720328 | tf_op jit(solution)/shard_map/ppermute | solution.py:398
  26.5 1.1 %slice.26 = bf16[320,896]{1,0:T(8,128)(2,1)S(1)} slice(bf16[320,1280]{1,0:T(8,128)(2,1)} %collective-permute-done.refs_1_), slice={[0:320], [0:896]} | slice | bytes 1146880 | tf_op jit(solution)/shard_map/slice | solution.py:464
  27.6 0.5 collective-permute-start.8
  28.1 11.8 %collective-permute-done.11.refs_4_ = bf16[320,896]{1,0:T(8,128)(2,1)S(1)} collective-permute-done((bf16[320,896]{1,0:T(8,128)(2,1)S(1)}, bf16[320,896]{1,0:T(8,128)(2,1)S(1)}, u32[]{:S(2)}, u32[]{:S(2)}) %collective-permute-start.11) | collective-permute-done | bytes 573472 | tf_op jit(solution)/shard_map/ppermute | solution.py:398
  40.0 1.5 %collective-permute-start.12 = (bf16[320,896]{1,0:T(8,128)(2,1)S(1)}, bf16[320,896]{1,0:T(8,128)(2,1)S(1)}, u32[]{:S(2)}, u32[]{:S(2)}) collective-permute-start(bf16[320,896]{1,0:T(8,128)(2,1)S(1)} %collective-permute-done.11.refs_4_), channel_id=1, source_target_pairs={{4,0},{8,4},{12,8},{14,12},{10,14},{6,10},{2,6},{0,2},{5,1},{9,5},... | collective-permute-start | bytes 1720328 | tf_op jit(solution)/shard_map/ppermute | solution.py:398
  41.5 0.9 collective-permute-done.8.refs_3_
  42.3 0.5 collective-permute-start.9
  42.9 11.3 %collective-permute-done.12.refs_6_ = bf16[320,896]{1,0:T(8,128)(2,1)S(1)} collective-permute-done((bf16[320,896]{1,0:T(8,128)(2,1)S(1)}, bf16[320,896]{1,0:T(8,128)(2,1)S(1)}, u32[]{:S(2)}, u32[]{:S(2)}) %collective-permute-start.12) | collective-permute-done | bytes 573472 | tf_op jit(solution)/shard_map/ppermute | solution.py:398
  54.2 2.0 %collective-permute-done.9.refs_5_ = bf16[320,896]{1,0:T(8,128)(2,1)S(1)} collective-permute-done((bf16[320,896]{1,0:T(8,128)(2,1)S(1)}, bf16[320,896]{1,0:T(8,128)(2,1)S(1)}, u32[]{:S(2)}, u32[]{:S(2)}) %collective-permute-start.9) | collective-permute-done | bytes 573472 | tf_op jit(solution)/shard_map/ppermute | solution.py:398
  56.2 0.0 collective-permute-start.15
  56.2 1.6 %collective-permute-start.13 = (bf16[160,896]{1,0:T(8,128)(2,1)S(1)}, bf16[160,896]{1,0:T(8,128)(2,1)S(1)}, u32[]{:S(2)}, u32[]{:S(2)}) collective-permute-start(bf16[160,896]{1,0:T(8,128)(2,1)S(1)} %slice.35), channel_id=1, source_target_pairs={{4,0},{8,4},{12,8},{14,12},{10,14},{6,10},{2,6},{0,2},{5,1},{9,5},... | collective-permute-start | bytes 860168 | tf_op jit(solution)/shard_map/ppermute | solution.py:398
  57.8 0.5 collective-permute-start.10
  58.4 1.0 slice.32
  59.4 0.7 collective-permute-start.6
  60.0 1.4 %collective-permute-start.7 = (bf16[320,384]{1,0:T(8,128)(2,1)S(1)}, bf16[320,384]{1,0:T(8,128)(2,1)S(1)}, u32[]{:S(2)}, u32[]{:S(2)}) collective-permute-start(bf16[320,384]{1,0:T(8,128)(2,1)S(1)} %slice.33), channel_id=1, source_target_pairs={{4,0},{8,4},{12,8},{14,12},{10,14},{6,10},{2,6},{0,2},{5,1},{9,5},... | collective-permute-start | bytes 737288 | tf_op jit(solution)/shard_map/ppermute | solution.py:398
  61.4 5.0 %project_most.4 = (f32[512,896]{1,0:T(8,128)S(1)}, bf16[512,384]{1,0:T(8,128)(2,1)S(1)}) custom-call(s32[3]{0:T(128)S(1)} %copy-done.3, bf16[320,1280]{1,0:T(8,128)(2,1)S(1)} %constant_dynamic-slice_fusion.1.refs_0_, bf16[320,1280]{1,0:T(8,128)(2,1)} %collective-permute-done.refs_1_, bf16[320,1280]{1,0:T(8,128)(2,1)S(1)} %collective-permute-done.1.refs_2_, ...), custom_call_target="tpu_custom_call" | custom-call | flops 2348810240 | tf_op jit(solution)/shard_map/project_most/pallas_call | solution.py:248
  66.4 0.0 copy-start.1
  66.5 0.0 collective-permute-done.13.bottom_ref
  66.5 1.1 %collective-permute-done.10.top_ref = bf16[160,896]{1,0:T(8,128)(2,1)S(1)} collective-permute-done((bf16[160,896]{1,0:T(8,128)(2,1)S(1)}, bf16[160,896]{1,0:T(8,128)(2,1)S(1)}, u32[]{:S(2)}, u32[]{:S(2)}) %collective-permute-start.10) | collective-permute-done | bytes 286752 | tf_op jit(solution)/shard_map/ppermute | solution.py:398
  67.6 1.3 %project_last.4 = bf16[512,896]{1,0:T(8,128)(2,1)S(1)} custom-call(s32[3]{0:T(128)S(1)} %copy-done.3, bf16[160,896]{1,0:T(8,128)(2,1)S(1)} %collective-permute-done.10.top_ref, bf16[160,896]{1,0:T(8,128)(2,1)S(1)} %collective-permute-done.13.bottom_ref, f32[512,896]{1,0:T(8,128)S(1)} %get-tuple-element.31.sums_ref, ...), custom_call_target="tpu_custom_call" | custom-call | tf_op jit(solution)/shard_map/project_last/pallas_call | solution.py:285
  68.9 0.1 collective-permute-start.23
  69.0 3.1 %collective-permute-done.6.refs_3_ = bf16[320,384]{1,0:T(8,128)(2,1)S(1)} collective-permute-done((bf16[320,384]{1,0:T(8,128)(2,1)S(1)}, bf16[320,384]{1,0:T(8,128)(2,1)S(1)}, u32[]{:S(2)}, u32[]{:S(2)}) %collective-permute-start.6) | collective-permute-done | bytes 245792 | tf_op jit(solution)/shard_map/ppermute | solution.py:398
  72.1 0.5 collective-permute-start.16
  72.6 1.6 %collective-permute-start.17 = (bf16[320,384]{1,0:T(8,128)(2,1)S(1)}, bf16[320,384]{1,0:T(8,128)(2,1)S(1)}, u32[]{:S(2)}, u32[]{:S(2)}) collective-permute-start(bf16[320,384]{1,0:T(8,128)(2,1)S(1)} %collective-permute-done.7.refs_4_), channel_id=1, source_target_pairs={{4,0},{8,4},{12,8},{14,12},{10,14},{6,10},{2,6},{0,2},{5,1},{9,5},... | collective-permute-start | bytes 737288 | tf_op jit(solution)/shard_map/ppermute | solution.py:398
  74.1 5.0 %project_most.5 = (f32[512,896]{1,0:T(8,128)S(1)}, bf16[512,384]{1,0:T(8,128)(2,1)S(1)}) custom-call(s32[3]{0:T(128)S(1)} %copy-done.3, bf16[320,1280]{1,0:T(8,128)(2,1)S(1)} %constant_dynamic-slice_fusion.1.refs_0_, bf16[320,1280]{1,0:T(8,128)(2,1)} %collective-permute-done.refs_1_, bf16[320,1280]{1,0:T(8,128)(2,1)S(1)} %collective-permute-done.1.refs_2_, ...), custom_call_target="tpu_custom_call" | custom-call | flops 2348810240 | tf_op jit(solution)/shard_map/project_most/pallas_call | solution.py:248
  79.1 1.3 %project_last.5.refs_0_ = bf16[512,896]{1,0:T(8,128)(2,1)S(1)} custom-call(s32[3]{0:T(128)S(1)} %copy-done.3, bf16[160,896]{1,0:T(8,128)(2,1)S(1)} %collective-permute-done.10.top_ref, bf16[160,896]{1,0:T(8,128)(2,1)S(1)} %collective-permute-done.13.bottom_ref, f32[512,896]{1,0:T(8,128)S(1)} %get-tuple-element.36.sums_ref, ...), custom_call_target="tpu_custom_call" | custom-call | flops 20000000000 | tf_op jit(solution)/shard_map/project_last/pallas_call | solution.py:285
  80.5 1.7 %collective-permute-start.19 = (bf16[160,384]{1,0:T(8,128)(2,1)S(1)}, bf16[160,384]{1,0:T(8,128)(2,1)S(1)}, u32[]{:S(2)}, u32[]{:S(2)}) collective-permute-start(bf16[160,384]{1,0:T(8,128)(2,1)S(1)} %slice.31), channel_id=1, source_target_pairs={{4,0},{8,4},{12,8},{14,12},{10,14},{6,10},{2,6},{0,2},{5,1},{9,5},... | collective-permute-start | bytes 368648 | tf_op jit(solution)/shard_map/ppermute | solution.py:398
  82.3 0.3 collective-permute-start.18
  82.6 4.1 %project_most.6 = (f32[512,384]{1,0:T(8,128)S(1)}, bf16[512,384]{1,0:T(8,128)(2,1)S(1)}) custom-call(s32[3]{0:T(128)S(1)} %copy-done.3, bf16[320,1280]{1,0:T(8,128)(2,1)S(1)} %constant_dynamic-slice_fusion.1.refs_0_, bf16[320,1280]{1,0:T(8,128)(2,1)} %collective-permute-done.refs_1_, bf16[320,1280]{1,0:T(8,128)(2,1)S(1)} %collective-permute-done.1.refs_2_, ...), custom_call_target="tpu_custom_call" | custom-call | flops 1006632960 | tf_op jit(solution)/shard_map/project_most/pallas_call | solution.py:248
  86.7 0.5 collective-permute-done.18.top_ref
  87.2 1.0 project_last.6
  88.2 0.4 collective-permute-start.20
  88.6 4.1 %project_most.7 = (f32[512,384]{1,0:T(8,128)S(1)}, bf16[512,384]{1,0:T(8,128)(2,1)S(1)}) custom-call(s32[3]{0:T(128)S(1)} %copy-done.3, bf16[320,1280]{1,0:T(8,128)(2,1)S(1)} %constant_dynamic-slice_fusion.1.refs_0_, bf16[320,1280]{1,0:T(8,128)(2,1)} %collective-permute-done.refs_1_, bf16[320,1280]{1,0:T(8,128)(2,1)S(1)} %collective-permute-done.1.refs_2_, ...), custom_call_target="tpu_custom_call" | custom-call | flops 1006632960 | tf_op jit(solution)/shard_map/project_most/pallas_call | solution.py:248
  92.7 0.1 collective-permute-start.24
  92.7 0.0 copy-start
  92.7 0.0 copy-start.2
  92.8 0.0 copy-start.4
  92.8 0.0 copy-start.5
  92.8 1.0 project_last.7.refs_0_
  93.8 0.5 collective-permute-start.21
  94.3 0.9 collective-permute-done.24.refs_3_
  95.2 3.4 %finish.4.refs_2_ = bf16[256,5120]{1,0:T(8,128)(2,1)} custom-call(s32[3]{0:T(128)S(1)} %copy-done.3, s32[1,2,2]{2,1,0:T(2,128)S(1)} %copy-done.4, s32[1,2]{1,0:T(1,128)S(1)} %copy-done.5, f32[1,5120]{1,0:T(1,128)S(1)} %bitcast.4, bf16[256,5120]{1,0:T(8,128)(2,1)S(1)} %copy-done, bf16[512,896]{1,0:T(8,128)(2,1)S(1)} %project_last.5.refs_0_, ...), custom_call_target="tpu_custom_call" | custom-call | flops 6000000000 | tf_op jit(solution)/shard_map/finish/pallas_call | solution.py:368
  98.7 2.1 %finish.5.refs_1_ = bf16[256,5120]{1,0:T(8,128)(2,1)} custom-call(s32[3]{0:T(128)S(1)} %copy-done.3, s32[1,2,2]{2,1,0:T(2,128)S(1)} %copy-done.4, s32[1,2]{1,0:T(1,128)S(1)} %copy-done.5, f32[1,5120]{1,0:T(1,128)S(1)} %bitcast.5, bf16[256,5120]{1,0:T(8,128)(2,1)S(1)} %copy-done, ...), custom_call_target="tpu_custom_call", output_to_operand_aliasing={{}: (7, {})} | custom-call | flops 3000000000 | tf_op jit(solution)/shard_map/finish/pallas_call | solution.py:368
  100.8 0.1 collective-permute-start.25
  100.8 1.7 %finish.6.refs_1_ = bf16[256,5120]{1,0:T(8,128)(2,1)} custom-call(s32[3]{0:T(128)S(1)} %copy-done.3, s32[1,2,2]{2,1,0:T(2,128)S(1)} %copy-done.4, s32[1,2]{1,0:T(1,128)S(1)} %copy-done.5, f32[1,5120]{1,0:T(1,128)S(1)} %bitcast.6, bf16[256,5120]{1,0:T(8,128)(2,1)S(1)} %copy-done, ...), custom_call_target="tpu_custom_call", output_to_operand_aliasing={{}: (6, {})} | custom-call | flops 1500000000 | tf_op jit(solution)/shard_map/finish/pallas_call | solution.py:368
  102.5 0.0 collective-permute-done.25.refs_0_
  102.5 1.6 %finish.7 = bf16[256,5120]{1,0:T(8,128)(2,1)} custom-call(s32[3]{0:T(128)S(1)} %copy-done.3, s32[1,2,2]{2,1,0:T(2,128)S(1)} %copy-done.4, s32[1,2]{1,0:T(1,128)S(1)} %copy-done.5, f32[1,5120]{1,0:T(1,128)S(1)} %bitcast.7, bf16[256,5120]{1,0:T(8,128)(2,1)S(1)} %copy-done, ...), custom_call_target="tpu_custom_call", output_to_operand_aliasing={{}: (6, {})} | custom-call | flops 1500000000 | tf_op jit(solution)/shard_map/finish/pallas_call | solution.py:368
  (27 shorter events, 0.2 us)
Async XLA Ops:
  0.0 6.1 %copy-start.6 = (s32[1,4,3]{1,0,2:T(1,128)S(1)}, s32[1,4,3]{1,0,2:T(1,128)}, u32[]{:S(2)}) copy-start(s32[1,4,3]{1,0,2:T(1,128)} %param.16) | copy-start | bytes 148
  0.0 9.8 %collective-permute-start.3 = (bf16[256,2,2560]{2,1,0:T(2,128)(2,1)}, bf16[256,2,2560]{2,1,0:T(2,128)(2,1)}, u32[]{:S(2)}, u32[]{:S(2)}) collective-permute-start(bf16[256,2,2560]{2,1,0:T(2,128)(2,1)} %own_fresh_ref.1), channel_id=1, source_target_pairs={{0,1},{1,0},{2,3},{3,2},{4,5},{5,4},{6,7},{7,6},{8,9},{9,8},{10,11... | collective-permute-start | bytes 7864328 | tf_op jit(solution)/shard_map/ppermute | solution.py:26
  0.5 9.4 %collective-permute-start.4 = (bf16[256,2,2560]{2,1,0:T(2,128)(2,1)}, bf16[256,2,2560]{2,1,0:T(2,128)(2,1)}, u32[]{:S(2)}, u32[]{:S(2)}) collective-permute-start(bf16[256,2,2560]{2,1,0:T(2,128)(2,1)} %own_cache_ref.1), channel_id=1, source_target_pairs={{0,1},{1,0},{2,3},{3,2},{4,5},{5,4},{6,7},{7,6},{8,9},{9,8},{10,11... | collective-permute-start | bytes 7864328 | tf_op jit(solution)/shard_map/ppermute | solution.py:26
  1.7 23.1 %collective-permute-start.1 = (bf16[320,1280]{1,0:T(8,128)(2,1)S(1)}, bf16[320,1280]{1,0:T(8,128)(2,1)S(1)}, u32[]{:S(2)}, u32[]{:S(2)}) collective-permute-start(bf16[320,1280]{1,0:T(8,128)(2,1)S(1)} %constant_dynamic-slice_fusion.1.refs_0_), channel_id=1, source_target_pairs={{4,0},{8,4},{12,8},{14,12},{10,14},{6,10},{2,6},{0,2},{5,1},{9,5},... | collective-permute-start | bytes 2457608 | tf_op jit(solution)/shard_map/ppermute | solution.py:398
  4.7 20.1 %collective-permute-start = (bf16[320,1280]{1,0:T(8,128)(2,1)S(1)}, bf16[320,1280]{1,0:T(8,128)(2,1)}, u32[]{:S(2)}, u32[]{:S(2)}) collective-permute-start(bf16[320,1280]{1,0:T(8,128)(2,1)S(1)} %constant_dynamic-slice_fusion.1.refs_0_), channel_id=1, source_target_pairs={{0,4},{4,8},{8,12},{12,14},{14,10},{10,6},{6,2},{2,0},{1,5},{5,9},... | collective-permute-start | bytes 2457608 | tf_op jit(solution)/shard_map/ppermute | solution.py:398
  6.0 3.8 %collective-permute-start.2 = (bf16[256,1280]{1,0:T(8,128)(2,1)S(1)}, bf16[256,1280]{1,0:T(8,128)(2,1)}, u32[]{:S(2)}, u32[]{:S(2)}) collective-permute-start(bf16[256,1280]{1,0:T(8,128)(2,1)S(1)} %constant_dynamic-slice_fusion), channel_id=1, source_target_pairs={{0,1},{1,0},{2,3},{3,2},{4,5},{5,4},{6,7},{7,6},{8,9},{9,8},{10,11... | collective-permute-start | bytes 1966088 | tf_op jit(solution)/shard_map/ppermute | solution.py:26
  21.7 39.7 %copy-start.3 = (s32[3]{0:T(128)S(1)}, s32[3]{0:T(128)}, u32[]{:S(2)}) copy-start(s32[3]{0:T(128)} %pad_add_fusion.ids_ref) | copy-start | bytes 40
  21.8 34.4 %collective-permute-start.14 = (bf16[512,1280]{1,0:T(8,128)(2,1)}, bf16[512,1280]{1,0:T(8,128)(2,1)S(1)}, u32[]{:S(2)}, u32[]{:S(2)}) collective-permute-start(bf16[512,1280]{1,0:T(8,128)(2,1)} %attend.1.refs_7_), channel_id=1, source_target_pairs={{0,1},{1,0},{2,3},{3,2},{4,5},{5,4},{6,7},{7,6},{8,9},{9,8},{10,11... | collective-permute-start | bytes 3932168 | tf_op jit(solution)/shard_map/ppermute | solution.py:26
  22.2 33.9 %collective-permute-start.5 = (bf16[512,1280]{1,0:T(8,128)(2,1)}, bf16[512,1280]{1,0:T(8,128)(2,1)S(1)}, u32[]{:S(2)}, u32[]{:S(2)}) collective-permute-start(bf16[512,1280]{1,0:T(8,128)(2,1)} %attend.1.refs_7_), channel_id=1, source_target_pairs={{0,16},{16,0},{1,17},{17,1},{2,18},{18,2},{3,19},{19,3},{4,20},{20... | collective-permute-start | bytes 3932168 | tf_op jit(solution)/shard_map/ppermute | solution.py:26
  24.9 15.1 %collective-permute-start.11 = (bf16[320,896]{1,0:T(8,128)(2,1)S(1)}, bf16[320,896]{1,0:T(8,128)(2,1)S(1)}, u32[]{:S(2)}, u32[]{:S(2)}) collective-permute-start(bf16[320,896]{1,0:T(8,128)(2,1)S(1)} %slice.28), channel_id=1, source_target_pairs={{4,0},{8,4},{12,8},{14,12},{10,14},{6,10},{2,6},{0,2},{5,1},{9,5},... | collective-permute-start | bytes 1720328 | tf_op jit(solution)/shard_map/ppermute | solution.py:398
  27.6 14.7 %collective-permute-start.8 = (bf16[320,896]{1,0:T(8,128)(2,1)S(1)}, bf16[320,896]{1,0:T(8,128)(2,1)S(1)}, u32[]{:S(2)}, u32[]{:S(2)}) collective-permute-start(bf16[320,896]{1,0:T(8,128)(2,1)S(1)} %slice.26), channel_id=1, source_target_pairs={{0,4},{4,8},{8,12},{12,14},{14,10},{10,6},{6,2},{2,0},{1,5},{5,9},... | collective-permute-start | bytes 1720328 | tf_op jit(solution)/shard_map/ppermute | solution.py:398
  40.0 14.2 %collective-permute-start.12 = (bf16[320,896]{1,0:T(8,128)(2,1)S(1)}, bf16[320,896]{1,0:T(8,128)(2,1)S(1)}, u32[]{:S(2)}, u32[]{:S(2)}) collective-permute-start(bf16[320,896]{1,0:T(8,128)(2,1)S(1)} %collective-permute-done.11.refs_4_), channel_id=1, source_target_pairs={{4,0},{8,4},{12,8},{14,12},{10,14},{6,10},{2,6},{0,2},{5,1},{9,5},... | collective-permute-start | bytes 1720328 | tf_op jit(solution)/shard_map/ppermute | solution.py:398
  42.3 13.8 %collective-permute-start.9 = (bf16[320,896]{1,0:T(8,128)(2,1)S(1)}, bf16[320,896]{1,0:T(8,128)(2,1)S(1)}, u32[]{:S(2)}, u32[]{:S(2)}) collective-permute-start(bf16[320,896]{1,0:T(8,128)(2,1)S(1)} %collective-permute-done.8.refs_3_), channel_id=1, source_target_pairs={{0,4},{4,8},{8,12},{12,14},{14,10},{10,6},{6,2},{2,0},{1,5},{5,9},... | collective-permute-start | bytes 1720328 | tf_op jit(solution)/shard_map/ppermute | solution.py:398
  56.2 5.3 %collective-permute-start.15 = (bf16[512,1280]{1,0:T(8,128)(2,1)S(1)}, bf16[512,1280]{1,0:T(8,128)(2,1)S(1)}, u32[]{:S(2)}, u32[]{:S(2)}) collective-permute-start(bf16[512,1280]{1,0:T(8,128)(2,1)S(1)} %collective-permute-done.5.refs_7_), channel_id=1, source_target_pairs={{0,1},{1,0},{2,3},{3,2},{4,5},{5,4},{6,7},{7,6},{8,9},{9,8},{10,11... | collective-permute-start | bytes 3932168 | tf_op jit(solution)/shard_map/ppermute | solution.py:26
  56.2 10.3 %collective-permute-start.13 = (bf16[160,896]{1,0:T(8,128)(2,1)S(1)}, bf16[160,896]{1,0:T(8,128)(2,1)S(1)}, u32[]{:S(2)}, u32[]{:S(2)}) collective-permute-start(bf16[160,896]{1,0:T(8,128)(2,1)S(1)} %slice.35), channel_id=1, source_target_pairs={{4,0},{8,4},{12,8},{14,12},{10,14},{6,10},{2,6},{0,2},{5,1},{9,5},... | collective-permute-start | bytes 860168 | tf_op jit(solution)/shard_map/ppermute | solution.py:398
  57.8 9.7 %collective-permute-start.10 = (bf16[160,896]{1,0:T(8,128)(2,1)S(1)}, bf16[160,896]{1,0:T(8,128)(2,1)S(1)}, u32[]{:S(2)}, u32[]{:S(2)}) collective-permute-start(bf16[160,896]{1,0:T(8,128)(2,1)S(1)} %slice.34), channel_id=1, source_target_pairs={{0,4},{4,8},{8,12},{12,14},{14,10},{10,6},{6,2},{2,0},{1,5},{5,9},... | collective-permute-start | bytes 860168 | tf_op jit(solution)/shard_map/ppermute | solution.py:398
  59.4 12.7 %collective-permute-start.6 = (bf16[320,384]{1,0:T(8,128)(2,1)S(1)}, bf16[320,384]{1,0:T(8,128)(2,1)S(1)}, u32[]{:S(2)}, u32[]{:S(2)}) collective-permute-start(bf16[320,384]{1,0:T(8,128)(2,1)S(1)} %slice.32), channel_id=1, source_target_pairs={{0,4},{4,8},{8,12},{12,14},{14,10},{10,6},{6,2},{2,0},{1,5},{5,9},... | collective-permute-start | bytes 737288 | tf_op jit(solution)/shard_map/ppermute | solution.py:398
  60.0 12.1 %collective-permute-start.7 = (bf16[320,384]{1,0:T(8,128)(2,1)S(1)}, bf16[320,384]{1,0:T(8,128)(2,1)S(1)}, u32[]{:S(2)}, u32[]{:S(2)}) collective-permute-start(bf16[320,384]{1,0:T(8,128)(2,1)S(1)} %slice.33), channel_id=1, source_target_pairs={{4,0},{8,4},{12,8},{14,12},{10,14},{6,10},{2,6},{0,2},{5,1},{9,5},... | collective-permute-start | bytes 737288 | tf_op jit(solution)/shard_map/ppermute | solution.py:398
  66.4 7.7 %copy-start.1 = (bf16[512,1280]{1,0:T(8,128)(2,1)S(1)}, bf16[512,1280]{1,0:T(8,128)(2,1)}, u32[]{:S(2)}) copy-start(bf16[512,1280]{1,0:T(8,128)(2,1)} %attend.1.refs_7_) | copy-start | bytes 3932164
  68.9 23.8 %collective-permute-start.23 = (bf16[512,896]{1,0:T(8,128)(2,1)S(1)}, bf16[512,896]{1,0:T(8,128)(2,1)S(1)}, u32[]{:S(2)}, u32[]{:S(2)}) collective-permute-start(bf16[512,896]{1,0:T(8,128)(2,1)S(1)} %project_last.4), channel_id=1, source_target_pairs={{0,16},{16,0},{1,17},{17,1},{2,18},{18,2},{3,19},{19,3},{4,20},{20... | collective-permute-start | bytes 2752520 | tf_op jit(solution)/shard_map/ppermute | solution.py:26
  72.1 8.4 %collective-permute-start.16 = (bf16[320,384]{1,0:T(8,128)(2,1)S(1)}, bf16[320,384]{1,0:T(8,128)(2,1)S(1)}, u32[]{:S(2)}, u32[]{:S(2)}) collective-permute-start(bf16[320,384]{1,0:T(8,128)(2,1)S(1)} %collective-permute-done.6.refs_3_), channel_id=1, source_target_pairs={{0,4},{4,8},{8,12},{12,14},{14,10},{10,6},{6,2},{2,0},{1,5},{5,9},... | collective-permute-start | bytes 737288 | tf_op jit(solution)/shard_map/ppermute | solution.py:398
  72.6 7.9 %collective-permute-start.17 = (bf16[320,384]{1,0:T(8,128)(2,1)S(1)}, bf16[320,384]{1,0:T(8,128)(2,1)S(1)}, u32[]{:S(2)}, u32[]{:S(2)}) collective-permute-start(bf16[320,384]{1,0:T(8,128)(2,1)S(1)} %collective-permute-done.7.refs_4_), channel_id=1, source_target_pairs={{4,0},{8,4},{12,8},{14,12},{10,14},{6,10},{2,6},{0,2},{5,1},{9,5},... | collective-permute-start | bytes 737288 | tf_op jit(solution)/shard_map/ppermute | solution.py:398
  80.5 6.2 %collective-permute-start.19 = (bf16[160,384]{1,0:T(8,128)(2,1)S(1)}, bf16[160,384]{1,0:T(8,128)(2,1)S(1)}, u32[]{:S(2)}, u32[]{:S(2)}) collective-permute-start(bf16[160,384]{1,0:T(8,128)(2,1)S(1)} %slice.31), channel_id=1, source_target_pairs={{4,0},{8,4},{12,8},{14,12},{10,14},{6,10},{2,6},{0,2},{5,1},{9,5},... | collective-permute-start | bytes 368648 | tf_op jit(solution)/shard_map/ppermute | solution.py:398
  82.3 4.9 %collective-permute-start.18 = (bf16[160,384]{1,0:T(8,128)(2,1)S(1)}, bf16[160,384]{1,0:T(8,128)(2,1)S(1)}, u32[]{:S(2)}, u32[]{:S(2)}) collective-permute-start(bf16[160,384]{1,0:T(8,128)(2,1)S(1)} %slice.30), channel_id=1, source_target_pairs={{0,4},{4,8},{8,12},{12,14},{14,10},{10,6},{6,2},{2,0},{1,5},{5,9},... | collective-permute-start | bytes 368648 | tf_op jit(solution)/shard_map/ppermute | solution.py:398
  82.6 11.7 %collective-permute-start.22 = (bf16[512,896]{1,0:T(8,128)(2,1)S(1)}, bf16[512,896]{1,0:T(8,128)(2,1)S(1)}, u32[]{:S(2)}, u32[]{:S(2)}) collective-permute-start(bf16[512,896]{1,0:T(8,128)(2,1)S(1)} %project_last.5.refs_0_), channel_id=1, source_target_pairs={{0,1},{1,0},{2,3},{3,2},{4,5},{5,4},{6,7},{7,6},{8,9},{9,8},{10,11... | collective-permute-start | bytes 2752520 | tf_op jit(solution)/shard_map/ppermute | solution.py:26
  88.2 12.6 %collective-permute-start.20 = (bf16[512,384]{1,0:T(8,128)(2,1)S(1)}, bf16[512,384]{1,0:T(8,128)(2,1)S(1)}, u32[]{:S(2)}, u32[]{:S(2)}) collective-permute-start(bf16[512,384]{1,0:T(8,128)(2,1)S(1)} %project_last.6), channel_id=1, source_target_pairs={{0,16},{16,0},{1,17},{17,1},{2,18},{18,2},{3,19},{19,3},{4,20},{20... | collective-permute-start | bytes 1179656 | tf_op jit(solution)/shard_map/ppermute | solution.py:26
  92.7 2.5 %collective-permute-start.24 = (bf16[512,896]{1,0:T(8,128)(2,1)S(1)}, bf16[512,896]{1,0:T(8,128)(2,1)S(1)}, u32[]{:S(2)}, u32[]{:S(2)}) collective-permute-start(bf16[512,896]{1,0:T(8,128)(2,1)S(1)} %collective-permute-done.23.refs_2_), channel_id=1, source_target_pairs={{0,1},{1,0},{2,3},{3,2},{4,5},{5,4},{6,7},{7,6},{8,9},{9,8},{10,11... | collective-permute-start | bytes 2752520 | tf_op jit(solution)/shard_map/ppermute | solution.py:26
  92.7 2.5 %copy-start = (bf16[256,5120]{1,0:T(8,128)(2,1)S(1)}, bf16[256,5120]{1,0:T(8,128)(2,1)}, u32[]{:S(2)}) copy-start(bf16[256,5120]{1,0:T(8,128)(2,1)} %input_ref.7) | copy-start | bytes 7864324
  92.7 2.5 %copy-start.2 = (f32[5120]{0:T(1024)S(1)}, f32[5120]{0:T(1024)}, u32[]{:S(2)}) copy-start(f32[5120]{0:T(1024)} %param.10) | copy-start | bytes 61444
  92.8 2.4 %copy-start.4 = (s32[1,2,2]{2,1,0:T(2,128)S(1)}, s32[1,2,2]{2,1,0:T(2,128)}, u32[]{:S(2)}) copy-start(s32[1,2,2]{2,1,0:T(2,128)} %list_ref.9) | copy-start | bytes 52
  92.8 2.4 %copy-start.5 = (s32[1,2]{1,0:T(1,128)S(1)}, s32[1,2]{1,0:T(1,128)}, u32[]{:S(2)}) copy-start(s32[1,2]{1,0:T(1,128)} %count_ref.9) | copy-start | bytes 28
  93.8 4.9 %collective-permute-start.21 = (bf16[512,384]{1,0:T(8,128)(2,1)S(1)}, bf16[512,384]{1,0:T(8,128)(2,1)S(1)}, u32[]{:S(2)}, u32[]{:S(2)}) collective-permute-start(bf16[512,384]{1,0:T(8,128)(2,1)S(1)} %project_last.7.refs_0_), channel_id=1, source_target_pairs={{0,1},{1,0},{2,3},{3,2},{4,5},{5,4},{6,7},{7,6},{8,9},{9,8},{10,11... | collective-permute-start | bytes 1179656 | tf_op jit(solution)/shard_map/ppermute | solution.py:26
  100.8 1.8 %collective-permute-start.25 = (bf16[512,384]{1,0:T(8,128)(2,1)S(1)}, bf16[512,384]{1,0:T(8,128)(2,1)S(1)}, u32[]{:S(2)}, u32[]{:S(2)}) collective-permute-start(bf16[512,384]{1,0:T(8,128)(2,1)S(1)} %collective-permute-done.20.refs_0_), channel_id=1, source_target_pairs={{0,1},{1,0},{2,3},{3,2},{4,5},{5,4},{6,7},{7,6},{8,9},{9,8},{10,11... | collective-permute-start | bytes 1179656 | tf_op jit(solution)/shard_map/ppermute | solution.py:26

commit v5 on v4

--- a/solution.py
+++ b/solution.py
@@ -63,7 +63,7 @@
     bias,
     sems,
 ):
-    spans, _, tokens, width = queries.shape
+    spans, tokens, width = queries.shape[0], queries.shape[1] // 2, queries.shape[2]
     tiles = list_ref.shape[2]
     rows = tokens // tiles
     own_side = ids_ref[2]
@@ -79,7 +79,9 @@
         else:
             source = other_q_ref.at[:, pl.ds(span * width, width)]
         return pltpu.make_async_copy(
-            source, queries.at[span, side], sems.at[span, 2 * tiles + side]
+            source,
+            queries.at[span, pl.ds(side * tokens, tokens)],
+            sems.at[span, 2 * tiles + side],
         )
 
     def load_pairs(span, index, ref):
@@ -116,7 +118,8 @@
                         listed = keys_ref[0, sides[asking] * tiles + query, slot]
                         allowed = jnp.where(listed == sides[side] * tiles + key, 1, allowed)
                     start = (side * tiles + key) * rows
-                    bias[asking, query * rows : (query + 1) * rows, start : start + rows] = jnp.full(
+                    at = (asking * tiles + query) * rows
+                    bias[at : at + rows, start : start + rows] = jnp.full(
                         (rows, rows), jnp.where(allowed != 0, 0.0, MASKED), jnp.float32
                     )
 
@@ -138,26 +141,23 @@
             value_rows[index * rows : (index + 1) * rows] = sorted_rows[rows:]
         for asking in range(2):
             load_queries(span, asking).wait()
-            for head in range(width // HEAD_DIM):
-                cols = slice(head * HEAD_DIM, (head + 1) * HEAD_DIM)
-                scores = lax.dot_general(
-                    queries[span, asking, :, cols],
-                    key_rows[:, cols],
-                    contract_last,
-                    preferred_element_type=jnp.float32,
-                )
-                scores = scores * scale + bias[asking]
-                terms = jnp.exp2(scores - jnp.max(scores, axis=1, keepdims=True))
-                total = jnp.sum(terms, axis=1, keepdims=True)
-                summed = jnp.dot(
-                    terms.astype(jnp.bfloat16),
-                    value_rows[:, cols],
-                    preferred_element_type=jnp.float32,
-                )
-                out_ref[
-                    asking * tokens : (asking + 1) * tokens,
-                    span * width + cols.start : span * width + cols.stop,
-                ] = (summed / total).astype(jnp.bfloat16)
+        for head in range(width // HEAD_DIM):
+            cols = slice(head * HEAD_DIM, (head + 1) * HEAD_DIM)
+            scores = lax.dot_general(
+                queries[span, :, cols],
+                key_rows[:, cols],
+                contract_last,
+                preferred_element_type=jnp.float32,
+            )
+            scores = scores * scale + bias[...]
+            terms = jnp.exp2(scores - jnp.max(scores, axis=1, keepdims=True))
+            total = jnp.sum(terms, axis=1, keepdims=True)
+            summed = jnp.dot(
+                terms.astype(jnp.bfloat16), value_rows[:, cols], preferred_element_type=jnp.float32
+            )
+            out_ref[:, span * width + cols.start : span * width + cols.stop] = (
+                summed / total
+            ).astype(jnp.bfloat16)
 
 
 def attended_heads(ids, active_list, active_count, key_list, queries, pairs):
@@ -171,11 +171,11 @@
         in_specs=[SMEM] * 4 + [HBM] * 6,
         out_specs=VMEM,
         scratch_shapes=[
-            pltpu.VMEM((spans, 2, tokens, span), jnp.bfloat16),
+            pltpu.VMEM((spans, 2 * tokens, span), jnp.bfloat16),
             pltpu.VMEM((spans, 2 * tiles, rows, 2, span), jnp.bfloat16),
             pltpu.VMEM((2 * tokens, span), jnp.bfloat16),
             pltpu.VMEM((2 * tokens, span), jnp.bfloat16),
-            pltpu.VMEM((2, tokens, 2 * tokens), jnp.float32),
+            pltpu.VMEM((2 * tokens, 2 * tokens), jnp.float32),
             pltpu.SemaphoreType.DMA((spans, 2 * tiles + 2)),
         ],
         compiler_params=params(ALL_VMEM),
@@ -190,21 +190,23 @@
     return pl.multiple_of(first, 128), pl.multiple_of(start - first, math.gcd(depth, 128))
 
 
-def most_kernel(shifts, starts, pairs, positions, ids_ref, *refs):
+def most_kernel(shifts, starts, pairs, positions, whole, ids_ref, *refs):
     pieces = len(shifts)
     piece_refs, row_refs, refs = refs[:pieces], refs[pieces:][: 2 * pairs], refs[pieces + 2 * pairs :]
-    sums, cuts, (weight, held, row_sems, sems) = refs[:pairs], refs[pairs:][:pairs], refs[2 * pairs :]
+    sums, cuts, (weight, held, row_sems, sems) = refs[:pairs], refs[pairs:-4], refs[-4:]
     depth = piece_refs[0].shape[0]
     blocks, rows, width = held.shape
     side = ids_ref[2]
     halves = [pl.ds(pl.multiple_of(at * (width // 2), 128), width // 2) for at in (side, 1 - side)]
 
     def load_piece(index):
-        place = ring_neighbour(ids_ref[1], shifts[index], positions)
-        start = pl.multiple_of(place * depth, math.gcd(depth, 64))
+        piece = piece_refs[index].shape[0]
+        later = piece if index == positions else 0
+        start = ring_neighbour(ids_ref[1], shifts[index], positions) * depth + later
+        start = pl.multiple_of(start, math.gcd(piece, 64))
         return pltpu.make_async_copy(
             piece_refs[index].at[:, pl.ds(starts[index], weight.shape[1])],
-            weight.at[pl.ds(start, depth)],
+            weight.at[pl.ds(start, piece)],
             sems.at[index],
         )
 
@@ -226,8 +228,9 @@
         for copy in load_rows(block):
             copy.start()
     missing = ring_neighbour(ids_ref[1], positions // 2, positions)
-    start = pl.multiple_of(missing * depth, math.gcd(depth, 64))
-    weight[pl.ds(start, depth)] = jnp.zeros((depth, weight.shape[1]), weight.dtype)
+    if not whole:
+        start = pl.multiple_of(missing * depth, math.gcd(depth, 64))
+        weight[pl.ds(start, depth)] = jnp.zeros((depth, weight.shape[1]), weight.dtype)
     for index in range(pieces):
         load_piece(index).wait()
     first, _ = window(missing, depth)
@@ -237,20 +240,22 @@
         span = slice(block % 2 * rows, (block % 2 + 1) * rows)
         sums[block // 2][span] = jnp.dot(
             held[block], weight[...], preferred_element_type=jnp.float32
-        )
-        cuts[block // 2][span] = held[block, :, pl.ds(first, cuts[0].shape[1])]
+        ).astype(sums[0].dtype)
+        if not whole:
+            cuts[block // 2][span] = held[block, :, pl.ds(first, cuts[0].shape[1])]
 
 
 def most_projected(ids, positions, pieces, shifts, starts, cols, row_halves):
     depth, pairs = pieces[0].shape[0], len(row_halves) // 2
     rows = row_halves[0].shape[0] // 2
-    cut = -(-(depth + 64) // 128) * 128
+    cut, whole = -(-(depth + 64) // 128) * 128, len(pieces) > positions
+    sums = jax.ShapeDtypeStruct((2 * rows, cols), jnp.bfloat16 if whole else jnp.float32)
+    cuts = [] if whole else [jax.ShapeDtypeStruct((2 * rows, cut), jnp.bfloat16)] * pairs
     return pl.pallas_call(
-        functools.partial(most_kernel, shifts, starts, pairs, positions),
-        out_shape=[jax.ShapeDtypeStruct((2 * rows, cols), jnp.float32)] * pairs
-        + [jax.ShapeDtypeStruct((2 * rows, cut), jnp.bfloat16)] * pairs,
+        functools.partial(most_kernel, shifts, starts, pairs, positions, whole),
+        out_shape=[sums] * pairs + cuts,
         in_specs=[SMEM] + [HBM] * (len(pieces) + 2 * pairs),
-        out_specs=[VMEM] * (2 * pairs),
+        out_specs=[VMEM] * (pairs + len(cuts)),
         scratch_shapes=[
             pltpu.VMEM((positions * depth, cols), jnp.bfloat16),
             pltpu.VMEM((2 * pairs, rows, positions * depth), jnp.bfloat16),
@@ -259,7 +264,9 @@
         ],
         compiler_params=params(SOME_VMEM),
         cost_estimate=pl.CostEstimate(
-            flops=4 * rows * pairs * depth * positions * cols, bytes_accessed=0, transcendentals=0
+            flops=22_000_000_000 if whole else 4 * rows * pairs * depth * positions * cols,
+            bytes_accessed=0,
+            transcendentals=0,
         ),
         name="project_most",
     )(ids, *pieces, *row_halves)
@@ -296,37 +303,40 @@
     return result[0] if count == 1 else result
 
 
-def finish_kernel(offset, places, ids_ref, list_ref, count_ref, gate_ref, input_ref, *refs):
+def finish_kernel(places, ids_ref, list_ref, count_ref, gate_ref, input_ref, *refs):
     sources = refs[: len(places)]
     out_ref, inputs, products, outputs, sems = refs[-5:]
-    tokens, width = outputs.shape[1:]
+    tokens = outputs.shape[1]
+    widths = [source.shape[1] for source in sources]
     quarter = input_ref.shape[1] // 4
     tiles = list_ref.shape[2]
     rows = tokens // tiles
     side = ids_ref[2]
 
     def columns(index):
-        far, other, _ = places[index]
+        far, other, _, offset = places[index]
         of_part = 1 - ids_ref[0] if far else ids_ref[0]
         of_side = 1 - side if other else side
         start = (of_part * 2 + of_side) * quarter + offset
-        return pl.ds(pl.multiple_of(start, 128), width)
+        return pl.ds(pl.multiple_of(start, 128), widths[index])
 
     def loads(index):
         return (
             pltpu.make_async_copy(
-                input_ref.at[:, columns(index)], inputs.at[index], sems.at[0, index]
+                input_ref.at[:, columns(index)], inputs.at[index, :, pl.ds(0, widths[index])], sems.at[0, index]
             ),
             pltpu.make_async_copy(
                 sources[index].at[pl.ds(places[index][2], tokens)],
-                products.at[index],
+                products.at[index, :, pl.ds(0, widths[index])],
                 sems.at[1, index],
             ),
         )
 
     def store(index):
         return pltpu.make_async_copy(
-            outputs.at[index], out_ref.at[:, columns(index)], sems.at[2, index]
+            outputs.at[index, :, pl.ds(0, widths[index])],
+            out_ref.at[:, columns(index)],
+            sems.at[2, index],
         )
 
     for index in range(len(places)):
@@ -335,29 +345,29 @@
     for index in range(len(places)):
         for copy in loads(index):
             copy.wait()
-        gate = gate_ref[:, columns(index)]
+        gate, cols = gate_ref[:, columns(index)], slice(0, widths[index])
         for tile in range(tiles):
             span = slice(tile * rows, (tile + 1) * rows)
             active = tile_active(list_ref, count_ref, side, tile)
 
             @pl.when(active)
-            def _(index=index, span=span, gate=gate):
-                mixed = inputs[index, span].astype(jnp.float32)
-                mixed = mixed + gate * products[index, span].astype(jnp.float32)
-                outputs[index, span] = mixed.astype(jnp.bfloat16)
+            def _(index=index, span=span, cols=cols, gate=gate):
+                mixed = inputs[index, span, cols].astype(jnp.float32)
+                mixed = mixed + gate * products[index, span, cols].astype(jnp.float32)
+                outputs[index, span, cols] = mixed.astype(jnp.bfloat16)
 
             @pl.when(jnp.logical_not(active))
-            def _(index=index, span=span):
-                outputs[index, span] = inputs[index, span]
+            def _(index=index, span=span, cols=cols):
+                outputs[index, span, cols] = inputs[index, span, cols]
 
         store(index).start()
     for index in range(len(places)):
         store(index).wait()
 
 
-def finished(ids, active_list, active_count, gate, block_input, sources, places, offset, earlier):
+def finished(ids, active_list, active_count, gate, block_input, sources, places, earlier):
     tokens, total = block_input.shape
-    width, count = sources[0].shape[1], len(sources)
+    width, count = max(source.shape[1] for source in sources), len(sources)
     args = [ids, active_list, active_count, gate[None], block_input, *sources]
     in_specs = [SMEM, SMEM, SMEM, VMEM, HBM] + [HBM] * count
     aliases = {}
@@ -366,7 +376,7 @@
         args.append(earlier)
         in_specs.append(HBM)
     return pl.pallas_call(
-        functools.partial(finish_kernel, offset, places),
+        functools.partial(finish_kernel, places),
         in_specs=in_specs,
         out_specs=HBM,
         out_shape=jax.ShapeDtypeStruct((tokens, total), jnp.bfloat16),
@@ -425,11 +435,8 @@
     ]
     own_rows = attended_heads(ids, active_list, active_count, key_list, queries, pairs)
 
-    def finish(index, sources, places, earlier):
-        start = (0, first)[index]
-        return finished(
-            ids, active_list, active_count, gate, block_input, sources, places, start, earlier
-        )
+    def finish(sources, places, earlier):
+        return finished(ids, active_list, active_count, gate, block_input, sources, places, earlier)
 
     tokens = block_input.shape[0]
     if not ringed:
@@ -449,17 +456,18 @@
                 if from_parts == 1:
                     rows = exchanged(rows, "groups")
                 sources = [rows, exchanged(rows, "blk")]
-                places = ((from_parts, 0, 0), (from_parts, 1, tokens))
-                result = finish(index, sources, places, result)
+                start = (0, first)[index]
+                places = ((from_parts, 0, 0, start), (from_parts, 1, tokens, start))
+                result = finish(sources, places, result)
         return result
 
     step, last_step = ring_steps(ring_order(positions))
 
     def most(pieces, start, width, *row_halves):
-        shifts, starts = (0, -1, 1, -2, 2, -3, 3), (start,) * 3 + (0,) * 4
+        shifts = (0, -1, 1, -2, 2, -3, 3, 4, 4)[: len(pieces)]
+        starts = ((start,) * 3 + (0,) * 6)[: len(pieces)]
         return most_projected(ids, positions, pieces, shifts, starts, width, row_halves)
 
-    much = 20_000_000_000
     both_1 = step([columns] * 2)
     first_1 = [block[:, :first] for block in all_after(both_1, own_rows)]
     first_2 = step(first_1)
@@ -474,8 +482,9 @@
     far_sums, far_cut = most(pieces, 0, first, far_rows, far_near_rows)
     away = last_projected(ids, positions, first_4, far_sums, far_cut, 0)
     back = exchanged(away, "groups")
-    own_sums, own_cut = most(pieces, 0, first, after(own_rows, away, *second_2), near_rows)
-    kept = last_projected(ids, positions, first_4, own_sums, own_cut, much)
+    (kept,) = most(
+        [*pieces, *first_4], 0, first, after(own_rows, away, *second_2), near_rows
+    )
     second_3 = step(all_after(second_2, away))
     second_4 = last_step(all_after(second_3, kept))
     kept_near = exchanged(kept, "blk")
@@ -483,22 +492,24 @@
     far_sums, far_cut = most(pieces, first, rest, far_rows, far_near_rows)
     away = last_projected(ids, positions, second_4, far_sums, far_cut, 0)
     last_back = exchanged(away, "groups")
-    own_sums, own_cut = most(pieces, first, rest, after(own_rows, away), near_rows)
-    rest_kept = last_projected(ids, positions, second_4, own_sums, own_cut, much)
+    (rest_kept,) = most(
+        [*pieces, *second_4], first, rest, after(own_rows, away), near_rows
+    )
     back = after(back, *second_4)
     result = finish(
-        0,
         [kept, kept_near, back, exchanged(back, "blk")],
-        ((0, 0, 0), (0, 1, tokens), (1, 0, 0), (1, 1, tokens)),
+        ((0, 0, 0, 0), (0, 1, tokens, 0), (1, 0, 0, 0), (1, 1, tokens, 0)),
         None,
     )
     result = finish(
-        1, [rest_kept, exchanged(rest_kept, "blk")], ((0, 0, 0), (0, 1, tokens)), result
+        [rest_kept, exchanged(rest_kept, "blk")],
+        ((0, 0, 0, first), (0, 1, tokens, first)),
+        result,
     )
     last_back = after(last_back, result)
     last_near = exchanged(last_back, "blk")
-    result = finish(1, [last_back], ((1, 0, 0),), result)
-    return finish(1, [last_near], ((1, 1, tokens),), result)
+    result = finish([last_back], ((1, 0, 0, first),), result)
+    return finish([last_near], ((1, 1, tokens, first),), result)
 
 
 def solution(mesh):

time: 105 us -> 102 us (0.971)
  Pallas kernels: 43.5 us -> 38.3 us
  starting transfers between devices: 20.4 us -> 23.4 us
    ppermute x12, starting transfers between devices: 4.83 us -> 7.82 us  [exchanged(): return lax.ppermute(block, axis, [(0, 1), (1, 0)])]
    pallas_call x1, Pallas kernels: 11.9 us -> 9.19 us  [attended_heads(): pl.pallas_call(attend_kernel, out_shape=jax.ShapeDtypeStruct((2 * tokens,...]
    pallas_call x4 -> x2, Pallas kernels: 4.63 us -> 2.31 us  [last_projected(): pl.pallas_call(functools.partial(last_kernel, positions), out_shape=[jax....]
    ppermute x7, waiting for transfers between devices: 23.2 us -> 21.9 us  [step(): lax.ppermute(held[1], 'fsdp', behind)]
  transfers between devices with their start and end apart: 26 -> 26, of which waited for: 9 -> 13; matrix products, arithmetic and copies ran while one was open for 6% -> 6% of each run, Pallas kernels for 40% -> 36%
where the time goes in v5:
time: 102 us; the launch traced here: 101 us
  Pallas kernels  38.3 us (38%)
  waiting for transfers between devices  33.4 us (33%)
  starting transfers between devices  23.4 us (23%)
  local copies, waits for them, and re-layouts  5.27 us (5%)
    ppermute x7, waiting for transfers between devices, step(): lax.ppermute(held[1], 'fsdp', behind)  21.9 us
    pallas_call x4, Pallas kernels, most_projected(): pl.pallas_call(functools.partial(most_kernel, shifts, starts, pairs, posi...  18.4 us
    ppermute x7, starting transfers between devices, step(): lax.ppermute(held[1], 'fsdp', behind)  12.6 us
    pallas_call x1, Pallas kernels, attended_heads(): pl.pallas_call(attend_kernel, out_shape=jax.ShapeDtypeStruct((2 * tokens,...  9.19 us
    pallas_call x4, Pallas kernels, finished(): pl.pallas_call(functools.partial(finish_kernel, places), in_specs=in_spec...  8.43 us
    ppermute x7, waiting for transfers between devices, step(): lax.ppermute(held[0], 'fsdp', ahead)  7.87 us
    ppermute x12, starting transfers between devices, exchanged(): return lax.ppermute(block, axis, [(0, 1), (1, 0)])  7.82 us
    ppermute x12, waiting for transfers between devices, exchanged(): return lax.ppermute(block, axis, [(0, 1), (1, 0)])  3.65 us
  transfers between devices with their start and end apart: 26, of which 13 were waited for; matrix products, arithmetic and copies ran while one was open for 6% of the time, Pallas kernels for 36%

profile of v5, /device:TPU:0, one launch (start us, length us, event | category | flops | bytes accessed | tf_op | source)
XLA Modules:
  0.0 101.5 jit_solution(7598025998244119950)
XLA Ops:
  0.0 0.5 collective-permute-start.3
  0.5 0.1 collective-permute-start.4
  0.5 1.2 %constant_dynamic-slice_fusion.1.refs_0_ = bf16[320,1280]{1,0:T(8,128)(2,1)S(1)} fusion(bf16[320,5120]{1,0:T(8,128)(2,1)} %param.17, s32[]{:T(128)S(6)} %select_n.6), kind=kLoop, calls=%fused_computation.2 | loop fusion | bytes 1638404 | tf_op jit(solution)/shard_map/dynamic_slice | solution.py:429
  1.7 3.0 %collective-permute-start.1 = (bf16[320,1280]{1,0:T(8,128)(2,1)S(1)}, bf16[320,1280]{1,0:T(8,128)(2,1)S(1)}, u32[]{:S(2)}, u32[]{:S(2)}) collective-permute-start(bf16[320,1280]{1,0:T(8,128)(2,1)S(1)} %constant_dynamic-slice_fusion.1.refs_0_), channel_id=1, source_target_pairs={{4,0},{8,4},{12,8},{14,12},{10,14},{6,10},{2,6},{0,2},{5,1},{9,5},... | collective-permute-start | bytes 2457608 | tf_op jit(solution)/shard_map/ppermute | solution.py:408
  4.7 0.2 collective-permute-start
  4.9 1.1 %constant_dynamic-slice_fusion = bf16[256,1280]{1,0:T(8,128)(2,1)S(1)} fusion(bf16[256,2560]{1,0:T(8,128)(2,1)} %own_q_ref.1, s32[]{:T(128)S(6)} %select_n.7), kind=kLoop, calls=%fused_computation.1 | loop fusion | bytes 1310724 | tf_op jit(solution)/shard_map/dynamic_slice | solution.py:434
  6.0 0.1 collective-permute-start.2
  6.1 0.7 copy.13.keys_ref
  6.8 0.6 pad_add_fusion.ids_ref
  7.4 2.5 %collective-permute-done.2.other_q_ref = bf16[256,1280]{1,0:T(8,128)(2,1)} collective-permute-done((bf16[256,1280]{1,0:T(8,128)(2,1)S(1)}, bf16[256,1280]{1,0:T(8,128)(2,1)}, u32[]{:S(2)}, u32[]{:S(2)}) %collective-permute-start.2) | collective-permute-done | bytes 655392 | tf_op jit(solution)/shard_map/ppermute | solution.py:26
  9.8 9.2 %attend.1.refs_9_ = bf16[512,1280]{1,0:T(8,128)(2,1)} custom-call(s32[3]{0:T(128)} %pad_add_fusion.ids_ref, s32[1,2,2]{2,1,0:T(2,128)} %list_ref.9, s32[1,2]{1,0:T(1,128)} %count_ref.9, s32[1,4,3]{2,1,0:T(4,128)} %copy.13.keys_ref, bf16[256,2560]{1,0:T(8,128)(2,1)} %own_q_ref.1, bf16[256,1280]{1,0:T(8,128)(2,1)} %collective-permute-done.2.other_q_ref, ...), custom_call_target="tpu_custom_call" | custom-call | tf_op jit(solution)/shard_map/attend/pallas_call | solution.py:168
  19.0 0.4 collective-permute-start.14
  19.5 2.7 %collective-permute-start.5 = (bf16[512,1280]{1,0:T(8,128)(2,1)}, bf16[512,1280]{1,0:T(8,128)(2,1)S(1)}, u32[]{:S(2)}, u32[]{:S(2)}) collective-permute-start(bf16[512,1280]{1,0:T(8,128)(2,1)} %attend.1.refs_9_), channel_id=1, source_target_pairs={{0,16},{16,0},{1,17},{17,1},{2,18},{18,2},{3,19},{19,3},{4,20},{20... | collective-permute-start | bytes 3932168 | tf_op jit(solution)/shard_map/ppermute | solution.py:26
  22.1 1.1 %collective-permute-done.1.refs_2_ = bf16[320,1280]{1,0:T(8,128)(2,1)S(1)} collective-permute-done((bf16[320,1280]{1,0:T(8,128)(2,1)S(1)}, bf16[320,1280]{1,0:T(8,128)(2,1)S(1)}, u32[]{:S(2)}, u32[]{:S(2)}) %collective-permute-start.1) | collective-permute-done | bytes 819232 | tf_op jit(solution)/shard_map/ppermute | solution.py:408
  23.3 1.5 %collective-permute-done.refs_1_ = bf16[320,1280]{1,0:T(8,128)(2,1)} collective-permute-done((bf16[320,1280]{1,0:T(8,128)(2,1)S(1)}, bf16[320,1280]{1,0:T(8,128)(2,1)}, u32[]{:S(2)}, u32[]{:S(2)}) %collective-permute-start) | collective-permute-done | bytes 819232 | tf_op jit(solution)/shard_map/ppermute | solution.py:408
  24.8 1.6 %collective-permute-start.11 = (bf16[320,896]{1,0:T(8,128)(2,1)S(1)}, bf16[320,896]{1,0:T(8,128)(2,1)S(1)}, u32[]{:S(2)}, u32[]{:S(2)}) collective-permute-start(bf16[320,896]{1,0:T(8,128)(2,1)S(1)} %slice.28), channel_id=1, source_target_pairs={{4,0},{8,4},{12,8},{14,12},{10,14},{6,10},{2,6},{0,2},{5,1},{9,5},... | collective-permute-start | bytes 1720328 | tf_op jit(solution)/shard_map/ppermute | solution.py:408
  26.4 1.1 %slice.26 = bf16[320,896]{1,0:T(8,128)(2,1)S(1)} slice(bf16[320,1280]{1,0:T(8,128)(2,1)} %collective-permute-done.refs_1_), slice={[0:320], [0:896]} | slice | bytes 1146880 | tf_op jit(solution)/shard_map/slice | solution.py:472
  27.5 0.5 collective-permute-start.8
  28.0 10.6 %collective-permute-done.11.refs_4_ = bf16[320,896]{1,0:T(8,128)(2,1)S(1)} collective-permute-done((bf16[320,896]{1,0:T(8,128)(2,1)S(1)}, bf16[320,896]{1,0:T(8,128)(2,1)S(1)}, u32[]{:S(2)}, u32[]{:S(2)}) %collective-permute-start.11) | collective-permute-done | bytes 573472 | tf_op jit(solution)/shard_map/ppermute | solution.py:408
  38.6 1.6 %collective-permute-start.12 = (bf16[320,896]{1,0:T(8,128)(2,1)S(1)}, bf16[320,896]{1,0:T(8,128)(2,1)S(1)}, u32[]{:S(2)}, u32[]{:S(2)}) collective-permute-start(bf16[320,896]{1,0:T(8,128)(2,1)S(1)} %collective-permute-done.11.refs_4_), channel_id=1, source_target_pairs={{4,0},{8,4},{12,8},{14,12},{10,14},{6,10},{2,6},{0,2},{5,1},{9,5},... | collective-permute-start | bytes 1720328 | tf_op jit(solution)/shard_map/ppermute | solution.py:408
  40.2 0.9 collective-permute-done.8.refs_3_
  41.1 0.4 collective-permute-start.9
  41.5 10.0 %collective-permute-done.12.refs_6_ = bf16[320,896]{1,0:T(8,128)(2,1)S(1)} collective-permute-done((bf16[320,896]{1,0:T(8,128)(2,1)S(1)}, bf16[320,896]{1,0:T(8,128)(2,1)S(1)}, u32[]{:S(2)}, u32[]{:S(2)}) %collective-permute-start.12) | collective-permute-done | bytes 573472 | tf_op jit(solution)/shard_map/ppermute | solution.py:408
  51.5 2.2 %collective-permute-done.9.refs_5_ = bf16[320,896]{1,0:T(8,128)(2,1)S(1)} collective-permute-done((bf16[320,896]{1,0:T(8,128)(2,1)S(1)}, bf16[320,896]{1,0:T(8,128)(2,1)S(1)}, u32[]{:S(2)}, u32[]{:S(2)}) %collective-permute-start.9) | collective-permute-done | bytes 573472 | tf_op jit(solution)/shard_map/ppermute | solution.py:408
  53.7 0.0 collective-permute-done.14.refs_10_
  53.7 0.0 collective-permute-done.5.refs_7_
  53.7 0.0 collective-permute-start.15
  53.7 1.6 %collective-permute-start.13 = (bf16[160,896]{1,0:T(8,128)(2,1)S(1)}, bf16[160,896]{1,0:T(8,128)(2,1)S(1)}, u32[]{:S(2)}, u32[]{:S(2)}) collective-permute-start(bf16[160,896]{1,0:T(8,128)(2,1)S(1)} %slice.35), channel_id=1, source_target_pairs={{4,0},{8,4},{12,8},{14,12},{10,14},{6,10},{2,6},{0,2},{5,1},{9,5},... | collective-permute-start | bytes 860168 | tf_op jit(solution)/shard_map/ppermute | solution.py:408
  55.4 0.5 collective-permute-start.10
  55.9 1.0 slice.32
  56.9 0.5 collective-permute-start.6
  57.4 1.6 %collective-permute-start.7 = (bf16[320,384]{1,0:T(8,128)(2,1)S(1)}, bf16[320,384]{1,0:T(8,128)(2,1)S(1)}, u32[]{:S(2)}, u32[]{:S(2)}) collective-permute-start(bf16[320,384]{1,0:T(8,128)(2,1)S(1)} %slice.33), channel_id=1, source_target_pairs={{4,0},{8,4},{12,8},{14,12},{10,14},{6,10},{2,6},{0,2},{5,1},{9,5},... | collective-permute-start | bytes 737288 | tf_op jit(solution)/shard_map/ppermute | solution.py:408
  59.0 0.0 collective-permute-done.15.refs_8_
  59.0 5.0 %project_most.4 = (f32[512,896]{1,0:T(8,128)S(1)}, bf16[512,384]{1,0:T(8,128)(2,1)S(1)}) custom-call(s32[3]{0:T(128)S(1)} %copy-done.3, bf16[320,1280]{1,0:T(8,128)(2,1)S(1)} %constant_dynamic-slice_fusion.1.refs_0_, bf16[320,1280]{1,0:T(8,128)(2,1)} %collective-permute-done.refs_1_, bf16[320,1280]{1,0:T(8,128)(2,1)S(1)} %collective-permute-done.1.refs_2_, ...), custom_call_target="tpu_custom_call" | custom-call | flops 2348810240 | tf_op jit(solution)/shard_map/project_most/pallas_call | solution.py:254
  64.0 0.0 copy-start.1
  64.0 0.0 collective-permute-done.13.bottom_ref.refs_8_
  64.0 1.1 %collective-permute-done.10.top_ref.refs_7_ = bf16[160,896]{1,0:T(8,128)(2,1)S(1)} collective-permute-done((bf16[160,896]{1,0:T(8,128)(2,1)S(1)}, bf16[160,896]{1,0:T(8,128)(2,1)S(1)}, u32[]{:S(2)}, u32[]{:S(2)}) %collective-permute-start.10) | collective-permute-done | bytes 286752 | tf_op jit(solution)/shard_map/ppermute | solution.py:408
  65.1 1.3 %project_last.2 = bf16[512,896]{1,0:T(8,128)(2,1)S(1)} custom-call(s32[3]{0:T(128)S(1)} %copy-done.3, bf16[160,896]{1,0:T(8,128)(2,1)S(1)} %collective-permute-done.10.top_ref.refs_7_, bf16[160,896]{1,0:T(8,128)(2,1)S(1)} %collective-permute-done.13.bottom_ref.refs_8_, f32[512,896]{1,0:T(8,128)S(1)} %get-tuple-element.27.sums_ref, ...), custom_call_target="tpu_custom_call" | custom-call | tf_op jit(solution)/shard_map/project_last/pallas_call | solution.py:292
  66.4 1.6 %collective-permute-start.23 = (bf16[512,896]{1,0:T(8,128)(2,1)S(1)}, bf16[512,896]{1,0:T(8,128)(2,1)S(1)}, u32[]{:S(2)}, u32[]{:S(2)}) collective-permute-start(bf16[512,896]{1,0:T(8,128)(2,1)S(1)} %project_last.2), channel_id=1, source_target_pairs={{0,16},{16,0},{1,17},{17,1},{2,18},{18,2},{3,19},{19,3},{4,20},{20... | collective-permute-start | bytes 2752520 | tf_op jit(solution)/shard_map/ppermute | solution.py:26
  68.0 1.6 %collective-permute-done.6.refs_3_ = bf16[320,384]{1,0:T(8,128)(2,1)S(1)} collective-permute-done((bf16[320,384]{1,0:T(8,128)(2,1)S(1)}, bf16[320,384]{1,0:T(8,128)(2,1)S(1)}, u32[]{:S(2)}, u32[]{:S(2)}) %collective-permute-start.6) | collective-permute-done | bytes 245792 | tf_op jit(solution)/shard_map/ppermute | solution.py:408
  69.7 0.5 collective-permute-start.16
  70.1 1.6 %collective-permute-start.17 = (bf16[320,384]{1,0:T(8,128)(2,1)S(1)}, bf16[320,384]{1,0:T(8,128)(2,1)S(1)}, u32[]{:S(2)}, u32[]{:S(2)}) collective-permute-start(bf16[320,384]{1,0:T(8,128)(2,1)S(1)} %collective-permute-done.7.refs_4_), channel_id=1, source_target_pairs={{4,0},{8,4},{12,8},{14,12},{10,14},{6,10},{2,6},{0,2},{5,1},{9,5},... | collective-permute-start | bytes 737288 | tf_op jit(solution)/shard_map/ppermute | solution.py:408
  71.7 5.0 %project_most.5.refs_0_ = bf16[512,896]{1,0:T(8,128)(2,1)S(1)} custom-call(s32[3]{0:T(128)S(1)} %copy-done.3, bf16[320,1280]{1,0:T(8,128)(2,1)S(1)} %constant_dynamic-slice_fusion.1.refs_0_, bf16[320,1280]{1,0:T(8,128)(2,1)} %collective-permute-done.refs_1_, bf16[320,1280]{1,0:T(8,128)(2,1)S(1)} %collective-permute-done.1.refs_2_, ...), custom_call_target="tpu_custom_call" | custom-call | flops 22000001024 | tf_op jit(solution)/shard_map/project_most/pallas_call | solution.py:254
  76.7 0.2 collective-permute-done.16.refs_5_
  76.9 0.2 collective-permute-done.17.refs_6_
  77.1 1.6 %collective-permute-start.19 = (bf16[160,384]{1,0:T(8,128)(2,1)S(1)}, bf16[160,384]{1,0:T(8,128)(2,1)S(1)}, u32[]{:S(2)}, u32[]{:S(2)}) collective-permute-start(bf16[160,384]{1,0:T(8,128)(2,1)S(1)} %slice.31), channel_id=1, source_target_pairs={{4,0},{8,4},{12,8},{14,12},{10,14},{6,10},{2,6},{0,2},{5,1},{9,5},... | collective-permute-start | bytes 368648 | tf_op jit(solution)/shard_map/ppermute | solution.py:408
  78.8 0.4 collective-permute-start.18
  79.2 0.0 collective-permute-start.22
  79.2 4.1 %project_most.6 = (f32[512,384]{1,0:T(8,128)S(1)}, bf16[512,384]{1,0:T(8,128)(2,1)S(1)}) custom-call(s32[3]{0:T(128)S(1)} %copy-done.3, bf16[320,1280]{1,0:T(8,128)(2,1)S(1)} %constant_dynamic-slice_fusion.1.refs_0_, bf16[320,1280]{1,0:T(8,128)(2,1)} %collective-permute-done.refs_1_, bf16[320,1280]{1,0:T(8,128)(2,1)S(1)} %collective-permute-done.1.refs_2_, ...), custom_call_target="tpu_custom_call" | custom-call | flops 1006632960 | tf_op jit(solution)/shard_map/project_most/pallas_call | solution.py:254
  83.3 0.3 collective-permute-done.18.top_ref.refs_7_
  83.6 1.0 project_last.3
  84.6 0.0 copy-start
  84.6 0.0 copy-start.2
  84.6 0.0 copy-start.4
  84.7 0.0 copy-start.5
  84.7 1.6 %collective-permute-start.20 = (bf16[512,384]{1,0:T(8,128)(2,1)S(1)}, bf16[512,384]{1,0:T(8,128)(2,1)S(1)}, u32[]{:S(2)}, u32[]{:S(2)}) collective-permute-start(bf16[512,384]{1,0:T(8,128)(2,1)S(1)} %project_last.3), channel_id=1, source_target_pairs={{0,16},{16,0},{1,17},{17,1},{2,18},{18,2},{3,19},{19,3},{4,20},{20... | collective-permute-start | bytes 1179656 | tf_op jit(solution)/shard_map/ppermute | solution.py:26
  86.3 1.2 %collective-permute-done.23.refs_2_ = bf16[512,896]{1,0:T(8,128)(2,1)S(1)} collective-permute-done((bf16[512,896]{1,0:T(8,128)(2,1)S(1)}, bf16[512,896]{1,0:T(8,128)(2,1)S(1)}, u32[]{:S(2)}, u32[]{:S(2)}) %collective-permute-start.23) | collective-permute-done | bytes 917536 | tf_op jit(solution)/shard_map/ppermute | solution.py:26
  87.4 4.4 %project_most.7.refs_0_ = bf16[512,384]{1,0:T(8,128)(2,1)S(1)} custom-call(s32[3]{0:T(128)S(1)} %copy-done.3, bf16[320,1280]{1,0:T(8,128)(2,1)S(1)} %constant_dynamic-slice_fusion.1.refs_0_, bf16[320,1280]{1,0:T(8,128)(2,1)} %collective-permute-done.refs_1_, bf16[320,1280]{1,0:T(8,128)(2,1)S(1)} %collective-permute-done.1.refs_2_, ...), custom_call_target="tpu_custom_call" | custom-call | flops 22000001024 | tf_op jit(solution)/shard_map/project_most/pallas_call | solution.py:254
  91.8 0.6 collective-permute-start.21
  92.4 3.2 %finish.4.refs_2_ = bf16[256,5120]{1,0:T(8,128)(2,1)} custom-call(s32[3]{0:T(128)S(1)} %copy-done.3, s32[1,2,2]{2,1,0:T(2,128)S(1)} %copy-done.4, s32[1,2]{1,0:T(1,128)S(1)} %copy-done.5, f32[1,5120]{1,0:T(1,128)S(1)} %bitcast.4, bf16[256,5120]{1,0:T(8,128)(2,1)S(1)} %copy-done, bf16[512,896]{1,0:T(8,128)(2,1)S(1)} %project_most.5.refs_0_, ...), custom_call_target="tpu_custom_call" | custom-call | flops 6000000000 | tf_op jit(solution)/shard_map/finish/pallas_call | solution.py:378
  95.7 2.0 %finish.5.refs_1_ = bf16[256,5120]{1,0:T(8,128)(2,1)} custom-call(s32[3]{0:T(128)S(1)} %copy-done.3, s32[1,2,2]{2,1,0:T(2,128)S(1)} %copy-done.4, s32[1,2]{1,0:T(1,128)S(1)} %copy-done.5, f32[1,5120]{1,0:T(1,128)S(1)} %bitcast.5, bf16[256,5120]{1,0:T(8,128)(2,1)S(1)} %copy-done, ...), custom_call_target="tpu_custom_call", output_to_operand_aliasing={{}: (7, {})} | custom-call | flops 3000000000 | tf_op jit(solution)/shard_map/finish/pallas_call | solution.py:378
  97.7 0.4 collective-permute-start.25
  98.1 1.6 %finish.6.refs_1_ = bf16[256,5120]{1,0:T(8,128)(2,1)} custom-call(s32[3]{0:T(128)S(1)} %copy-done.3, s32[1,2,2]{2,1,0:T(2,128)S(1)} %copy-done.4, s32[1,2]{1,0:T(1,128)S(1)} %copy-done.5, f32[1,5120]{1,0:T(1,128)S(1)} %bitcast.6, bf16[256,5120]{1,0:T(8,128)(2,1)S(1)} %copy-done, ...), custom_call_target="tpu_custom_call", output_to_operand_aliasing={{}: (6, {})} | custom-call | flops 1500000000 | tf_op jit(solution)/shard_map/finish/pallas_call | solution.py:378
  99.7 1.6 %finish.7 = bf16[256,5120]{1,0:T(8,128)(2,1)} custom-call(s32[3]{0:T(128)S(1)} %copy-done.3, s32[1,2,2]{2,1,0:T(2,128)S(1)} %copy-done.4, s32[1,2]{1,0:T(1,128)S(1)} %copy-done.5, f32[1,5120]{1,0:T(1,128)S(1)} %bitcast.7, bf16[256,5120]{1,0:T(8,128)(2,1)S(1)} %copy-done, ...), custom_call_target="tpu_custom_call", output_to_operand_aliasing={{}: (6, {})} | custom-call | flops 1500000000 | tf_op jit(solution)/shard_map/finish/pallas_call | solution.py:378
  (25 shorter events, 0.2 us)
Async XLA Ops:
  0.0 6.1 %copy-start.6 = (s32[1,4,3]{1,0,2:T(1,128)S(1)}, s32[1,4,3]{1,0,2:T(1,128)}, u32[]{:S(2)}) copy-start(s32[1,4,3]{1,0,2:T(1,128)} %param.16) | copy-start | bytes 148
  0.0 9.8 %collective-permute-start.3 = (bf16[256,2,2560]{2,1,0:T(2,128)(2,1)}, bf16[256,2,2560]{2,1,0:T(2,128)(2,1)}, u32[]{:S(2)}, u32[]{:S(2)}) collective-permute-start(bf16[256,2,2560]{2,1,0:T(2,128)(2,1)} %own_fresh_ref.1), channel_id=1, source_target_pairs={{0,1},{1,0},{2,3},{3,2},{4,5},{5,4},{6,7},{7,6},{8,9},{9,8},{10,11... | collective-permute-start | bytes 7864328 | tf_op jit(solution)/shard_map/ppermute | solution.py:26
  0.5 9.4 %collective-permute-start.4 = (bf16[256,2,2560]{2,1,0:T(2,128)(2,1)}, bf16[256,2,2560]{2,1,0:T(2,128)(2,1)}, u32[]{:S(2)}, u32[]{:S(2)}) collective-permute-start(bf16[256,2,2560]{2,1,0:T(2,128)(2,1)} %own_cache_ref.1), channel_id=1, source_target_pairs={{0,1},{1,0},{2,3},{3,2},{4,5},{5,4},{6,7},{7,6},{8,9},{9,8},{10,11... | collective-permute-start | bytes 7864328 | tf_op jit(solution)/shard_map/ppermute | solution.py:26
  1.7 21.5 %collective-permute-start.1 = (bf16[320,1280]{1,0:T(8,128)(2,1)S(1)}, bf16[320,1280]{1,0:T(8,128)(2,1)S(1)}, u32[]{:S(2)}, u32[]{:S(2)}) collective-permute-start(bf16[320,1280]{1,0:T(8,128)(2,1)S(1)} %constant_dynamic-slice_fusion.1.refs_0_), channel_id=1, source_target_pairs={{4,0},{8,4},{12,8},{14,12},{10,14},{6,10},{2,6},{0,2},{5,1},{9,5},... | collective-permute-start | bytes 2457608 | tf_op jit(solution)/shard_map/ppermute | solution.py:408
  4.7 20.0 %collective-permute-start = (bf16[320,1280]{1,0:T(8,128)(2,1)S(1)}, bf16[320,1280]{1,0:T(8,128)(2,1)}, u32[]{:S(2)}, u32[]{:S(2)}) collective-permute-start(bf16[320,1280]{1,0:T(8,128)(2,1)S(1)} %constant_dynamic-slice_fusion.1.refs_0_), channel_id=1, source_target_pairs={{0,4},{4,8},{8,12},{12,14},{14,10},{10,6},{6,2},{2,0},{1,5},{5,9},... | collective-permute-start | bytes 2457608 | tf_op jit(solution)/shard_map/ppermute | solution.py:408
  6.0 3.8 %collective-permute-start.2 = (bf16[256,1280]{1,0:T(8,128)(2,1)S(1)}, bf16[256,1280]{1,0:T(8,128)(2,1)}, u32[]{:S(2)}, u32[]{:S(2)}) collective-permute-start(bf16[256,1280]{1,0:T(8,128)(2,1)S(1)} %constant_dynamic-slice_fusion), channel_id=1, source_target_pairs={{0,1},{1,0},{2,3},{3,2},{4,5},{5,4},{6,7},{7,6},{8,9},{9,8},{10,11... | collective-permute-start | bytes 1966088 | tf_op jit(solution)/shard_map/ppermute | solution.py:26
  19.0 39.9 %copy-start.3 = (s32[3]{0:T(128)S(1)}, s32[3]{0:T(128)}, u32[]{:S(2)}) copy-start(s32[3]{0:T(128)} %pad_add_fusion.ids_ref) | copy-start | bytes 40
  19.0 34.6 %collective-permute-start.14 = (bf16[512,1280]{1,0:T(8,128)(2,1)}, bf16[512,1280]{1,0:T(8,128)(2,1)S(1)}, u32[]{:S(2)}, u32[]{:S(2)}) collective-permute-start(bf16[512,1280]{1,0:T(8,128)(2,1)} %attend.1.refs_9_), channel_id=1, source_target_pairs={{0,1},{1,0},{2,3},{3,2},{4,5},{5,4},{6,7},{7,6},{8,9},{9,8},{10,11... | collective-permute-start | bytes 3932168 | tf_op jit(solution)/shard_map/ppermute | solution.py:26
  19.5 34.2 %collective-permute-start.5 = (bf16[512,1280]{1,0:T(8,128)(2,1)}, bf16[512,1280]{1,0:T(8,128)(2,1)S(1)}, u32[]{:S(2)}, u32[]{:S(2)}) collective-permute-start(bf16[512,1280]{1,0:T(8,128)(2,1)} %attend.1.refs_9_), channel_id=1, source_target_pairs={{0,16},{16,0},{1,17},{17,1},{2,18},{18,2},{3,19},{19,3},{4,20},{20... | collective-permute-start | bytes 3932168 | tf_op jit(solution)/shard_map/ppermute | solution.py:26
  24.8 13.8 %collective-permute-start.11 = (bf16[320,896]{1,0:T(8,128)(2,1)S(1)}, bf16[320,896]{1,0:T(8,128)(2,1)S(1)}, u32[]{:S(2)}, u32[]{:S(2)}) collective-permute-start(bf16[320,896]{1,0:T(8,128)(2,1)S(1)} %slice.28), channel_id=1, source_target_pairs={{4,0},{8,4},{12,8},{14,12},{10,14},{6,10},{2,6},{0,2},{5,1},{9,5},... | collective-permute-start | bytes 1720328 | tf_op jit(solution)/shard_map/ppermute | solution.py:408
  27.5 13.6 %collective-permute-start.8 = (bf16[320,896]{1,0:T(8,128)(2,1)S(1)}, bf16[320,896]{1,0:T(8,128)(2,1)S(1)}, u32[]{:S(2)}, u32[]{:S(2)}) collective-permute-start(bf16[320,896]{1,0:T(8,128)(2,1)S(1)} %slice.26), channel_id=1, source_target_pairs={{0,4},{4,8},{8,12},{12,14},{14,10},{10,6},{6,2},{2,0},{1,5},{5,9},... | collective-permute-start | bytes 1720328 | tf_op jit(solution)/shard_map/ppermute | solution.py:408
  38.6 12.9 %collective-permute-start.12 = (bf16[320,896]{1,0:T(8,128)(2,1)S(1)}, bf16[320,896]{1,0:T(8,128)(2,1)S(1)}, u32[]{:S(2)}, u32[]{:S(2)}) collective-permute-start(bf16[320,896]{1,0:T(8,128)(2,1)S(1)} %collective-permute-done.11.refs_4_), channel_id=1, source_target_pairs={{4,0},{8,4},{12,8},{14,12},{10,14},{6,10},{2,6},{0,2},{5,1},{9,5},... | collective-permute-start | bytes 1720328 | tf_op jit(solution)/shard_map/ppermute | solution.py:408
  41.1 12.6 %collective-permute-start.9 = (bf16[320,896]{1,0:T(8,128)(2,1)S(1)}, bf16[320,896]{1,0:T(8,128)(2,1)S(1)}, u32[]{:S(2)}, u32[]{:S(2)}) collective-permute-start(bf16[320,896]{1,0:T(8,128)(2,1)S(1)} %collective-permute-done.8.refs_3_), channel_id=1, source_target_pairs={{0,4},{4,8},{8,12},{12,14},{14,10},{10,6},{6,2},{2,0},{1,5},{5,9},... | collective-permute-start | bytes 1720328 | tf_op jit(solution)/shard_map/ppermute | solution.py:408
  53.7 5.3 %collective-permute-start.15 = (bf16[512,1280]{1,0:T(8,128)(2,1)S(1)}, bf16[512,1280]{1,0:T(8,128)(2,1)S(1)}, u32[]{:S(2)}, u32[]{:S(2)}) collective-permute-start(bf16[512,1280]{1,0:T(8,128)(2,1)S(1)} %collective-permute-done.5.refs_7_), channel_id=1, source_target_pairs={{0,1},{1,0},{2,3},{3,2},{4,5},{5,4},{6,7},{7,6},{8,9},{9,8},{10,11... | collective-permute-start | bytes 3932168 | tf_op jit(solution)/shard_map/ppermute | solution.py:26
  53.7 10.3 %collective-permute-start.13 = (bf16[160,896]{1,0:T(8,128)(2,1)S(1)}, bf16[160,896]{1,0:T(8,128)(2,1)S(1)}, u32[]{:S(2)}, u32[]{:S(2)}) collective-permute-start(bf16[160,896]{1,0:T(8,128)(2,1)S(1)} %slice.35), channel_id=1, source_target_pairs={{4,0},{8,4},{12,8},{14,12},{10,14},{6,10},{2,6},{0,2},{5,1},{9,5},... | collective-permute-start | bytes 860168 | tf_op jit(solution)/shard_map/ppermute | solution.py:408
  55.4 9.7 %collective-permute-start.10 = (bf16[160,896]{1,0:T(8,128)(2,1)S(1)}, bf16[160,896]{1,0:T(8,128)(2,1)S(1)}, u32[]{:S(2)}, u32[]{:S(2)}) collective-permute-start(bf16[160,896]{1,0:T(8,128)(2,1)S(1)} %slice.34), channel_id=1, source_target_pairs={{0,4},{4,8},{8,12},{12,14},{14,10},{10,6},{6,2},{2,0},{1,5},{5,9},... | collective-permute-start | bytes 860168 | tf_op jit(solution)/shard_map/ppermute | solution.py:408
  56.9 12.8 %collective-permute-start.6 = (bf16[320,384]{1,0:T(8,128)(2,1)S(1)}, bf16[320,384]{1,0:T(8,128)(2,1)S(1)}, u32[]{:S(2)}, u32[]{:S(2)}) collective-permute-start(bf16[320,384]{1,0:T(8,128)(2,1)S(1)} %slice.32), channel_id=1, source_target_pairs={{0,4},{4,8},{8,12},{12,14},{14,10},{10,6},{6,2},{2,0},{1,5},{5,9},... | collective-permute-start | bytes 737288 | tf_op jit(solution)/shard_map/ppermute | solution.py:408
  57.4 12.3 %collective-permute-start.7 = (bf16[320,384]{1,0:T(8,128)(2,1)S(1)}, bf16[320,384]{1,0:T(8,128)(2,1)S(1)}, u32[]{:S(2)}, u32[]{:S(2)}) collective-permute-start(bf16[320,384]{1,0:T(8,128)(2,1)S(1)} %slice.33), channel_id=1, source_target_pairs={{4,0},{8,4},{12,8},{14,12},{10,14},{6,10},{2,6},{0,2},{5,1},{9,5},... | collective-permute-start | bytes 737288 | tf_op jit(solution)/shard_map/ppermute | solution.py:408
  64.0 7.7 %copy-start.1 = (bf16[512,1280]{1,0:T(8,128)(2,1)S(1)}, bf16[512,1280]{1,0:T(8,128)(2,1)}, u32[]{:S(2)}) copy-start(bf16[512,1280]{1,0:T(8,128)(2,1)} %attend.1.refs_9_) | copy-start | bytes 3932164
  66.4 21.0 %collective-permute-start.23 = (bf16[512,896]{1,0:T(8,128)(2,1)S(1)}, bf16[512,896]{1,0:T(8,128)(2,1)S(1)}, u32[]{:S(2)}, u32[]{:S(2)}) collective-permute-start(bf16[512,896]{1,0:T(8,128)(2,1)S(1)} %project_last.2), channel_id=1, source_target_pairs={{0,16},{16,0},{1,17},{17,1},{2,18},{18,2},{3,19},{19,3},{4,20},{20... | collective-permute-start | bytes 2752520 | tf_op jit(solution)/shard_map/ppermute | solution.py:26
  69.7 7.3 %collective-permute-start.16 = (bf16[320,384]{1,0:T(8,128)(2,1)S(1)}, bf16[320,384]{1,0:T(8,128)(2,1)S(1)}, u32[]{:S(2)}, u32[]{:S(2)}) collective-permute-start(bf16[320,384]{1,0:T(8,128)(2,1)S(1)} %collective-permute-done.6.refs_3_), channel_id=1, source_target_pairs={{0,4},{4,8},{8,12},{12,14},{14,10},{10,6},{6,2},{2,0},{1,5},{5,9},... | collective-permute-start | bytes 737288 | tf_op jit(solution)/shard_map/ppermute | solution.py:408
  70.1 7.0 %collective-permute-start.17 = (bf16[320,384]{1,0:T(8,128)(2,1)S(1)}, bf16[320,384]{1,0:T(8,128)(2,1)S(1)}, u32[]{:S(2)}, u32[]{:S(2)}) collective-permute-start(bf16[320,384]{1,0:T(8,128)(2,1)S(1)} %collective-permute-done.7.refs_4_), channel_id=1, source_target_pairs={{4,0},{8,4},{12,8},{14,12},{10,14},{6,10},{2,6},{0,2},{5,1},{9,5},... | collective-permute-start | bytes 737288 | tf_op jit(solution)/shard_map/ppermute | solution.py:408
  77.1 6.2 %collective-permute-start.19 = (bf16[160,384]{1,0:T(8,128)(2,1)S(1)}, bf16[160,384]{1,0:T(8,128)(2,1)S(1)}, u32[]{:S(2)}, u32[]{:S(2)}) collective-permute-start(bf16[160,384]{1,0:T(8,128)(2,1)S(1)} %slice.31), channel_id=1, source_target_pairs={{4,0},{8,4},{12,8},{14,12},{10,14},{6,10},{2,6},{0,2},{5,1},{9,5},... | collective-permute-start | bytes 368648 | tf_op jit(solution)/shard_map/ppermute | solution.py:408
  78.8 4.9 %collective-permute-start.18 = (bf16[160,384]{1,0:T(8,128)(2,1)S(1)}, bf16[160,384]{1,0:T(8,128)(2,1)S(1)}, u32[]{:S(2)}, u32[]{:S(2)}) collective-permute-start(bf16[160,384]{1,0:T(8,128)(2,1)S(1)} %slice.30), channel_id=1, source_target_pairs={{0,4},{4,8},{8,12},{12,14},{14,10},{10,6},{6,2},{2,0},{1,5},{5,9},... | collective-permute-start | bytes 368648 | tf_op jit(solution)/shard_map/ppermute | solution.py:408
  79.2 13.2 %collective-permute-start.22 = (bf16[512,896]{1,0:T(8,128)(2,1)S(1)}, bf16[512,896]{1,0:T(8,128)(2,1)S(1)}, u32[]{:S(2)}, u32[]{:S(2)}) collective-permute-start(bf16[512,896]{1,0:T(8,128)(2,1)S(1)} %project_most.5.refs_0_), channel_id=1, source_target_pairs={{0,1},{1,0},{2,3},{3,2},{4,5},{5,4},{6,7},{7,6},{8,9},{9,8},{10,11... | collective-permute-start | bytes 2752520 | tf_op jit(solution)/shard_map/ppermute | solution.py:26
  84.6 7.8 %copy-start = (bf16[256,5120]{1,0:T(8,128)(2,1)S(1)}, bf16[256,5120]{1,0:T(8,128)(2,1)}, u32[]{:S(2)}) copy-start(bf16[256,5120]{1,0:T(8,128)(2,1)} %input_ref.7) | copy-start | bytes 7864324
  84.6 7.8 %copy-start.2 = (f32[5120]{0:T(1024)S(1)}, f32[5120]{0:T(1024)}, u32[]{:S(2)}) copy-start(f32[5120]{0:T(1024)} %param.10) | copy-start | bytes 61444
  84.6 7.8 %copy-start.4 = (s32[1,2,2]{2,1,0:T(2,128)S(1)}, s32[1,2,2]{2,1,0:T(2,128)}, u32[]{:S(2)}) copy-start(s32[1,2,2]{2,1,0:T(2,128)} %list_ref.9) | copy-start | bytes 52
  84.7 7.8 %copy-start.5 = (s32[1,2]{1,0:T(1,128)S(1)}, s32[1,2]{1,0:T(1,128)}, u32[]{:S(2)}) copy-start(s32[1,2]{1,0:T(1,128)} %count_ref.9) | copy-start | bytes 28
  84.7 13.0 %collective-permute-start.20 = (bf16[512,384]{1,0:T(8,128)(2,1)S(1)}, bf16[512,384]{1,0:T(8,128)(2,1)S(1)}, u32[]{:S(2)}, u32[]{:S(2)}) collective-permute-start(bf16[512,384]{1,0:T(8,128)(2,1)S(1)} %project_last.3), channel_id=1, source_target_pairs={{0,16},{16,0},{1,17},{17,1},{2,18},{18,2},{3,19},{19,3},{4,20},{20... | collective-permute-start | bytes 1179656 | tf_op jit(solution)/shard_map/ppermute | solution.py:26
  87.4 5.0 %collective-permute-start.24 = (bf16[512,896]{1,0:T(8,128)(2,1)S(1)}, bf16[512,896]{1,0:T(8,128)(2,1)S(1)}, u32[]{:S(2)}, u32[]{:S(2)}) collective-permute-start(bf16[512,896]{1,0:T(8,128)(2,1)S(1)} %collective-permute-done.23.refs_2_), channel_id=1, source_target_pairs={{0,1},{1,0},{2,3},{3,2},{4,5},{5,4},{6,7},{7,6},{8,9},{9,8},{10,11... | collective-permute-start | bytes 2752520 | tf_op jit(solution)/shard_map/ppermute | solution.py:26
  91.8 3.9 %collective-permute-start.21 = (bf16[512,384]{1,0:T(8,128)(2,1)S(1)}, bf16[512,384]{1,0:T(8,128)(2,1)S(1)}, u32[]{:S(2)}, u32[]{:S(2)}) collective-permute-start(bf16[512,384]{1,0:T(8,128)(2,1)S(1)} %project_most.7.refs_0_), channel_id=1, source_target_pairs={{0,1},{1,0},{2,3},{3,2},{4,5},{5,4},{6,7},{7,6},{8,9},{9,8},{10,11... | collective-permute-start | bytes 1179656 | tf_op jit(solution)/shard_map/ppermute | solution.py:26
  97.7 2.0 %collective-permute-start.25 = (bf16[512,384]{1,0:T(8,128)(2,1)S(1)}, bf16[512,384]{1,0:T(8,128)(2,1)S(1)}, u32[]{:S(2)}, u32[]{:S(2)}) collective-permute-start(bf16[512,384]{1,0:T(8,128)(2,1)S(1)} %collective-permute-done.20.refs_0_), channel_id=1, source_target_pairs={{0,1},{1,0},{2,3},{3,2},{4,5},{5,4},{6,7},{7,6},{8,9},{9,8},{10,11... | collective-permute-start | bytes 1179656 | tf_op jit(solution)/shard_map/ppermute | solution.py:26

commit v6 on v5

--- a/solution.py
+++ b/solution.py
@@ -489,11 +489,13 @@
     second_4 = last_step(all_after(second_3, kept))
     kept_near = exchanged(kept, "blk")
     pieces, rest = [columns, *both_1, *second_2, *second_3], quarter - first
-    far_sums, far_cut = most(pieces, first, rest, far_rows, far_near_rows)
+    far_sums, own_sums, far_cut, own_cut = most(
+        pieces, first, rest, far_rows, far_near_rows, own_rows, near_rows
+    )
     away = last_projected(ids, positions, second_4, far_sums, far_cut, 0)
     last_back = exchanged(away, "groups")
-    (rest_kept,) = most(
-        [*pieces, *second_4], first, rest, after(own_rows, away), near_rows
+    rest_kept = last_projected(
+        ids, positions, second_4, after(own_sums, away), own_cut, 22_000_000_000
     )
     back = after(back, *second_4)
     result = finish(

time: 102 us -> 101 us (level)
    pallas_call x4 -> x3, Pallas kernels: 18.4 us -> 16 us  [most_projected(): pl.pallas_call(functools.partial(most_kernel, shifts, starts, pairs, posi...]
    pallas_call x2 -> x3, Pallas kernels: 2.31 us -> 3.29 us  [last_projected(): pl.pallas_call(functools.partial(last_kernel, positions), out_shape=[jax....]
  transfers between devices with their start and end apart: 26 -> 26, of which waited for: 13 -> 14; matrix products, arithmetic and copies ran while one was open for 6% -> 6% of each run, Pallas kernels for 36% -> 35%
where the time goes in v6:
time: 101 us; the launch traced here: 100 us
  Pallas kernels  37.3 us (37%)
  waiting for transfers between devices  33.8 us (33%)
  starting transfers between devices  23.1 us (23%)
  local copies, waits for them, and re-layouts  5.26 us (5%)
    ppermute x7, waiting for transfers between devices, step(): lax.ppermute(held[1], 'fsdp', behind)  21.9 us
    pallas_call x3, Pallas kernels, most_projected(): pl.pallas_call(functools.partial(most_kernel, shifts, starts, pairs, posi...  16 us
    ppermute x7, starting transfers between devices, step(): lax.ppermute(held[1], 'fsdp', behind)  12.6 us
    pallas_call x1, Pallas kernels, attended_heads(): pl.pallas_call(attend_kernel, out_shape=jax.ShapeDtypeStruct((2 * tokens,...  9.19 us
    pallas_call x4, Pallas kernels, finished(): pl.pallas_call(functools.partial(finish_kernel, places), in_specs=in_spec...  8.8 us
    ppermute x12, starting transfers between devices, exchanged(): return lax.ppermute(block, axis, [(0, 1), (1, 0)])  7.49 us
    ppermute x7, waiting for transfers between devices, step(): lax.ppermute(held[0], 'fsdp', ahead)  7.46 us
    ppermute x12, waiting for transfers between devices, exchanged(): return lax.ppermute(block, axis, [(0, 1), (1, 0)])  4.5 us
  transfers between devices with their start and end apart: 26, of which 14 were waited for; matrix products, arithmetic and copies ran while one was open for 6% of the time, Pallas kernels for 35%

profile of v6, /device:TPU:0, one launch (start us, length us, event | category | flops | bytes accessed | tf_op | source)
XLA Modules:
  0.0 100.5 jit_solution(16185435138805684809)
XLA Ops:
  0.0 0.5 collective-permute-start.3
  0.5 0.1 collective-permute-start.4
  0.5 1.2 %constant_dynamic-slice_fusion.1.refs_0_ = bf16[320,1280]{1,0:T(8,128)(2,1)S(1)} fusion(bf16[320,5120]{1,0:T(8,128)(2,1)} %param.17, s32[]{:T(128)S(6)} %select_n.6), kind=kLoop, calls=%fused_computation.2 | loop fusion | bytes 1638404 | tf_op jit(solution)/shard_map/dynamic_slice | solution.py:429
  1.7 3.0 %collective-permute-start.1 = (bf16[320,1280]{1,0:T(8,128)(2,1)S(1)}, bf16[320,1280]{1,0:T(8,128)(2,1)S(1)}, u32[]{:S(2)}, u32[]{:S(2)}) collective-permute-start(bf16[320,1280]{1,0:T(8,128)(2,1)S(1)} %constant_dynamic-slice_fusion.1.refs_0_), channel_id=1, source_target_pairs={{4,0},{8,4},{12,8},{14,12},{10,14},{6,10},{2,6},{0,2},{5,1},{9,5},... | collective-permute-start | bytes 2457608 | tf_op jit(solution)/shard_map/ppermute | solution.py:408
  4.7 0.2 collective-permute-start
  4.9 1.1 %constant_dynamic-slice_fusion = bf16[256,1280]{1,0:T(8,128)(2,1)S(1)} fusion(bf16[256,2560]{1,0:T(8,128)(2,1)} %own_q_ref.1, s32[]{:T(128)S(6)} %select_n.7), kind=kLoop, calls=%fused_computation.1 | loop fusion | bytes 1310724 | tf_op jit(solution)/shard_map/dynamic_slice | solution.py:434
  6.0 0.1 collective-permute-start.2
  6.1 0.7 copy.13.keys_ref
  6.8 0.6 pad_add_fusion.ids_ref
  7.4 2.5 %collective-permute-done.2.other_q_ref = bf16[256,1280]{1,0:T(8,128)(2,1)} collective-permute-done((bf16[256,1280]{1,0:T(8,128)(2,1)S(1)}, bf16[256,1280]{1,0:T(8,128)(2,1)}, u32[]{:S(2)}, u32[]{:S(2)}) %collective-permute-start.2) | collective-permute-done | bytes 655392 | tf_op jit(solution)/shard_map/ppermute | solution.py:26
  9.8 0.0 collective-permute-done.3.other_fresh_ref
  9.8 0.0 collective-permute-done.4.other_cache_ref
  9.8 9.2 %attend.1.refs_9_ = bf16[512,1280]{1,0:T(8,128)(2,1)} custom-call(s32[3]{0:T(128)} %pad_add_fusion.ids_ref, s32[1,2,2]{2,1,0:T(2,128)} %list_ref.9, s32[1,2]{1,0:T(1,128)} %count_ref.9, s32[1,4,3]{2,1,0:T(4,128)} %copy.13.keys_ref, bf16[256,2560]{1,0:T(8,128)(2,1)} %own_q_ref.1, bf16[256,1280]{1,0:T(8,128)(2,1)} %collective-permute-done.2.other_q_ref, ...), custom_call_target="tpu_custom_call" | custom-call | tf_op jit(solution)/shard_map/attend/pallas_call | solution.py:168
  19.0 0.4 collective-permute-start.14
  19.5 2.7 %collective-permute-start.5 = (bf16[512,1280]{1,0:T(8,128)(2,1)}, bf16[512,1280]{1,0:T(8,128)(2,1)S(1)}, u32[]{:S(2)}, u32[]{:S(2)}) collective-permute-start(bf16[512,1280]{1,0:T(8,128)(2,1)} %attend.1.refs_9_), channel_id=1, source_target_pairs={{0,16},{16,0},{1,17},{17,1},{2,18},{18,2},{3,19},{19,3},{4,20},{20... | collective-permute-start | bytes 3932168 | tf_op jit(solution)/shard_map/ppermute | solution.py:26
  22.1 1.1 %collective-permute-done.1.refs_2_ = bf16[320,1280]{1,0:T(8,128)(2,1)S(1)} collective-permute-done((bf16[320,1280]{1,0:T(8,128)(2,1)S(1)}, bf16[320,1280]{1,0:T(8,128)(2,1)S(1)}, u32[]{:S(2)}, u32[]{:S(2)}) %collective-permute-start.1) | collective-permute-done | bytes 819232 | tf_op jit(solution)/shard_map/ppermute | solution.py:408
  23.3 1.5 %collective-permute-done.refs_1_ = bf16[320,1280]{1,0:T(8,128)(2,1)} collective-permute-done((bf16[320,1280]{1,0:T(8,128)(2,1)S(1)}, bf16[320,1280]{1,0:T(8,128)(2,1)}, u32[]{:S(2)}, u32[]{:S(2)}) %collective-permute-start) | collective-permute-done | bytes 819232 | tf_op jit(solution)/shard_map/ppermute | solution.py:408
  24.8 1.6 %collective-permute-start.11 = (bf16[320,896]{1,0:T(8,128)(2,1)S(1)}, bf16[320,896]{1,0:T(8,128)(2,1)S(1)}, u32[]{:S(2)}, u32[]{:S(2)}) collective-permute-start(bf16[320,896]{1,0:T(8,128)(2,1)S(1)} %slice.28), channel_id=1, source_target_pairs={{4,0},{8,4},{12,8},{14,12},{10,14},{6,10},{2,6},{0,2},{5,1},{9,5},... | collective-permute-start | bytes 1720328 | tf_op jit(solution)/shard_map/ppermute | solution.py:408
  26.4 1.1 %slice.26 = bf16[320,896]{1,0:T(8,128)(2,1)S(1)} slice(bf16[320,1280]{1,0:T(8,128)(2,1)} %collective-permute-done.refs_1_), slice={[0:320], [0:896]} | slice | bytes 1146880 | tf_op jit(solution)/shard_map/slice | solution.py:472
  27.5 0.5 collective-permute-start.8
  28.0 10.6 %collective-permute-done.11.refs_4_ = bf16[320,896]{1,0:T(8,128)(2,1)S(1)} collective-permute-done((bf16[320,896]{1,0:T(8,128)(2,1)S(1)}, bf16[320,896]{1,0:T(8,128)(2,1)S(1)}, u32[]{:S(2)}, u32[]{:S(2)}) %collective-permute-start.11) | collective-permute-done | bytes 573472 | tf_op jit(solution)/shard_map/ppermute | solution.py:408
  38.6 1.6 %collective-permute-start.12 = (bf16[320,896]{1,0:T(8,128)(2,1)S(1)}, bf16[320,896]{1,0:T(8,128)(2,1)S(1)}, u32[]{:S(2)}, u32[]{:S(2)}) collective-permute-start(bf16[320,896]{1,0:T(8,128)(2,1)S(1)} %collective-permute-done.11.refs_4_), channel_id=1, source_target_pairs={{4,0},{8,4},{12,8},{14,12},{10,14},{6,10},{2,6},{0,2},{5,1},{9,5},... | collective-permute-start | bytes 1720328 | tf_op jit(solution)/shard_map/ppermute | solution.py:408
  40.2 0.9 collective-permute-done.8.refs_3_
  41.1 0.4 collective-permute-start.9
  41.5 10.0 %collective-permute-done.12.refs_6_ = bf16[320,896]{1,0:T(8,128)(2,1)S(1)} collective-permute-done((bf16[320,896]{1,0:T(8,128)(2,1)S(1)}, bf16[320,896]{1,0:T(8,128)(2,1)S(1)}, u32[]{:S(2)}, u32[]{:S(2)}) %collective-permute-start.12) | collective-permute-done | bytes 573472 | tf_op jit(solution)/shard_map/ppermute | solution.py:408
  51.5 2.2 %collective-permute-done.9.refs_5_ = bf16[320,896]{1,0:T(8,128)(2,1)S(1)} collective-permute-done((bf16[320,896]{1,0:T(8,128)(2,1)S(1)}, bf16[320,896]{1,0:T(8,128)(2,1)S(1)}, u32[]{:S(2)}, u32[]{:S(2)}) %collective-permute-start.9) | collective-permute-done | bytes 573472 | tf_op jit(solution)/shard_map/ppermute | solution.py:408
  53.7 1.6 %collective-permute-start.13 = (bf16[160,896]{1,0:T(8,128)(2,1)S(1)}, bf16[160,896]{1,0:T(8,128)(2,1)S(1)}, u32[]{:S(2)}, u32[]{:S(2)}) collective-permute-start(bf16[160,896]{1,0:T(8,128)(2,1)S(1)} %slice.35), channel_id=1, source_target_pairs={{4,0},{8,4},{12,8},{14,12},{10,14},{6,10},{2,6},{0,2},{5,1},{9,5},... | collective-permute-start | bytes 860168 | tf_op jit(solution)/shard_map/ppermute | solution.py:408
  55.4 0.5 collective-permute-start.10
  55.9 1.0 slice.32
  56.9 0.5 collective-permute-start.6
  57.4 1.6 %collective-permute-start.7 = (bf16[320,384]{1,0:T(8,128)(2,1)S(1)}, bf16[320,384]{1,0:T(8,128)(2,1)S(1)}, u32[]{:S(2)}, u32[]{:S(2)}) collective-permute-start(bf16[320,384]{1,0:T(8,128)(2,1)S(1)} %slice.33), channel_id=1, source_target_pairs={{4,0},{8,4},{12,8},{14,12},{10,14},{6,10},{2,6},{0,2},{5,1},{9,5},... | collective-permute-start | bytes 737288 | tf_op jit(solution)/shard_map/ppermute | solution.py:408
  59.0 5.0 %project_most.3 = (f32[512,896]{1,0:T(8,128)S(1)}, bf16[512,384]{1,0:T(8,128)(2,1)S(1)}) custom-call(s32[3]{0:T(128)S(1)} %copy-done.3, bf16[320,1280]{1,0:T(8,128)(2,1)S(1)} %constant_dynamic-slice_fusion.1.refs_0_, bf16[320,1280]{1,0:T(8,128)(2,1)} %collective-permute-done.refs_1_, bf16[320,1280]{1,0:T(8,128)(2,1)S(1)} %collective-permute-done.1.refs_2_, ...), custom_call_target="tpu_custom_call" | custom-call | flops 2348810240 | tf_op jit(solution)/shard_map/project_most/pallas_call | solution.py:254
  64.0 0.0 copy-start.1
  64.0 0.0 collective-permute-done.13.bottom_ref.refs_8_
  64.0 1.1 %collective-permute-done.10.top_ref.refs_7_ = bf16[160,896]{1,0:T(8,128)(2,1)S(1)} collective-permute-done((bf16[160,896]{1,0:T(8,128)(2,1)S(1)}, bf16[160,896]{1,0:T(8,128)(2,1)S(1)}, u32[]{:S(2)}, u32[]{:S(2)}) %collective-permute-start.10) | collective-permute-done | bytes 286752 | tf_op jit(solution)/shard_map/ppermute | solution.py:408
  65.1 1.3 %project_last.3 = bf16[512,896]{1,0:T(8,128)(2,1)S(1)} custom-call(s32[3]{0:T(128)S(1)} %copy-done.3, bf16[160,896]{1,0:T(8,128)(2,1)S(1)} %collective-permute-done.10.top_ref.refs_7_, bf16[160,896]{1,0:T(8,128)(2,1)S(1)} %collective-permute-done.13.bottom_ref.refs_8_, f32[512,896]{1,0:T(8,128)S(1)} %get-tuple-element.29.sums_ref, ...), custom_call_target="tpu_custom_call" | custom-call | tf_op jit(solution)/shard_map/project_last/pallas_call | solution.py:292
  66.4 1.6 %collective-permute-start.23 = (bf16[512,896]{1,0:T(8,128)(2,1)S(1)}, bf16[512,896]{1,0:T(8,128)(2,1)S(1)}, u32[]{:S(2)}, u32[]{:S(2)}) collective-permute-start(bf16[512,896]{1,0:T(8,128)(2,1)S(1)} %project_last.3), channel_id=1, source_target_pairs={{0,16},{16,0},{1,17},{17,1},{2,18},{18,2},{3,19},{19,3},{4,20},{20... | collective-permute-start | bytes 2752520 | tf_op jit(solution)/shard_map/ppermute | solution.py:26
  68.0 1.6 %collective-permute-done.6.refs_3_ = bf16[320,384]{1,0:T(8,128)(2,1)S(1)} collective-permute-done((bf16[320,384]{1,0:T(8,128)(2,1)S(1)}, bf16[320,384]{1,0:T(8,128)(2,1)S(1)}, u32[]{:S(2)}, u32[]{:S(2)}) %collective-permute-start.6) | collective-permute-done | bytes 245792 | tf_op jit(solution)/shard_map/ppermute | solution.py:408
  69.7 0.0 collective-permute-done.7.refs_4_
  69.7 0.5 collective-permute-start.16
  70.1 1.6 %collective-permute-start.17 = (bf16[320,384]{1,0:T(8,128)(2,1)S(1)}, bf16[320,384]{1,0:T(8,128)(2,1)S(1)}, u32[]{:S(2)}, u32[]{:S(2)}) collective-permute-start(bf16[320,384]{1,0:T(8,128)(2,1)S(1)} %collective-permute-done.7.refs_4_), channel_id=1, source_target_pairs={{4,0},{8,4},{12,8},{14,12},{10,14},{6,10},{2,6},{0,2},{5,1},{9,5},... | collective-permute-start | bytes 737288 | tf_op jit(solution)/shard_map/ppermute | solution.py:408
  71.7 5.0 %project_most.4.refs_0_ = bf16[512,896]{1,0:T(8,128)(2,1)S(1)} custom-call(s32[3]{0:T(128)S(1)} %copy-done.3, bf16[320,1280]{1,0:T(8,128)(2,1)S(1)} %constant_dynamic-slice_fusion.1.refs_0_, bf16[320,1280]{1,0:T(8,128)(2,1)} %collective-permute-done.refs_1_, bf16[320,1280]{1,0:T(8,128)(2,1)S(1)} %collective-permute-done.1.refs_2_, ...), custom_call_target="tpu_custom_call" | custom-call | flops 22000001024 | tf_op jit(solution)/shard_map/project_most/pallas_call | solution.py:254
  76.7 0.1 collective-permute-start.22
  76.7 0.2 collective-permute-done.16.refs_5_
  76.9 0.2 collective-permute-done.17.refs_6_
  77.1 1.6 %collective-permute-start.19 = (bf16[160,384]{1,0:T(8,128)(2,1)S(1)}, bf16[160,384]{1,0:T(8,128)(2,1)S(1)}, u32[]{:S(2)}, u32[]{:S(2)}) collective-permute-start(bf16[160,384]{1,0:T(8,128)(2,1)S(1)} %slice.31), channel_id=1, source_target_pairs={{4,0},{8,4},{12,8},{14,12},{10,14},{6,10},{2,6},{0,2},{5,1},{9,5},... | collective-permute-start | bytes 368648 | tf_op jit(solution)/shard_map/ppermute | solution.py:408
  78.8 0.4 collective-permute-start.18
  79.2 6.0 %project_most.5 = (f32[512,384]{1,0:T(8,128)S(1)}, f32[512,384]{1,0:T(8,128)S(1)}, bf16[512,384]{1,0:T(8,128)(2,1)S(1)}, bf16[512,384]{1,0:T(8,128)(2,1)S(1)}) custom-call(s32[3]{0:T(128)S(1)} %copy-done.3, bf16[320,1280]{1,0:T(8,128)(2,1)S(1)} %constant_dynamic-slice_fusion.1.refs_0_, bf16[320,1280]{1,0:T(8,128)(2,1)} %collective-permute-done.refs_1_, ...), custom_call_target="tpu_custom_call" | custom-call | flops 2013265920 | tf_op jit(solution)/shard_map/project_most/pallas_call | solution.py:254
  85.2 0.0 collective-permute-done.19.bottom_ref
  85.2 1.0 project_last.4
  86.2 1.6 %collective-permute-start.20 = (bf16[512,384]{1,0:T(8,128)(2,1)S(1)}, bf16[512,384]{1,0:T(8,128)(2,1)S(1)}, u32[]{:S(2)}, u32[]{:S(2)}) collective-permute-start(bf16[512,384]{1,0:T(8,128)(2,1)S(1)} %project_last.4), channel_id=1, source_target_pairs={{0,16},{16,0},{1,17},{17,1},{2,18},{18,2},{3,19},{19,3},{4,20},{20... | collective-permute-start | bytes 1179656 | tf_op jit(solution)/shard_map/ppermute | solution.py:26
  87.8 0.0 collective-permute-done.23.refs_2_
  87.8 0.0 copy-start.2
  87.8 0.0 copy-start.4
  87.9 0.0 copy-start.5
  87.9 1.0 project_last.5.refs_0_
  88.9 0.5 collective-permute-start.21
  89.4 0.9 collective-permute-done.24.refs_3_
  90.3 3.4 %finish.4.refs_2_ = bf16[256,5120]{1,0:T(8,128)(2,1)} custom-call(s32[3]{0:T(128)S(1)} %copy-done.3, s32[1,2,2]{2,1,0:T(2,128)S(1)} %copy-done.4, s32[1,2]{1,0:T(1,128)S(1)} %copy-done.5, f32[1,5120]{1,0:T(1,128)S(1)} %bitcast.4, bf16[256,5120]{1,0:T(8,128)(2,1)S(1)} %copy-done, bf16[512,896]{1,0:T(8,128)(2,1)S(1)} %project_most.4.refs_0_, ...), custom_call_target="tpu_custom_call" | custom-call | flops 6000000000 | tf_op jit(solution)/shard_map/finish/pallas_call | solution.py:378
  93.8 2.1 %finish.5.refs_1_ = bf16[256,5120]{1,0:T(8,128)(2,1)} custom-call(s32[3]{0:T(128)S(1)} %copy-done.3, s32[1,2,2]{2,1,0:T(2,128)S(1)} %copy-done.4, s32[1,2]{1,0:T(1,128)S(1)} %copy-done.5, f32[1,5120]{1,0:T(1,128)S(1)} %bitcast.5, bf16[256,5120]{1,0:T(8,128)(2,1)S(1)} %copy-done, ...), custom_call_target="tpu_custom_call", output_to_operand_aliasing={{}: (7, {})} | custom-call | flops 3000000000 | tf_op jit(solution)/shard_map/finish/pallas_call | solution.py:378
  95.8 1.1 %collective-permute-done.20.refs_0_ = bf16[512,384]{1,0:T(8,128)(2,1)S(1)} collective-permute-done((bf16[512,384]{1,0:T(8,128)(2,1)S(1)}, bf16[512,384]{1,0:T(8,128)(2,1)S(1)}, u32[]{:S(2)}, u32[]{:S(2)}) %collective-permute-start.20) | collective-permute-done | bytes 393248 | tf_op jit(solution)/shard_map/ppermute | solution.py:26
  96.9 1.6 %finish.6.refs_1_ = bf16[256,5120]{1,0:T(8,128)(2,1)} custom-call(s32[3]{0:T(128)S(1)} %copy-done.3, s32[1,2,2]{2,1,0:T(2,128)S(1)} %copy-done.4, s32[1,2]{1,0:T(1,128)S(1)} %copy-done.5, f32[1,5120]{1,0:T(1,128)S(1)} %bitcast.6, bf16[256,5120]{1,0:T(8,128)(2,1)S(1)} %copy-done, ...), custom_call_target="tpu_custom_call", output_to_operand_aliasing={{}: (6, {})} | custom-call | flops 1500000000 | tf_op jit(solution)/shard_map/finish/pallas_call | solution.py:378
  98.6 0.1 collective-permute-done.25.refs_0_
  98.7 1.6 %finish.7 = bf16[256,5120]{1,0:T(8,128)(2,1)} custom-call(s32[3]{0:T(128)S(1)} %copy-done.3, s32[1,2,2]{2,1,0:T(2,128)S(1)} %copy-done.4, s32[1,2]{1,0:T(1,128)S(1)} %copy-done.5, f32[1,5120]{1,0:T(1,128)S(1)} %bitcast.7, bf16[256,5120]{1,0:T(8,128)(2,1)S(1)} %copy-done, ...), custom_call_target="tpu_custom_call", output_to_operand_aliasing={{}: (6, {})} | custom-call | flops 1500000000 | tf_op jit(solution)/shard_map/finish/pallas_call | solution.py:378
  (25 shorter events, 0.2 us)
Async XLA Ops:
  0.0 6.1 %copy-start.6 = (s32[1,4,3]{1,0,2:T(1,128)S(1)}, s32[1,4,3]{1,0,2:T(1,128)}, u32[]{:S(2)}) copy-start(s32[1,4,3]{1,0,2:T(1,128)} %param.16) | copy-start | bytes 148
  0.0 9.8 %collective-permute-start.3 = (bf16[256,2,2560]{2,1,0:T(2,128)(2,1)}, bf16[256,2,2560]{2,1,0:T(2,128)(2,1)}, u32[]{:S(2)}, u32[]{:S(2)}) collective-permute-start(bf16[256,2,2560]{2,1,0:T(2,128)(2,1)} %own_fresh_ref.1), channel_id=1, source_target_pairs={{0,1},{1,0},{2,3},{3,2},{4,5},{5,4},{6,7},{7,6},{8,9},{9,8},{10,11... | collective-permute-start | bytes 7864328 | tf_op jit(solution)/shard_map/ppermute | solution.py:26
  0.5 9.4 %collective-permute-start.4 = (bf16[256,2,2560]{2,1,0:T(2,128)(2,1)}, bf16[256,2,2560]{2,1,0:T(2,128)(2,1)}, u32[]{:S(2)}, u32[]{:S(2)}) collective-permute-start(bf16[256,2,2560]{2,1,0:T(2,128)(2,1)} %own_cache_ref.1), channel_id=1, source_target_pairs={{0,1},{1,0},{2,3},{3,2},{4,5},{5,4},{6,7},{7,6},{8,9},{9,8},{10,11... | collective-permute-start | bytes 7864328 | tf_op jit(solution)/shard_map/ppermute | solution.py:26
  1.7 21.5 %collective-permute-start.1 = (bf16[320,1280]{1,0:T(8,128)(2,1)S(1)}, bf16[320,1280]{1,0:T(8,128)(2,1)S(1)}, u32[]{:S(2)}, u32[]{:S(2)}) collective-permute-start(bf16[320,1280]{1,0:T(8,128)(2,1)S(1)} %constant_dynamic-slice_fusion.1.refs_0_), channel_id=1, source_target_pairs={{4,0},{8,4},{12,8},{14,12},{10,14},{6,10},{2,6},{0,2},{5,1},{9,5},... | collective-permute-start | bytes 2457608 | tf_op jit(solution)/shard_map/ppermute | solution.py:408
  4.7 20.0 %collective-permute-start = (bf16[320,1280]{1,0:T(8,128)(2,1)S(1)}, bf16[320,1280]{1,0:T(8,128)(2,1)}, u32[]{:S(2)}, u32[]{:S(2)}) collective-permute-start(bf16[320,1280]{1,0:T(8,128)(2,1)S(1)} %constant_dynamic-slice_fusion.1.refs_0_), channel_id=1, source_target_pairs={{0,4},{4,8},{8,12},{12,14},{14,10},{10,6},{6,2},{2,0},{1,5},{5,9},... | collective-permute-start | bytes 2457608 | tf_op jit(solution)/shard_map/ppermute | solution.py:408
  6.0 3.8 %collective-permute-start.2 = (bf16[256,1280]{1,0:T(8,128)(2,1)S(1)}, bf16[256,1280]{1,0:T(8,128)(2,1)}, u32[]{:S(2)}, u32[]{:S(2)}) collective-permute-start(bf16[256,1280]{1,0:T(8,128)(2,1)S(1)} %constant_dynamic-slice_fusion), channel_id=1, source_target_pairs={{0,1},{1,0},{2,3},{3,2},{4,5},{5,4},{6,7},{7,6},{8,9},{9,8},{10,11... | collective-permute-start | bytes 1966088 | tf_op jit(solution)/shard_map/ppermute | solution.py:26
  19.0 39.9 %copy-start.3 = (s32[3]{0:T(128)S(1)}, s32[3]{0:T(128)}, u32[]{:S(2)}) copy-start(s32[3]{0:T(128)} %pad_add_fusion.ids_ref) | copy-start | bytes 40
  19.0 34.6 %collective-permute-start.14 = (bf16[512,1280]{1,0:T(8,128)(2,1)}, bf16[512,1280]{1,0:T(8,128)(2,1)S(1)}, u32[]{:S(2)}, u32[]{:S(2)}) collective-permute-start(bf16[512,1280]{1,0:T(8,128)(2,1)} %attend.1.refs_9_), channel_id=1, source_target_pairs={{0,1},{1,0},{2,3},{3,2},{4,5},{5,4},{6,7},{7,6},{8,9},{9,8},{10,11... | collective-permute-start | bytes 3932168 | tf_op jit(solution)/shard_map/ppermute | solution.py:26
  19.5 34.2 %collective-permute-start.5 = (bf16[512,1280]{1,0:T(8,128)(2,1)}, bf16[512,1280]{1,0:T(8,128)(2,1)S(1)}, u32[]{:S(2)}, u32[]{:S(2)}) collective-permute-start(bf16[512,1280]{1,0:T(8,128)(2,1)} %attend.1.refs_9_), channel_id=1, source_target_pairs={{0,16},{16,0},{1,17},{17,1},{2,18},{18,2},{3,19},{19,3},{4,20},{20... | collective-permute-start | bytes 3932168 | tf_op jit(solution)/shard_map/ppermute | solution.py:26
  24.8 13.8 %collective-permute-start.11 = (bf16[320,896]{1,0:T(8,128)(2,1)S(1)}, bf16[320,896]{1,0:T(8,128)(2,1)S(1)}, u32[]{:S(2)}, u32[]{:S(2)}) collective-permute-start(bf16[320,896]{1,0:T(8,128)(2,1)S(1)} %slice.28), channel_id=1, source_target_pairs={{4,0},{8,4},{12,8},{14,12},{10,14},{6,10},{2,6},{0,2},{5,1},{9,5},... | collective-permute-start | bytes 1720328 | tf_op jit(solution)/shard_map/ppermute | solution.py:408
  27.5 13.6 %collective-permute-start.8 = (bf16[320,896]{1,0:T(8,128)(2,1)S(1)}, bf16[320,896]{1,0:T(8,128)(2,1)S(1)}, u32[]{:S(2)}, u32[]{:S(2)}) collective-permute-start(bf16[320,896]{1,0:T(8,128)(2,1)S(1)} %slice.26), channel_id=1, source_target_pairs={{0,4},{4,8},{8,12},{12,14},{14,10},{10,6},{6,2},{2,0},{1,5},{5,9},... | collective-permute-start | bytes 1720328 | tf_op jit(solution)/shard_map/ppermute | solution.py:408
  38.6 12.9 %collective-permute-start.12 = (bf16[320,896]{1,0:T(8,128)(2,1)S(1)}, bf16[320,896]{1,0:T(8,128)(2,1)S(1)}, u32[]{:S(2)}, u32[]{:S(2)}) collective-permute-start(bf16[320,896]{1,0:T(8,128)(2,1)S(1)} %collective-permute-done.11.refs_4_), channel_id=1, source_target_pairs={{4,0},{8,4},{12,8},{14,12},{10,14},{6,10},{2,6},{0,2},{5,1},{9,5},... | collective-permute-start | bytes 1720328 | tf_op jit(solution)/shard_map/ppermute | solution.py:408
  41.1 12.6 %collective-permute-start.9 = (bf16[320,896]{1,0:T(8,128)(2,1)S(1)}, bf16[320,896]{1,0:T(8,128)(2,1)S(1)}, u32[]{:S(2)}, u32[]{:S(2)}) collective-permute-start(bf16[320,896]{1,0:T(8,128)(2,1)S(1)} %collective-permute-done.8.refs_3_), channel_id=1, source_target_pairs={{0,4},{4,8},{8,12},{12,14},{14,10},{10,6},{6,2},{2,0},{1,5},{5,9},... | collective-permute-start | bytes 1720328 | tf_op jit(solution)/shard_map/ppermute | solution.py:408
  53.7 5.3 %collective-permute-start.15 = (bf16[512,1280]{1,0:T(8,128)(2,1)S(1)}, bf16[512,1280]{1,0:T(8,128)(2,1)S(1)}, u32[]{:S(2)}, u32[]{:S(2)}) collective-permute-start(bf16[512,1280]{1,0:T(8,128)(2,1)S(1)} %collective-permute-done.5.refs_7_), channel_id=1, source_target_pairs={{0,1},{1,0},{2,3},{3,2},{4,5},{5,4},{6,7},{7,6},{8,9},{9,8},{10,11... | collective-permute-start | bytes 3932168 | tf_op jit(solution)/shard_map/ppermute | solution.py:26
  53.7 10.3 %collective-permute-start.13 = (bf16[160,896]{1,0:T(8,128)(2,1)S(1)}, bf16[160,896]{1,0:T(8,128)(2,1)S(1)}, u32[]{:S(2)}, u32[]{:S(2)}) collective-permute-start(bf16[160,896]{1,0:T(8,128)(2,1)S(1)} %slice.35), channel_id=1, source_target_pairs={{4,0},{8,4},{12,8},{14,12},{10,14},{6,10},{2,6},{0,2},{5,1},{9,5},... | collective-permute-start | bytes 860168 | tf_op jit(solution)/shard_map/ppermute | solution.py:408
  55.4 9.7 %collective-permute-start.10 = (bf16[160,896]{1,0:T(8,128)(2,1)S(1)}, bf16[160,896]{1,0:T(8,128)(2,1)S(1)}, u32[]{:S(2)}, u32[]{:S(2)}) collective-permute-start(bf16[160,896]{1,0:T(8,128)(2,1)S(1)} %slice.34), channel_id=1, source_target_pairs={{0,4},{4,8},{8,12},{12,14},{14,10},{10,6},{6,2},{2,0},{1,5},{5,9},... | collective-permute-start | bytes 860168 | tf_op jit(solution)/shard_map/ppermute | solution.py:408
  56.9 12.8 %collective-permute-start.6 = (bf16[320,384]{1,0:T(8,128)(2,1)S(1)}, bf16[320,384]{1,0:T(8,128)(2,1)S(1)}, u32[]{:S(2)}, u32[]{:S(2)}) collective-permute-start(bf16[320,384]{1,0:T(8,128)(2,1)S(1)} %slice.32), channel_id=1, source_target_pairs={{0,4},{4,8},{8,12},{12,14},{14,10},{10,6},{6,2},{2,0},{1,5},{5,9},... | collective-permute-start | bytes 737288 | tf_op jit(solution)/shard_map/ppermute | solution.py:408
  57.4 12.3 %collective-permute-start.7 = (bf16[320,384]{1,0:T(8,128)(2,1)S(1)}, bf16[320,384]{1,0:T(8,128)(2,1)S(1)}, u32[]{:S(2)}, u32[]{:S(2)}) collective-permute-start(bf16[320,384]{1,0:T(8,128)(2,1)S(1)} %slice.33), channel_id=1, source_target_pairs={{4,0},{8,4},{12,8},{14,12},{10,14},{6,10},{2,6},{0,2},{5,1},{9,5},... | collective-permute-start | bytes 737288 | tf_op jit(solution)/shard_map/ppermute | solution.py:408
  64.0 7.7 %copy-start.1 = (bf16[512,1280]{1,0:T(8,128)(2,1)S(1)}, bf16[512,1280]{1,0:T(8,128)(2,1)}, u32[]{:S(2)}) copy-start(bf16[512,1280]{1,0:T(8,128)(2,1)} %attend.1.refs_9_) | copy-start | bytes 3932164
  66.4 21.4 %collective-permute-start.23 = (bf16[512,896]{1,0:T(8,128)(2,1)S(1)}, bf16[512,896]{1,0:T(8,128)(2,1)S(1)}, u32[]{:S(2)}, u32[]{:S(2)}) collective-permute-start(bf16[512,896]{1,0:T(8,128)(2,1)S(1)} %project_last.3), channel_id=1, source_target_pairs={{0,16},{16,0},{1,17},{17,1},{2,18},{18,2},{3,19},{19,3},{4,20},{20... | collective-permute-start | bytes 2752520 | tf_op jit(solution)/shard_map/ppermute | solution.py:26
  69.7 7.3 %collective-permute-start.16 = (bf16[320,384]{1,0:T(8,128)(2,1)S(1)}, bf16[320,384]{1,0:T(8,128)(2,1)S(1)}, u32[]{:S(2)}, u32[]{:S(2)}) collective-permute-start(bf16[320,384]{1,0:T(8,128)(2,1)S(1)} %collective-permute-done.6.refs_3_), channel_id=1, source_target_pairs={{0,4},{4,8},{8,12},{12,14},{14,10},{10,6},{6,2},{2,0},{1,5},{5,9},... | collective-permute-start | bytes 737288 | tf_op jit(solution)/shard_map/ppermute | solution.py:408
  70.1 7.0 %collective-permute-start.17 = (bf16[320,384]{1,0:T(8,128)(2,1)S(1)}, bf16[320,384]{1,0:T(8,128)(2,1)S(1)}, u32[]{:S(2)}, u32[]{:S(2)}) collective-permute-start(bf16[320,384]{1,0:T(8,128)(2,1)S(1)} %collective-permute-done.7.refs_4_), channel_id=1, source_target_pairs={{4,0},{8,4},{12,8},{14,12},{10,14},{6,10},{2,6},{0,2},{5,1},{9,5},... | collective-permute-start | bytes 737288 | tf_op jit(solution)/shard_map/ppermute | solution.py:408
  76.7 12.8 %collective-permute-start.22 = (bf16[512,896]{1,0:T(8,128)(2,1)S(1)}, bf16[512,896]{1,0:T(8,128)(2,1)S(1)}, u32[]{:S(2)}, u32[]{:S(2)}) collective-permute-start(bf16[512,896]{1,0:T(8,128)(2,1)S(1)} %project_most.4.refs_0_), channel_id=1, source_target_pairs={{0,1},{1,0},{2,3},{3,2},{4,5},{5,4},{6,7},{7,6},{8,9},{9,8},{10,11... | collective-permute-start | bytes 2752520 | tf_op jit(solution)/shard_map/ppermute | solution.py:26
  77.1 8.1 %collective-permute-start.19 = (bf16[160,384]{1,0:T(8,128)(2,1)S(1)}, bf16[160,384]{1,0:T(8,128)(2,1)S(1)}, u32[]{:S(2)}, u32[]{:S(2)}) collective-permute-start(bf16[160,384]{1,0:T(8,128)(2,1)S(1)} %slice.31), channel_id=1, source_target_pairs={{4,0},{8,4},{12,8},{14,12},{10,14},{6,10},{2,6},{0,2},{5,1},{9,5},... | collective-permute-start | bytes 368648 | tf_op jit(solution)/shard_map/ppermute | solution.py:408
  78.8 6.5 %collective-permute-start.18 = (bf16[160,384]{1,0:T(8,128)(2,1)S(1)}, bf16[160,384]{1,0:T(8,128)(2,1)S(1)}, u32[]{:S(2)}, u32[]{:S(2)}) collective-permute-start(bf16[160,384]{1,0:T(8,128)(2,1)S(1)} %slice.30), channel_id=1, source_target_pairs={{0,4},{4,8},{8,12},{12,14},{14,10},{10,6},{6,2},{2,0},{1,5},{5,9},... | collective-permute-start | bytes 368648 | tf_op jit(solution)/shard_map/ppermute | solution.py:408
  86.2 10.7 %collective-permute-start.20 = (bf16[512,384]{1,0:T(8,128)(2,1)S(1)}, bf16[512,384]{1,0:T(8,128)(2,1)S(1)}, u32[]{:S(2)}, u32[]{:S(2)}) collective-permute-start(bf16[512,384]{1,0:T(8,128)(2,1)S(1)} %project_last.4), channel_id=1, source_target_pairs={{0,16},{16,0},{1,17},{17,1},{2,18},{18,2},{3,19},{19,3},{4,20},{20... | collective-permute-start | bytes 1179656 | tf_op jit(solution)/shard_map/ppermute | solution.py:26
  87.8 2.5 %collective-permute-start.24 = (bf16[512,896]{1,0:T(8,128)(2,1)S(1)}, bf16[512,896]{1,0:T(8,128)(2,1)S(1)}, u32[]{:S(2)}, u32[]{:S(2)}) collective-permute-start(bf16[512,896]{1,0:T(8,128)(2,1)S(1)} %collective-permute-done.23.refs_2_), channel_id=1, source_target_pairs={{0,1},{1,0},{2,3},{3,2},{4,5},{5,4},{6,7},{7,6},{8,9},{9,8},{10,11... | collective-permute-start | bytes 2752520 | tf_op jit(solution)/shard_map/ppermute | solution.py:26
  87.8 2.5 %copy-start = (bf16[256,5120]{1,0:T(8,128)(2,1)S(1)}, bf16[256,5120]{1,0:T(8,128)(2,1)}, u32[]{:S(2)}) copy-start(bf16[256,5120]{1,0:T(8,128)(2,1)} %input_ref.7) | copy-start | bytes 7864324
  87.8 2.5 %copy-start.2 = (f32[5120]{0:T(1024)S(1)}, f32[5120]{0:T(1024)}, u32[]{:S(2)}) copy-start(f32[5120]{0:T(1024)} %param.10) | copy-start | bytes 61444
  87.8 2.5 %copy-start.4 = (s32[1,2,2]{2,1,0:T(2,128)S(1)}, s32[1,2,2]{2,1,0:T(2,128)}, u32[]{:S(2)}) copy-start(s32[1,2,2]{2,1,0:T(2,128)} %list_ref.9) | copy-start | bytes 52
  87.9 2.5 %copy-start.5 = (s32[1,2]{1,0:T(1,128)S(1)}, s32[1,2]{1,0:T(1,128)}, u32[]{:S(2)}) copy-start(s32[1,2]{1,0:T(1,128)} %count_ref.9) | copy-start | bytes 28
  88.9 4.9 %collective-permute-start.21 = (bf16[512,384]{1,0:T(8,128)(2,1)S(1)}, bf16[512,384]{1,0:T(8,128)(2,1)S(1)}, u32[]{:S(2)}, u32[]{:S(2)}) collective-permute-start(bf16[512,384]{1,0:T(8,128)(2,1)S(1)} %project_last.5.refs_0_), channel_id=1, source_target_pairs={{0,1},{1,0},{2,3},{3,2},{4,5},{5,4},{6,7},{7,6},{8,9},{9,8},{10,11... | collective-permute-start | bytes 1179656 | tf_op jit(solution)/shard_map/ppermute | solution.py:26
  96.9 1.7 %collective-permute-start.25 = (bf16[512,384]{1,0:T(8,128)(2,1)S(1)}, bf16[512,384]{1,0:T(8,128)(2,1)S(1)}, u32[]{:S(2)}, u32[]{:S(2)}) collective-permute-start(bf16[512,384]{1,0:T(8,128)(2,1)S(1)} %collective-permute-done.20.refs_0_), channel_id=1, source_target_pairs={{0,1},{1,0},{2,3},{3,2},{4,5},{5,4},{6,7},{7,6},{8,9},{9,8},{10,11... | collective-permute-start | bytes 1179656 | tf_op jit(solution)/shard_map/ppermute | solution.py:26
